TPU v7x, 128 devices: a whole 4x4x4 slice. The times are simulated.
128 devices in a mesh: gy: 16 (over y, z), gz: 8 (over x, core).
Axes of the slice: x: 4, y: 4, z: 4, core: 2. Of those that a mesh axis runs over, the one named last changes fastest.
Arguments:
- fields: float32 [12, 16, 1024, 1024], P(None, None, 'gy', 'gz'), may hold values from -6 to 6
- source_term: bfloat16 [12, 16, 1024, 1024], P(None, None, 'gy', 'gz'), may hold values from -15 to 15
- resistivity: float32 [1024], P('gz'), may hold values from 0.05 to 8000, as said below
Outputs:
- advanced: float32 [12, 16, 1024, 1024], P(None, None, 'gy', 'gz')
Inputs may be any that keep to these rules, and one draw needn't show every extreme that they name: resistivity is positive.
All inputs are finite; a program needn't handle non-finite values.
Results may differ from a plain program's by a relative error of at most 0.005.
Values sent between devices are 32-bit elements; how exact they have to be, the bound alone decides.
No kernel may reach another device: no remote copies, remote signals or barrier semaphores. Data moves between devices by JAX's collectives and lax.ppermute only.
A program may use at most 128 MiB of HBM per device.

v0:
```python
import jax
import jax.numpy as jnp
from jax import lax
from jax.experimental import pallas as pl
from jax.experimental.pallas import tpu as pltpu
from jax.sharding import PartitionSpec as P

f32 = jnp.float32
bf16 = jnp.bfloat16
z_rate = 1.0
y_rate = 0.25

LINES = 192
CY = 64
CZ = 128
GROUP = 8
PER = 32
STEPS = LINES // PER
PAIRS = PER // (2 * GROUP)
TILES = GROUP * CY // 8
NGY = 16
NGZ = 8
VMEM_LIMIT = 48 * 1024 * 1024


def lanes(shape=(8, CZ)):
    return lax.broadcasted_iota(jnp.int32, shape, len(shape) - 1)


def rows_of(shape=(8, CZ)):
    return lax.broadcasted_iota(jnp.int32, shape, 0)


def root_of(eta):
    k = y_rate * eta
    root = jnp.sqrt(1.0 + 4.0 * k)
    return 2.0 * k / (1.0 + 2.0 * k + root), 1.0 / root


def power_64(r):
    for _ in range(6):
        r = r * r
    return r


def split_3(x):
    high = x.astype(bf16)
    rest = x - high.astype(f32)
    mid = rest.astype(bf16)
    low = (rest - mid.astype(f32)).astype(bf16)
    return high, mid, low


def columns_kernel(u_ref, up_ref, down_ref):
    lane = lanes()
    odd = lane % 2 == 1

    def pair(p, _):
        packed = []
        for half in range(2):
            acc = jnp.zeros((8, CZ), f32)
            for k in range(TILES):
                line = (2 * p + half) * GROUP + k // 8
                tile = u_ref[line, pl.ds((k % 8) * 8, 8), :]
                if k:
                    tile = pltpu.roll(tile, 2 * k, 1)
                here = (lane == 2 * k) | (lane == (2 * k + CZ - 1) % CZ)
                acc = jnp.where(here, tile, acc)
            packed.append(acc)
        first, second = packed
        up_ref[p] = jnp.where(odd, first, pltpu.roll(second, 1, 1))
        down_ref[p] = jnp.where(odd, pltpu.roll(second, CZ - 1, 1), first)
        return 0

    lax.fori_loop(0, PAIRS, pair, 0)


def end_columns(u):
    return pl.pallas_call(
        columns_kernel,
        grid=(STEPS,),
        in_specs=[pl.BlockSpec((PER, CY, CZ), lambda i: (i, 0, 0))],
        out_specs=[pl.BlockSpec((PAIRS, 8, CZ), lambda i: (i, 0, 0))] * 2,
        out_shape=[jax.ShapeDtypeStruct((LINES // 16, 8, CZ), f32)] * 2,
        compiler_params=pltpu.CompilerParams(vmem_limit_bytes=VMEM_LIMIT),
        name="end_columns",
    )(u)


def sweep_kernel(rank_ref, u_ref, q_ref, low_ref, high_ref, eta_ref, m_ref, ends_ref, x_buf, f_buf):
    lane = lanes()
    even = lane % 2 == 0
    is_first = lane == 0
    is_last = lane == CZ - 1
    rank = rank_ref[0]
    eta_prev = jnp.broadcast_to(eta_ref[0:1, :], (8, CZ))
    eta = jnp.broadcast_to(eta_ref[1:2, :], (8, CZ))
    eta_next = jnp.broadcast_to(eta_ref[2:3, :], (8, CZ))
    eta_prev = jnp.where(rank > 0, eta_prev, 0.0)
    eta_next = jnp.where(rank < NGZ - 1, eta_next, 0.0)
    below = jnp.where(is_first, pltpu.roll(eta_prev, 1, 1), pltpu.roll(eta, 1, 1))
    above = jnp.where(is_last, pltpu.roll(eta_next, CZ - 1, 1), pltpu.roll(eta, CZ - 1, 1))
    face_low = z_rate * 0.5 * (below + eta)
    face_high = z_rate * 0.5 * (eta + above)
    decay, peak = root_of(eta)

    def pair(p, _):
        low, high = low_ref[p], high_ref[p]
        both = (
            jnp.where(even, pltpu.roll(low, 1, 1), pltpu.roll(high, CZ - 1, 1)),
            jnp.where(even, low, high),
        )
        for half in range(2):
            for k in range(TILES):
                line = (2 * p + half) * GROUP + k // 8
                at = pl.ds((k % 8) * 8, 8)
                here = u_ref[line, at, :]
                halo = both[half] if k == 0 else pltpu.roll(both[half], (CZ - 2 * k) % CZ, 1)
                under = jnp.where(is_first, halo, pltpu.roll(here, 1, 1))
                over = jnp.where(is_last, halo, pltpu.roll(here, CZ - 1, 1))
                q = q_ref[line, at, :].astype(f32)
                explicit = face_high * (over - here) - face_low * (here - under)
                x_buf[pl.ds(line * CY + (k % 8) * 8, 8), :] = here + explicit + q
        return 0

    lax.fori_loop(0, PAIRS, pair, 0)

    groups = PER // GROUP

    def at(g, y):
        return pl.ds(g * GROUP * CY + y, GROUP, stride=CY)

    total = [jnp.zeros((8, CZ), f32) for _ in range(groups)]
    for y in range(CY):
        for g in range(groups):
            total[g] = total[g] * decay + x_buf[at(g, y), :]
            f_buf[at(g, y), :] = total[g]
    for g in range(groups):
        ends_ref[0, pl.ds(g * GROUP, GROUP), :] = total[g]
    total = [jnp.zeros((8, CZ), f32) for _ in range(groups)]
    for y in reversed(range(CY)):
        for g in range(groups):
            kept = total[g] * decay
            total[g] = kept + x_buf[at(g, y), :]
            f_buf[at(g, y), :] = peak * (f_buf[at(g, y), :] + kept)
    for g in range(groups):
        ends_ref[1, pl.ds(g * GROUP, GROUP), :] = total[g]

    def copy(line, _):
        m_ref[line] = f_buf[pl.ds(pl.multiple_of(line * CY, CY), CY), :]
        return 0

    lax.fori_loop(0, PER, copy, 0)


def sweeps(ranks, u, q, low, high, etas):
    block = pl.BlockSpec((PER, CY, CZ), lambda i: (i, 0, 0))
    halo = pl.BlockSpec((PAIRS, 8, CZ), lambda i: (i, 0, 0))
    return pl.pallas_call(
        sweep_kernel,
        grid=(STEPS,),
        in_specs=[
            pl.BlockSpec(memory_space=pltpu.SMEM),
            block,
            block,
            halo,
            halo,
            pl.BlockSpec((8, CZ), lambda i: (0, 0)),
        ],
        out_specs=[block, pl.BlockSpec((2, PER, CZ), lambda i: (0, i, 0))],
        out_shape=[
            jax.ShapeDtypeStruct((LINES, CY, CZ), f32),
            jax.ShapeDtypeStruct((2, LINES, CZ), f32),
        ],
        scratch_shapes=[pltpu.VMEM((PER * CY, CZ), f32)] * 2,
        compiler_params=pltpu.CompilerParams(vmem_limit_bytes=VMEM_LIMIT),
        name="y_sweeps",
    )(ranks, u, q, low, high, etas)


def ring_kernel(rank_ref, ends_ref, eta_ref, out_ref):
    rows = 2 * LINES // NGY
    upward = rank_ref[1] < NGY // 2
    decay, _ = root_of(jnp.broadcast_to(eta_ref[1:2, :], (8, CZ)))
    whole = power_64(decay)
    turn = whole
    for _ in range(4):
        turn = turn * turn
    closing = 1.0 / (1.0 - turn)
    for part in range(rows // 8):

        def at(node):
            return pl.ds(node * rows + part * 8, 8)

        up = jnp.zeros((8, CZ), f32)
        down = jnp.zeros((8, CZ), f32)
        for node in range(NGY):
            up = up * whole + ends_ref[at(node), :]
            down = down * whole + ends_ref[at(NGY - 1 - node), :]
        up = up * closing
        down = down * closing
        ups, downs = [], [None] * NGY
        for node in range(NGY):
            ups.append(up)
            up = up * whole + ends_ref[at(node), :]
            downs[NGY - 1 - node] = down
            down = down * whole + ends_ref[at(NGY - 1 - node), :]
        for node in range(NGY):
            out_ref[at(node), :] = jnp.where(upward, ups[node], downs[node])


def ring_scan(ranks, ends, etas):
    return pl.pallas_call(
        ring_kernel,
        in_specs=[
            pl.BlockSpec(memory_space=pltpu.SMEM),
            pl.BlockSpec(memory_space=pltpu.VMEM),
            pl.BlockSpec(memory_space=pltpu.VMEM),
        ],
        out_specs=pl.BlockSpec(memory_space=pltpu.VMEM),
        out_shape=jax.ShapeDtypeStruct(ends.shape, f32),
        name="ring_scan",
    )(ranks, ends, etas)


def coefficient_kernel(rank_ref, eta_ref, table_ref, weight_ref, vector_ref, share_ref):
    rank = rank_ref[0]
    lane, row = lanes(), rows_of()
    eta = pltpu.roll(eta_ref[...], lax.rem(rank + 5, 8), 0)

    def before(x, fill):
        y = pltpu.roll(x, 1, 1)
        return jnp.where(lane == 0, jnp.where(row == 0, fill, pltpu.roll(y, 1, 0)), y)

    def after(x, fill):
        y = pltpu.roll(x, CZ - 1, 1)
        edge = jnp.where(row == NGZ - 1, fill, pltpu.roll(y, NGZ - 1, 0))
        return jnp.where(lane == CZ - 1, edge, y)

    def last_of(x, end):
        return jnp.broadcast_to(x[:, end : end + 1], (8, CZ))

    face_low = z_rate * 0.5 * (before(eta, 0.0) + eta)
    face_high = z_rate * 0.5 * (eta + after(eta, 0.0))

    def pivots(face, up):
        scale = 1.0 / (1.0 + face)
        a = jnp.ones((8, CZ), f32)
        b = face * scale
        c = scale
        d = b
        step = 1
        while step < CZ:
            shift = step if up else CZ - step
            inside = lane >= step if up else lane < CZ - step
            pa, pb, pc, pd = (pltpu.roll(x, shift, 1) for x in (a, b, c, d))
            na, nb = a * pa + b * pc, a * pb + b * pd
            nc, nd = c * pa + d * pc, c * pb + d * pd
            a, b = jnp.where(inside, na, a), jnp.where(inside, nb, b)
            c, d = jnp.where(inside, nc, c), jnp.where(inside, nd, d)
            step *= 2
        end = CZ - 1 if up else 0
        ta, tb, tc, td = (last_of(x, end) for x in (a, b, c, d))
        edge = row == (0 if up else NGZ - 1)
        va, vc = jnp.ones((8, CZ), f32), jnp.zeros((8, CZ), f32)
        for _ in range(NGZ - 1):
            na, nc = ta * va + tb * vc, tc * va + td * vc
            size = 1.0 / (na + nc)
            shift = 1 if up else NGZ - 1
            va = jnp.where(edge, 1.0, pltpu.roll(na * size, shift, 0))
            vc = jnp.where(edge, 0.0, pltpu.roll(nc * size, shift, 0))
        return (a * va + b * vc) / (c * va + d * vc)

    delta_up = pivots(face_low, True)
    delta_down = pivots(face_high, False)
    inverse = 1.0 / (delta_up + delta_down - 1.0)
    first_cell = (lane == 0) & (row == 0)
    last_cell = (lane == CZ - 1) & (row == NGZ - 1)
    link_up = jnp.where(first_cell, 0.0, face_low / (face_low + before(delta_up, 1.0)))
    link_down = jnp.where(last_cell, 0.0, face_high / (face_high + after(delta_down, 1.0)))

    def running(x, up):
        step = 1
        while step < CZ:
            moved = pltpu.roll(x, step if up else CZ - step, 1)
            x = jnp.where(lane >= step if up else lane < CZ - step, x * moved, x)
            step *= 2
        return x

    product_up, product_down = running(link_up, True), running(link_down, False)
    across_up, across_down = last_of(product_up, CZ - 1), last_of(product_down, 0)
    share_up = jnp.zeros((8, CZ), f32)
    share_down = jnp.zeros((8, CZ), f32)
    for _ in range(NGZ - 1):
        moved = pltpu.roll(across_up * share_up, NGZ - 1, 0)
        share_up = jnp.where(row == rank - 1, 1.0, jnp.where(row < rank - 1, moved, 0.0))
        moved = pltpu.roll(across_down * share_down, 1, 0)
        share_down = jnp.where(row == rank + 1, 1.0, jnp.where(row > rank + 1, moved, 0.0))
    back = lax.rem(NGZ - rank, NGZ)
    share_ref[0] = pltpu.roll(share_up, back, 0)
    share_ref[1] = pltpu.roll(share_down, back, 0)

    def own(x):
        return jnp.sum(jnp.where(row == rank, x, 0.0), axis=0, keepdims=True)

    scale = own(inverse)
    vector_ref[0:1, :] = own(product_up) * scale
    vector_ref[1:2, :] = own(product_down) * scale

    square = (CZ, CZ)
    lane_sq, row_sq = lanes(square), rows_of(square)
    identity = jnp.where(lane_sq == row_sq, 1.0, 0.0).astype(f32)

    def triangle(link, up):
        link = jnp.where(lanes((1, CZ)) == (0 if up else CZ - 1), 0.0, link)
        link = jnp.broadcast_to(link, (8, CZ))
        out = identity
        step = 1
        while step < CZ:
            shift = step if up else CZ - step
            out = out + jnp.broadcast_to(link[0:1, :], square) * pltpu.roll(out, shift, 1)
            link = link * pltpu.roll(link, shift, 1)
            step *= 2
        return out

    lower, upper = triangle(own(link_up), True), triangle(own(link_down), False)
    green = 2.0 * (lower + upper - identity) * jnp.broadcast_to(scale, square)
    ends = 2.0 * jnp.where(
        lane_sq < CZ // 2,
        jnp.broadcast_to(lower[:, CZ - 1 : CZ], square),
        jnp.broadcast_to(upper[:, 0:1], square),
    )
    for half, matrix in enumerate((green, ends)):
        high, mid, low = split_3(matrix)
        columns = pl.ds(half * CZ, CZ)
        for place, part in enumerate((high, high, mid, mid, high, low)):
            weight_ref[pl.ds(place * CZ, CZ), columns] = part

    decay, peak = root_of(own(eta))
    tall = (CY, CZ)
    y = rows_of(tall)
    powers_up = jnp.broadcast_to(peak * decay, tall)
    powers_down = powers_up
    factor = decay
    for bit in range(6):
        wide = jnp.broadcast_to(factor, tall)
        powers_up = jnp.where((y >> bit) & 1 == 1, powers_up * wide, powers_up)
        powers_down = jnp.where(((CY - 1 - y) >> bit) & 1 == 1, powers_down * wide, powers_down)
        factor = factor * factor
    table_ref[0] = powers_up
    table_ref[1] = powers_down


def coefficients(ranks, etas):
    vmem = pl.BlockSpec(memory_space=pltpu.VMEM)
    return pl.pallas_call(
        coefficient_kernel,
        in_specs=[pl.BlockSpec(memory_space=pltpu.SMEM), vmem],
        out_specs=[vmem] * 4,
        out_shape=[
            jax.ShapeDtypeStruct((2, CY, CZ), f32),
            jax.ShapeDtypeStruct((6 * CZ, 2 * CZ), bf16),
            jax.ShapeDtypeStruct((8, CZ), f32),
            jax.ShapeDtypeStruct((2, NGZ, CZ), f32),
        ],
        name="z_coefficients",
    )(ranks, etas)


def solve_kernel(rank_ref, m_ref, u_ref, carry_ref, table_ref, weight_ref, out_ref, *rest):
    message_refs, left = rest[: NGZ - 1], rest[NGZ - 1]
    rank = rank_ref[0]
    lane = lanes()

    def pair(p, _):
        packed = []
        for half in range(2):
            for c in range(GROUP):
                line = (2 * p + half) * GROUP + c
                tall = (CY, CZ)
                carry_up = jnp.broadcast_to(carry_ref[0, pl.ds(line, 1), :], tall)
                carry_down = jnp.broadcast_to(carry_ref[1, pl.ds(line, 1), :], tall)
                change = m_ref[line] - u_ref[line]
                change = change + table_ref[0] * carry_up + table_ref[1] * carry_down
                high, mid, low = split_3(change)
                at = pl.ds(c * CY, CY)
                left[at, 0:CZ] = high
                left[at, CZ : 2 * CZ] = mid
                left[at, 2 * CZ : 3 * CZ] = low
                left[at, 3 * CZ : 4 * CZ] = high
            near = left[:, : 2 * CZ]
            result = jnp.dot(near, weight_ref[: 2 * CZ], preferred_element_type=f32)
            result += jnp.dot(near, weight_ref[2 * CZ : 4 * CZ], preferred_element_type=f32)
            result += jnp.dot(
                left[:, 2 * CZ :], weight_ref[4 * CZ :], preferred_element_type=f32
            )
            for c in range(GROUP):
                line = (2 * p + half) * GROUP + c
                out_ref[line] = u_ref[line] + result[c * CY : (c + 1) * CY, :CZ]
            acc = jnp.zeros((8, CZ), f32)
            for k in range(TILES):
                acc = jnp.where(lane % 64 == k, result[8 * k : 8 * k + 8, CZ:], acc)
            packed.append(acc)
        first, second = packed
        up = jnp.where(lane < 64, first, pltpu.roll(second, 64, 1))
        down = jnp.where(lane < 64, pltpu.roll(first, 64, 1), second)
        for k in range(1, NGZ):
            message_refs[k - 1][p] = jnp.where(rank >= k, down, up)
        return 0

    lax.fori_loop(0, PAIRS, pair, 0)


def local_solve(ranks, m, u, carries, table, weight):
    block = pl.BlockSpec((PER, CY, CZ), lambda i: (i, 0, 0))
    message = pl.BlockSpec((PAIRS, 8, CZ), lambda i: (i, 0, 0))
    return pl.pallas_call(
        solve_kernel,
        grid=(STEPS,),
        in_specs=[
            pl.BlockSpec(memory_space=pltpu.SMEM),
            block,
            block,
            pl.BlockSpec((2, PER, CZ), lambda i: (0, i, 0)),
            pl.BlockSpec((2, CY, CZ), lambda i: (0, 0, 0)),
            pl.BlockSpec((6 * CZ, 2 * CZ), lambda i: (0, 0)),
        ],
        out_specs=[block] + [message] * (NGZ - 1),
        out_shape=[jax.ShapeDtypeStruct((LINES, CY, CZ), f32)]
        + [jax.ShapeDtypeStruct((LINES // 16, 8, CZ), f32)] * (NGZ - 1),
        scratch_shapes=[pltpu.VMEM((GROUP * CY, 4 * CZ), bf16)],
        compiler_params=pltpu.CompilerParams(vmem_limit_bytes=VMEM_LIMIT),
        name="z_local_solve",
    )(ranks, m, u, carries, table, weight)


def finish_kernel(y_ref, vector_ref, share_ref, *rest):
    got, out_ref = rest[: NGZ - 1], rest[NGZ - 1]
    lane = lanes()
    left = jnp.broadcast_to(vector_ref[0:1, :], (8, CZ))
    right = jnp.broadcast_to(vector_ref[1:2, :], (8, CZ))

    def pair(p, _):
        up = jnp.zeros((8, CZ), f32)
        down = jnp.zeros((8, CZ), f32)
        for k in range(1, NGZ):
            value = got[k - 1][p]
            up += jnp.broadcast_to(share_ref[0, k : k + 1, :], (8, CZ)) * value
            down += jnp.broadcast_to(share_ref[1, k : k + 1, :], (8, CZ)) * value
        both = (
            jnp.where(lane < 64, up, pltpu.roll(down, 64, 1)),
            jnp.where(lane < 64, pltpu.roll(up, 64, 1), down),
        )
        for half in range(2):
            for k in range(TILES):
                line = (2 * p + half) * GROUP + k // 8
                at = pl.ds((k % 8) * 8, 8)
                low = jnp.broadcast_to(both[half][:, k : k + 1], (8, CZ))
                high = jnp.broadcast_to(both[half][:, 64 + k : 65 + k], (8, CZ))
                out_ref[line, at, :] = y_ref[line, at, :] + low * left + high * right
        return 0

    lax.fori_loop(0, PAIRS, pair, 0)


def finish(y, vector, share, got):
    block = pl.BlockSpec((PER, CY, CZ), lambda i: (i, 0, 0))
    message = pl.BlockSpec((PAIRS, 8, CZ), lambda i: (i, 0, 0))
    return pl.pallas_call(
        finish_kernel,
        grid=(STEPS,),
        in_specs=[
            block,
            pl.BlockSpec((8, CZ), lambda i: (0, 0)),
            pl.BlockSpec((2, NGZ, CZ), lambda i: (0, 0, 0)),
        ]
        + [message] * (NGZ - 1),
        out_specs=block,
        out_shape=jax.ShapeDtypeStruct((LINES, CY, CZ), f32),
        compiler_params=pltpu.CompilerParams(vmem_limit_bytes=VMEM_LIMIT),
        name="z_carries",
    )(y, vector, share, *got)


def shifted(x, axis, by, wrap=True):
    n = lax.axis_size(axis)
    pairs = [(i, (i + by) % n) for i in range(n) if wrap or 0 <= i + by < n]
    return lax.ppermute(x, axis, pairs)


def body(fields, source_term, resistivity):
    u = fields.reshape(LINES, CY, CZ)
    q = source_term.reshape(LINES, CY, CZ)
    ranks = jnp.stack([lax.axis_index("gz"), lax.axis_index("gy")]).astype(jnp.int32)
    own = resistivity.reshape(1, CZ)
    prev_eta, next_eta = shifted(own, "gz", 1), shifted(own, "gz", -1)
    near = jnp.concatenate([prev_eta, own, next_eta, jnp.zeros((5, CZ), f32)], axis=0)
    up, down = end_columns(u)
    low = shifted(up, "gz", 1, wrap=False)
    high = shifted(down, "gz", -1, wrap=False)
    far_low, far_high = shifted(near, "gz", 3), shifted(near, "gz", -3)
    all_eta = jnp.concatenate([far_low[1:3], near[:3], far_high[:3]], axis=0)
    table, weight, vector, share = coefficients(ranks, all_eta)
    m, ends = sweeps(ranks, u, q, low, high, near)
    nodes = lax.all_to_all(ends.reshape(2 * LINES, CZ), "gy", 0, 0, tiled=True)
    nodes = ring_scan(ranks, nodes, near)
    carries = lax.all_to_all(nodes, "gy", 0, 0, tiled=True).reshape(2, LINES, CZ)
    y, *messages = local_solve(ranks, m, u, carries, table, weight)
    got = [shifted(x, "gz", -k) for k, x in enumerate(messages, start=1)]
    return finish(y, vector, share, got).reshape(fields.shape)


def solution(mesh):
    return jax.shard_map(
        body,
        mesh=mesh,
        in_specs=(P(None, None, "gy", "gz"), P(None, None, "gy", "gz"), P("gz")),
        out_specs=P(None, None, "gy", "gz"),
        check_vma=False,
    )
```

profile of v0, /device:TPU:1, one launch (start us, length us, event | category | flops | bytes accessed | tf_op | source)
XLA Modules:
  0.0 115.7 jit_solution(3678263274843991594)
XLA Ops:
  0.0 1.4 %collective-permute-start.3 = (f32[1,128]{1,0:T(1,128)}, f32[1,128]{1,0:T(1,128)S(1)}, u32[]{:S(2)}, u32[]{:S(2)}) collective-permute-start(f32[1,128]{1,0:T(1,128)} %bitcast.18), channel_id=1, source_target_pairs={{0,7},{1,0},{2,1},{3,2},{4,3},{5,4},{6,5},{7,6},{8,15},{9,8},{10,9... | collective-permute-start | bytes 1544 | tf_op jit(solution)/shard_map/ppermute | solution.py:488
  1.4 1.2 %collective-permute-start.2 = (f32[1,128]{1,0:T(1,128)}, f32[1,128]{1,0:T(1,128)S(1)}, u32[]{:S(2)}, u32[]{:S(2)}) collective-permute-start(f32[1,128]{1,0:T(1,128)} %bitcast.19), channel_id=1, source_target_pairs={{0,1},{1,2},{2,3},{3,4},{4,5},{5,6},{6,7},{7,0},{8,9},{9,10},{10,1... | collective-permute-start | bytes 1544 | tf_op jit(solution)/shard_map/ppermute | solution.py:488
  2.6 5.7 %end_columns.1 = (f32[12,8,128]{2,1,0:T(8,128)S(1)}, f32[12,8,128]{2,1,0:T(8,128)S(1)}) custom-call(f32[192,64,128]{2,1,0:T(8,128)} %bitcast.13), custom_call_target="tpu_custom_call" | custom-call | tf_op jit(solution)/shard_map/end_columns/pallas_call | solution.py:79
  8.3 2.7 %collective-permute-start = (f32[12,8,128]{2,1,0:T(8,128)S(1)}, f32[12,8,128]{2,1,0:T(8,128)S(1)}, u32[]{:S(2)}, u32[]{:S(2)}) collective-permute-start(f32[12,8,128]{2,1,0:T(8,128)S(1)} %get-tuple-element.21), channel_id=1, source_target_pairs={{0,1},{1,2},{2,3},{3,4},{4,5},{5,6},{6,7},{8,9},{9,10},{10,11},{11... | collective-permute-start | bytes 147464 | tf_op jit(solution)/shard_map/ppermute | solution.py:488
  11.0 1.9 %collective-permute-start.1 = (f32[12,8,128]{2,1,0:T(8,128)S(1)}, f32[12,8,128]{2,1,0:T(8,128)S(1)}, u32[]{:S(2)}, u32[]{:S(2)}) collective-permute-start(f32[12,8,128]{2,1,0:T(8,128)S(1)} %get-tuple-element.22), channel_id=1, source_target_pairs={{1,0},{2,1},{3,2},{4,3},{5,4},{6,5},{7,6},{9,8},{10,9},{11,10},{12... | collective-permute-start | bytes 147464 | tf_op jit(solution)/shard_map/ppermute | solution.py:488
  13.2 3.2 %collective-permute-done.1.high_ref = f32[12,8,128]{2,1,0:T(8,128)S(1)} collective-permute-done((f32[12,8,128]{2,1,0:T(8,128)S(1)}, f32[12,8,128]{2,1,0:T(8,128)S(1)}, u32[]{:S(2)}, u32[]{:S(2)}) %collective-permute-start.1) | collective-permute-done | bytes 49184 | tf_op jit(solution)/shard_map/ppermute | solution.py:488
  16.4 31.3 %y_sweeps.1 = (f32[192,64,128]{2,1,0:T(8,128)}, f32[2,192,128]{2,1,0:T(8,128)S(1)}) custom-call(s32[2]{0:T(128)S(1)} %pad_add_fusion.rank_ref, f32[192,64,128]{2,1,0:T(8,128)} %bitcast.14, bf16[192,64,128]{2,1,0:T(8,128)(2,1)S(1)} %bitcast.10, f32[12,8,128]{2,1,0:T(8,128)S(1)} %collective-permute-done.low_ref, ...), custom_call_target="tpu_custom_call" | custom-call | tf_op jit(solution)/shard_map/y_sweeps/pallas_call | solution.py:159
  47.7 14.7 %all_to_all.20 = f32[16,24,128]{2,1,0:T(8,128)} all-to-all(f32[16,24,128]{2,1,0:T(8,128)S(1)} %bitcast.12), channel_id=1, replica_groups=mesh['gy'=16,'gz'=8] {'gy'}, dimensions={0} | all-to-all | bytes 393216 | tf_op jit(solution)/shard_map/all_to_all | solution.py:505
  62.4 1.7 %ring_scan.1 = f32[384,128]{1,0:T(8,128)} custom-call(s32[2]{0:T(128)} %copy-done.4, f32[384,128]{1,0:T(8,128)} %bitcast.17, f32[8,128]{1,0:T(8,128)} %copy-done.3), custom_call_target="tpu_custom_call" | custom-call | tf_op jit(solution)/shard_map/ring_scan/pallas_call | solution.py:213
  64.1 3.5 %all-to-all-start.1 = ((f32[16,24,128]{2,1,0:T(8,128)}), f32[16,24,128]{2,1,0:T(8,128)S(1)}, u32[]{:S(2)}, u32[]{:S(2)}) async-start(f32[16,24,128]{2,1,0:T(8,128)} %bitcast.16), calls=%async_computation.1 | async-start | bytes 393216 | tf_op jit(solution)/shard_map/all_to_all | solution.py:507
  67.6 3.1 %collective-permute-start.5 = (f32[8,128]{1,0:T(8,128)}, f32[8,128]{1,0:T(8,128)S(1)}, u32[]{:S(2)}, u32[]{:S(2)}) collective-permute-start(f32[8,128]{1,0:T(8,128)} %copy-done.3), channel_id=1, source_target_pairs={{0,5},{1,6},{2,7},{3,0},{4,1},{5,2},{6,3},{7,4},{8,13},{9,14},{10,... | collective-permute-start | bytes 12296 | tf_op jit(solution)/shard_map/ppermute | solution.py:488
  70.8 0.9 collective-permute-start.4
  71.6 1.7 %collective-permute-done.5 = f32[8,128]{1,0:T(8,128)S(1)} collective-permute-done((f32[8,128]{1,0:T(8,128)}, f32[8,128]{1,0:T(8,128)S(1)}, u32[]{:S(2)}, u32[]{:S(2)}) %collective-permute-start.5) | collective-permute-done | bytes 4128 | tf_op jit(solution)/shard_map/ppermute | solution.py:488
  73.3 2.2 %collective-permute-done.4 = f32[8,128]{1,0:T(8,128)S(1)} collective-permute-done((f32[8,128]{1,0:T(8,128)}, f32[8,128]{1,0:T(8,128)S(1)}, u32[]{:S(2)}, u32[]{:S(2)}) %collective-permute-start.4) | collective-permute-done | bytes 4128 | tf_op jit(solution)/shard_map/ppermute | solution.py:488
  76.1 2.9 %z_coefficients.1 = (f32[2,64,128]{2,1,0:T(8,128)}, bf16[768,256]{1,0:T(8,128)(2,1)}, f32[8,128]{1,0:T(8,128)}, f32[2,8,128]{2,1,0:T(8,128)}) custom-call(s32[2]{0:T(128)} %copy-done.4, f32[8,128]{1,0:T(8,128)} %concatenate.9.eta_ref), custom_call_target="tpu_custom_call" | custom-call | tf_op jit(solution)/shard_map/z_coefficients/pallas_call | solution.py:356
  79.0 1.0 copy-done.1
  81.5 12.9 %z_local_solve.1 = (f32[192,64,128]{2,1,0:T(8,128)}, f32[12,8,128]{2,1,0:T(8,128)S(1)}, f32[12,8,128]{2,1,0:T(8,128)S(1)}, f32[12,8,128]{2,1,0:T(8,128)S(1)}, f3...) custom-call(s32[2]{0:T(128)S(1)} %copy-done.5, ...), custom_call_target="tpu_custom_call" | custom-call | tf_op jit(solution)/shard_map/z_local_solve/pallas_call | solution.py:417
  95.1 0.9 collective-permute-start.7
  96.2 2.3 %collective-permute-start.9 = (f32[12,8,128]{2,1,0:T(8,128)S(1)}, f32[12,8,128]{2,1,0:T(8,128)S(1)}, u32[]{:S(2)}, u32[]{:S(2)}) collective-permute-start(f32[12,8,128]{2,1,0:T(8,128)S(1)} %get-tuple-element.33), channel_id=1, source_target_pairs={{0,4},{1,5},{2,6},{3,7},{4,0},{5,1},{6,2},{7,3},{8,12},{9,13},{10,... | collective-permute-start | bytes 147464 | tf_op jit(solution)/shard_map/ppermute | solution.py:488
  98.5 0.9 collective-permute-start.10
  100.1 1.3 %collective-permute-start.12 = (f32[12,8,128]{2,1,0:T(8,128)S(1)}, f32[12,8,128]{2,1,0:T(8,128)S(1)}, u32[]{:S(2)}, u32[]{:S(2)}) collective-permute-start(f32[12,8,128]{2,1,0:T(8,128)S(1)} %get-tuple-element.36), channel_id=1, source_target_pairs={{0,1},{1,2},{2,3},{3,4},{4,5},{5,6},{6,7},{7,0},{8,9},{9,10},{10,1... | collective-permute-start | bytes 147464 | tf_op jit(solution)/shard_map/ppermute | solution.py:488
  101.4 1.8 %collective-permute-done.10.rest_4_ = f32[12,8,128]{2,1,0:T(8,128)S(1)} collective-permute-done((f32[12,8,128]{2,1,0:T(8,128)S(1)}, f32[12,8,128]{2,1,0:T(8,128)S(1)}, u32[]{:S(2)}, u32[]{:S(2)}) %collective-permute-start.10) | collective-permute-done | bytes 49184 | tf_op jit(solution)/shard_map/ppermute | solution.py:488
  103.3 2.0 %collective-permute-done.11.rest_5_ = f32[12,8,128]{2,1,0:T(8,128)S(1)} collective-permute-done((f32[12,8,128]{2,1,0:T(8,128)S(1)}, f32[12,8,128]{2,1,0:T(8,128)S(1)}, u32[]{:S(2)}, u32[]{:S(2)}) %collective-permute-start.11) | collective-permute-done | bytes 49184 | tf_op jit(solution)/shard_map/ppermute | solution.py:488
  105.3 10.4 %z_carries.1 = f32[192,64,128]{2,1,0:T(8,128)} custom-call(f32[192,64,128]{2,1,0:T(8,128)} %get-tuple-element.27.y_ref, f32[8,128]{1,0:T(8,128)S(1)} %copy-done.7, f32[2,8,128]{2,1,0:T(8,128)S(1)} %copy-done.6, f32[12,8,128]{2,1,0:T(8,128)S(1)} %collective-permute-done.6.rest_0_, f32[12,8,128]{2,1,0:T(8,128)S(1)} %collective-permute-done.7.rest_1_, ...), custom_call_target="tpu_custom_call" | custom-call | tf_op jit(solution)/shard_map/z_carries/pallas_call | solution.py:469
  (36 shorter events, 4.0 us)
Async XLA Ops:
  0.0 13.1 %copy-start.8 = (f32[128]{0:T(128)S(1)}, f32[128]{0:T(128)}, u32[]{:S(2)}) copy-start(f32[128]{0:T(128)} %param.5) | copy-start | bytes 1540
  0.0 16.4 %copy-start = (bf16[12,16,64,128]{3,2,1,0:T(8,128)(2,1)S(1)}, bf16[12,16,64,128]{3,2,1,0:T(8,128)(2,1)}, u32[]{:S(2)}) copy-start(bf16[12,16,64,128]{3,2,1,0:T(8,128)(2,1)} %param.4) | copy-start | bytes 9437188
  0.0 13.1 %collective-permute-start.3 = (f32[1,128]{1,0:T(1,128)}, f32[1,128]{1,0:T(1,128)S(1)}, u32[]{:S(2)}, u32[]{:S(2)}) collective-permute-start(f32[1,128]{1,0:T(1,128)} %bitcast.18), channel_id=1, source_target_pairs={{0,7},{1,0},{2,1},{3,2},{4,3},{5,4},{6,5},{7,6},{8,15},{9,8},{10,9... | collective-permute-start | bytes 1544 | tf_op jit(solution)/shard_map/ppermute | solution.py:488
  1.4 11.7 %collective-permute-start.2 = (f32[1,128]{1,0:T(1,128)}, f32[1,128]{1,0:T(1,128)S(1)}, u32[]{:S(2)}, u32[]{:S(2)}) collective-permute-start(f32[1,128]{1,0:T(1,128)} %bitcast.19), channel_id=1, source_target_pairs={{0,1},{1,2},{2,3},{3,4},{4,5},{5,6},{6,7},{7,0},{8,9},{9,10},{10,1... | collective-permute-start | bytes 1544 | tf_op jit(solution)/shard_map/ppermute | solution.py:488
  8.3 4.9 %collective-permute-start = (f32[12,8,128]{2,1,0:T(8,128)S(1)}, f32[12,8,128]{2,1,0:T(8,128)S(1)}, u32[]{:S(2)}, u32[]{:S(2)}) collective-permute-start(f32[12,8,128]{2,1,0:T(8,128)S(1)} %get-tuple-element.21), channel_id=1, source_target_pairs={{0,1},{1,2},{2,3},{3,4},{4,5},{5,6},{6,7},{8,9},{9,10},{10,11},{11... | collective-permute-start | bytes 147464 | tf_op jit(solution)/shard_map/ppermute | solution.py:488
  11.0 5.4 %collective-permute-start.1 = (f32[12,8,128]{2,1,0:T(8,128)S(1)}, f32[12,8,128]{2,1,0:T(8,128)S(1)}, u32[]{:S(2)}, u32[]{:S(2)}) collective-permute-start(f32[12,8,128]{2,1,0:T(8,128)S(1)} %get-tuple-element.22), channel_id=1, source_target_pairs={{1,0},{2,1},{3,2},{4,3},{5,4},{6,5},{7,6},{9,8},{10,9},{11,10},{12... | collective-permute-start | bytes 147464 | tf_op jit(solution)/shard_map/ppermute | solution.py:488
  13.0 49.4 %copy-start.4 = (s32[2]{0:T(128)}, s32[2]{0:T(128)S(1)}, u32[]{:S(2)}) copy-start(s32[2]{0:T(128)S(1)} %pad_add_fusion.rank_ref) | copy-start | bytes 28
  13.2 49.2 %copy-start.3 = (f32[8,128]{1,0:T(8,128)}, f32[8,128]{1,0:T(8,128)S(1)}, u32[]{:S(2)}) copy-start(f32[8,128]{1,0:T(8,128)S(1)} %maximum_maximum_fusion.eta_ref) | copy-start | bytes 12292
  64.1 14.9 %all-to-all-start.1 = ((f32[16,24,128]{2,1,0:T(8,128)}), f32[16,24,128]{2,1,0:T(8,128)S(1)}, u32[]{:S(2)}, u32[]{:S(2)}) async-start(f32[16,24,128]{2,1,0:T(8,128)} %bitcast.16), calls=%async_computation.1 | async-start | bytes 393216 | tf_op jit(solution)/shard_map/all_to_all | solution.py:507
  67.6 5.7 %collective-permute-start.5 = (f32[8,128]{1,0:T(8,128)}, f32[8,128]{1,0:T(8,128)S(1)}, u32[]{:S(2)}, u32[]{:S(2)}) collective-permute-start(f32[8,128]{1,0:T(8,128)} %copy-done.3), channel_id=1, source_target_pairs={{0,5},{1,6},{2,7},{3,0},{4,1},{5,2},{6,3},{7,4},{8,13},{9,14},{10,... | collective-permute-start | bytes 12296 | tf_op jit(solution)/shard_map/ppermute | solution.py:488
  70.8 4.7 %collective-permute-start.4 = (f32[8,128]{1,0:T(8,128)}, f32[8,128]{1,0:T(8,128)S(1)}, u32[]{:S(2)}, u32[]{:S(2)}) collective-permute-start(f32[8,128]{1,0:T(8,128)} %copy-done.3), channel_id=1, source_target_pairs={{0,3},{1,4},{2,5},{3,6},{4,7},{5,0},{6,1},{7,2},{8,11},{9,12},{10,... | collective-permute-start | bytes 12296 | tf_op jit(solution)/shard_map/ppermute | solution.py:488
  79.0 1.0 copy-start.1
  80.0 0.8 copy-start.2
  80.8 0.7 copy-start.5
  81.5 23.8 %copy-start.6 = (f32[2,8,128]{2,1,0:T(8,128)S(1)}, f32[2,8,128]{2,1,0:T(8,128)}, u32[]{:S(2)}) copy-start(f32[2,8,128]{2,1,0:T(8,128)} %get-tuple-element.29.share_ref) | copy-start | bytes 24580
  81.5 23.8 %copy-start.7 = (f32[8,128]{1,0:T(8,128)S(1)}, f32[8,128]{1,0:T(8,128)}, u32[]{:S(2)}) copy-start(f32[8,128]{1,0:T(8,128)} %get-tuple-element.28.vector_ref) | copy-start | bytes 12292
  94.4 5.0 %collective-permute-start.6 = (f32[12,8,128]{2,1,0:T(8,128)S(1)}, f32[12,8,128]{2,1,0:T(8,128)S(1)}, u32[]{:S(2)}, u32[]{:S(2)}) collective-permute-start(f32[12,8,128]{2,1,0:T(8,128)S(1)} %get-tuple-element.30), channel_id=1, source_target_pairs={{0,7},{1,0},{2,1},{3,2},{4,3},{5,4},{6,5},{7,6},{8,15},{9,8},{10,9... | collective-permute-start | bytes 147464 | tf_op jit(solution)/shard_map/ppermute | solution.py:488
  95.1 5.0 %collective-permute-start.7 = (f32[12,8,128]{2,1,0:T(8,128)S(1)}, f32[12,8,128]{2,1,0:T(8,128)S(1)}, u32[]{:S(2)}, u32[]{:S(2)}) collective-permute-start(f32[12,8,128]{2,1,0:T(8,128)S(1)} %get-tuple-element.31), channel_id=1, source_target_pairs={{0,6},{1,7},{2,0},{3,1},{4,2},{5,3},{6,4},{7,5},{8,14},{9,15},{10,... | collective-permute-start | bytes 147464 | tf_op jit(solution)/shard_map/ppermute | solution.py:488
  96.0 5.5 %collective-permute-start.8 = (f32[12,8,128]{2,1,0:T(8,128)S(1)}, f32[12,8,128]{2,1,0:T(8,128)S(1)}, u32[]{:S(2)}, u32[]{:S(2)}) collective-permute-start(f32[12,8,128]{2,1,0:T(8,128)S(1)} %get-tuple-element.32), channel_id=1, source_target_pairs={{0,5},{1,6},{2,7},{3,0},{4,1},{5,2},{6,3},{7,4},{8,13},{9,14},{10,... | collective-permute-start | bytes 147464 | tf_op jit(solution)/shard_map/ppermute | solution.py:488
  96.2 5.2 %collective-permute-start.9 = (f32[12,8,128]{2,1,0:T(8,128)S(1)}, f32[12,8,128]{2,1,0:T(8,128)S(1)}, u32[]{:S(2)}, u32[]{:S(2)}) collective-permute-start(f32[12,8,128]{2,1,0:T(8,128)S(1)} %get-tuple-element.33), channel_id=1, source_target_pairs={{0,4},{1,5},{2,6},{3,7},{4,0},{5,1},{6,2},{7,3},{8,12},{9,13},{10,... | collective-permute-start | bytes 147464 | tf_op jit(solution)/shard_map/ppermute | solution.py:488
  98.5 4.7 %collective-permute-start.10 = (f32[12,8,128]{2,1,0:T(8,128)S(1)}, f32[12,8,128]{2,1,0:T(8,128)S(1)}, u32[]{:S(2)}, u32[]{:S(2)}) collective-permute-start(f32[12,8,128]{2,1,0:T(8,128)S(1)} %get-tuple-element.34), channel_id=1, source_target_pairs={{0,3},{1,4},{2,5},{3,6},{4,7},{5,0},{6,1},{7,2},{8,11},{9,12},{10,... | collective-permute-start | bytes 147464 | tf_op jit(solution)/shard_map/ppermute | solution.py:488
  99.4 5.9 %collective-permute-start.11 = (f32[12,8,128]{2,1,0:T(8,128)S(1)}, f32[12,8,128]{2,1,0:T(8,128)S(1)}, u32[]{:S(2)}, u32[]{:S(2)}) collective-permute-start(f32[12,8,128]{2,1,0:T(8,128)S(1)} %get-tuple-element.35), channel_id=1, source_target_pairs={{0,2},{1,3},{2,4},{3,5},{4,6},{5,7},{6,0},{7,1},{8,10},{9,11},{10,... | collective-permute-start | bytes 147464 | tf_op jit(solution)/shard_map/ppermute | solution.py:488
  100.1 5.2 %collective-permute-start.12 = (f32[12,8,128]{2,1,0:T(8,128)S(1)}, f32[12,8,128]{2,1,0:T(8,128)S(1)}, u32[]{:S(2)}, u32[]{:S(2)}) collective-permute-start(f32[12,8,128]{2,1,0:T(8,128)S(1)} %get-tuple-element.36), channel_id=1, source_target_pairs={{0,1},{1,2},{2,3},{3,4},{4,5},{5,6},{6,7},{7,0},{8,9},{9,10},{10,1... | collective-permute-start | bytes 147464 | tf_op jit(solution)/shard_map/ppermute | solution.py:488
where the time goes:
time: 117 us; the launch traced here: 116 us
  Pallas kernels  64.9 us (55%)
  starting transfers between devices  21.7 us (19%)
  blocking collectives  14.7 us (13%)
  waiting for transfers between devices  11 us (9%)
  local copies, waits for them, and re-layouts  3.21 us (3%)
    pallas_call x1, Pallas kernels, sweeps(): pl.pallas_call(sweep_kernel, grid=(STEPS,), in_specs=[pl.BlockSpec(memory...  31.3 us
    ppermute x13, starting transfers between devices, shifted(): return lax.ppermute(x, axis, pairs)  18.2 us
    all_to_all x1, blocking collectives, body(): nodes = lax.all_to_all(ends.reshape(2 * LINES, CZ), 'gy', 0, 0, tiled=True)  14.7 us
    pallas_call x1, Pallas kernels, local_solve(): pl.pallas_call(solve_kernel, grid=(STEPS,), in_specs=[pl.BlockSpec(memory...  12.9 us
    ppermute x13, waiting for transfers between devices, shifted(): return lax.ppermute(x, axis, pairs)  11 us
    pallas_call x1, Pallas kernels, finish(): pl.pallas_call(finish_kernel, grid=(STEPS,), in_specs=[block, pl.BlockSpe...  10.4 us
    pallas_call x1, Pallas kernels, end_columns(): pl.pallas_call(columns_kernel, grid=(STEPS,), in_specs=[pl.BlockSpec((PER...  5.72 us
    all_to_all x1, starting transfers between devices, body(): lax.all_to_all(nodes, 'gy', 0, 0, tiled=True).reshape(2, LINES, CZ)  3.52 us
  transfers between devices with their start and end apart: 14, of which 5 were waited for; matrix products, arithmetic and copies ran while one was open for 1% of the time, Pallas kernels for 7%

commit v1 on v0

v1 whole, which is shorter than its diff:
```python
import jax
import jax.numpy as jnp
from jax import lax
from jax.experimental import pallas as pl
from jax.experimental.pallas import tpu as pltpu
from jax.sharding import PartitionSpec as P

f32 = jnp.float32
bf16 = jnp.bfloat16
z_rate = 1.0
y_rate = 0.25

LINES = 192
CY = 64
CZ = 128
GROUP = 8
PER = 32
STEPS = LINES // PER
SLOTS = 2
AHEAD = 3
PITCH = 65
NGY = 16
NGZ = 8


def lanes(shape=(8, CZ)):
    return lax.broadcasted_iota(jnp.int32, shape, len(shape) - 1)


def rows_of(shape=(8, CZ)):
    return lax.broadcasted_iota(jnp.int32, shape, 0)


def root_of(eta):
    k = y_rate * eta
    root = jnp.sqrt(1.0 + 4.0 * k)
    return 2.0 * k / (1.0 + 2.0 * k + root), 1.0 / root


def power_64(r):
    for _ in range(6):
        r = r * r
    return r


def split(x):
    high = x.astype(bf16)
    return high, (x - high.astype(f32)).astype(bf16)


def chunk(ref, step):
    return ref.at[pl.ds(step * PER, PER)]


def kernel_call(kernel, out_shape, out_specs, in_specs, scratch=(), name=None, us=1):
    return pl.pallas_call(
        kernel,
        in_specs=in_specs,
        out_specs=out_specs,
        out_shape=out_shape,
        scratch_shapes=list(scratch),
        compiler_params=pltpu.CompilerParams(vmem_limit_bytes=60 * 1024 * 1024),
        cost_estimate=pl.CostEstimate(flops=0, bytes_accessed=us * 3_000_000, transcendentals=0),
        name=name,
    )


def pipeline(fetches, stores, work, prepare=None):
    for i in range(AHEAD):
        for copy in fetches(i):
            copy.start()
    if prepare:
        prepare()

    def step(i, _):
        @pl.when(i + AHEAD < STEPS)
        def _():
            for copy in fetches(i + AHEAD):
                copy.start()

        for copy in fetches(i):
            copy.wait()
        work(i)
        for copy in stores(i):
            copy.start()
        return 0

    lax.fori_loop(0, STEPS, step, 0)

    def drain(i, _):
        for copy in stores(i):
            copy.wait()
        return 0

    lax.fori_loop(0, STEPS, drain, 0)


def pitched(ref, step):
    return ref.at[pl.ds(step * PER * PITCH, PER * PITCH)]


def no_copies(i):
    return ()


def unit_mask(tall):
    return (lanes(tall) & 63) == rows_of(tall)


VMEM = pl.BlockSpec(memory_space=pltpu.VMEM)
SMEM = pl.BlockSpec(memory_space=pltpu.SMEM)
HBM = pl.BlockSpec(memory_space=pltpu.HBM)
CUBE = jax.ShapeDtypeStruct((LINES, CY, CZ), f32)
FLAT = jax.ShapeDtypeStruct((LINES, CZ), f32)
PITCHED = (LINES * PITCH, CZ)
ROWS = LINES // 2


def sweep_kernel(
    u_hbm, q_hbm, eta_ref, m_hbm, ends_ref, columns_ref, u_ref, q_ref, m_ref, x_buf, f_buf, sems
):
    lane = lanes()
    place = ((lane + 1) >> 1) & 63

    def fetches(i):
        return (
            pltpu.make_async_copy(chunk(u_hbm, i), chunk(u_ref, i), sems.at[0, i]),
            pltpu.make_async_copy(chunk(q_hbm, i), chunk(q_ref, i), sems.at[1, i]),
        )

    def stores(i):
        return (pltpu.make_async_copy(pitched(m_ref, i), pitched(m_hbm, i), sems.at[2, i]),)

    eta = jnp.broadcast_to(eta_ref[...], (8, CZ))
    columns_ref[pl.ds(LINES, 8), :] = eta
    face_low = jnp.where(lane == 0, 0.0, z_rate * 0.5 * (pltpu.roll(eta, 1, 1) + eta))
    face_high = jnp.where(lane == CZ - 1, 0.0, z_rate * 0.5 * (eta + pltpu.roll(eta, CZ - 1, 1)))
    decay, peak = root_of(eta)
    groups = PER // GROUP

    def work(i):
        def rows(g):
            return pl.ds(pl.multiple_of(i * PER + g * GROUP, 8), GROUP)

        def right_side(g, _):
            acc = jnp.zeros((8, CZ), f32)
            for k in range(8 * GROUP):
                c, at = g * GROUP + k // 8, pl.ds((k % 8) * 8, 8)
                here = u_ref[i * PER + c, at, :]
                under = pltpu.roll(here, 1, 1)
                over = pltpu.roll(here, CZ - 1, 1)
                acc = jnp.where(place == k, pltpu.roll(here, 2 * k, 1) if k else here, acc)
                q = q_ref[i * PER + c, at, :].astype(f32)
                explicit = face_high * (over - here) - face_low * (here - under)
                x_buf[pl.ds(c * PITCH + (k % 8) * 8, 8), :] = here + explicit + q
            columns_ref[rows(g), :] = acc
            return 0

        lax.fori_loop(0, groups, right_side, 0)

        def at(g, y):
            return pl.ds(g * GROUP * PITCH + y, GROUP, stride=PITCH)

        def out(g, y):
            return pl.ds((i * PER + g * GROUP) * PITCH + y, GROUP, stride=PITCH)

        total = [jnp.zeros((8, CZ), f32) for _ in range(groups)]
        for y in range(CY):
            for g in range(groups):
                total[g] = total[g] * decay + x_buf[at(g, y), :]
                f_buf[at(g, y), :] = total[g]
        for g in range(groups):
            ends_ref[0, rows(g), :] = total[g]
        total = [jnp.zeros((8, CZ), f32) for _ in range(groups)]
        for y in reversed(range(CY)):
            for g in range(groups):
                kept = total[g] * decay
                total[g] = kept + x_buf[at(g, y), :]
                m_ref[out(g, y), :] = peak * (f_buf[at(g, y), :] + kept)
        for g in range(groups):
            ends_ref[1, rows(g), :] = total[g]

    pipeline(fetches, stores, work)


def sweeps(u, q, own):
    return kernel_call(
        sweep_kernel,
        [
            jax.ShapeDtypeStruct(PITCHED, f32),
            jax.ShapeDtypeStruct((2, LINES, CZ), f32),
            jax.ShapeDtypeStruct((LINES + 8, CZ), f32),
        ],
        [HBM, VMEM, VMEM],
        [HBM, HBM, VMEM],
        [
            pltpu.VMEM((LINES, CY, CZ), f32),
            pltpu.VMEM((LINES, CY, CZ), bf16),
            pltpu.VMEM(PITCHED, f32),
            pltpu.VMEM((PER * PITCH, CZ), f32),
            pltpu.VMEM((PER * PITCH, CZ), f32),
            pltpu.SemaphoreType.DMA((3, STEPS)),
        ],
        name="y_sweeps",
        us=12,
    )(u, q, own)


def raised(base, exponent, bits=6):
    out = jnp.ones_like(base)
    for bit in range(bits):
        out = jnp.where((exponent >> bit) & 1 == 1, out * base, out)
        base = base * base
    return out


def exact_dot(a, b):
    return jnp.dot(a, b, preferred_element_type=f32, precision=lax.Precision.HIGHEST)


def flux_place(l):
    return 8 * ((l >> 1) & 7) + (l >> 4), l & 1


def turned(x):
    lane, row = lanes(x.shape), rows_of(x.shape)
    for bit in range(3):
        rows, columns = 1 << bit, 16 << bit
        in_row, in_lane = (row >> bit) & 1, (lane >> (4 + bit)) & 1
        count = x.shape[0]
        forth = pltpu.roll(pltpu.roll(x, count - rows, 0), columns, 1)
        back = pltpu.roll(pltpu.roll(x, rows, 0), CZ - columns, 1)
        x = jnp.where(in_row == in_lane, x, jnp.where(in_row == 0, forth, back))
    return x


def repair_kernel(rank_ref, ends_ref, columns_ref, low_ref, high_ref, out_ref, flux_ref, near_ref):
    rank = rank_ref[0]
    square = (CZ, CZ)
    lane = lanes(square)
    inner_low, inner_high = rank > 0, rank < NGZ - 1
    own_eta, low_eta, high_eta = (
        ref[pl.ds(LINES, 8), :] for ref in (columns_ref, low_ref, high_ref)
    )
    row = rows_of()
    near_ref[...] = jnp.where(row == 0, low_eta, jnp.where(row == 1, own_eta, high_eta))
    own = own_eta[:1]
    low_eta = jnp.where(inner_low, low_eta[:1], 0.0)[:, CZ - 1 :]
    high_eta = jnp.where(inner_high, high_eta[:1], 0.0)[:, :1]
    face_low = jnp.broadcast_to(z_rate * 0.5 * (low_eta + own[:, :1]), (1, CZ))
    face_high = jnp.broadcast_to(z_rate * 0.5 * (own[:, CZ - 1 :] + high_eta), (1, CZ))
    even = lanes((LINES, CZ)) & 1 == 0
    low, high, columns = (ref[pl.ds(0, LINES), :] for ref in (low_ref, high_ref, columns_ref))
    outer = jnp.where(
        even,
        jnp.where(inner_low, pltpu.roll(low, 1, 1), 0.0),
        jnp.where(inner_high, pltpu.roll(high, 1, 1), 0.0),
    )
    inner = jnp.where(even, columns, pltpu.roll(columns, 2, 1))
    face = jnp.where(lanes((1, CZ)) & 1 == 0, face_low, face_high)
    flux = turned(jnp.broadcast_to(face, (LINES, CZ)) * (outer - inner))
    flux_ref[...] = flux
    decay, _ = root_of(own)
    y, side = flux_place(rows_of(square))
    base = jnp.where(
        side == 0,
        jnp.broadcast_to(decay[:, :1], square),
        jnp.broadcast_to(decay[:, CZ - 1 :], square),
    )
    place = lane == jnp.where(side == 0, 0, CZ - 1)
    out_ref[0] = ends_ref[0] + exact_dot(flux, jnp.where(place, raised(base, 63 - y), 0.0))
    out_ref[1] = ends_ref[1] + exact_dot(flux, jnp.where(place, raised(base, y), 0.0))


def repair(ranks, ends, columns, low, high):
    shapes = [
        jax.ShapeDtypeStruct((2, LINES, CZ), f32),
        FLAT,
        jax.ShapeDtypeStruct((NGZ, CZ), f32),
    ]
    call = kernel_call(repair_kernel, shapes, [VMEM] * 3, [SMEM] + [VMEM] * 4, name="repair")
    return call(ranks, ends, columns, low, high)


def ring_kernel(rank_ref, ends_ref, eta_ref, out_ref):
    rows = 2 * LINES // NGY
    upward = rank_ref[1] < NGY // 2
    decay, _ = root_of(jnp.broadcast_to(eta_ref[...], (8, CZ)))
    whole = power_64(decay)
    turn = whole
    for _ in range(4):
        turn = turn * turn
    closing = 1.0 / (1.0 - turn)
    for part in range(rows // 8):

        def at(node):
            return pl.ds(node * rows + part * 8, 8)

        up = jnp.zeros((8, CZ), f32)
        down = jnp.zeros((8, CZ), f32)
        for node in range(NGY):
            up = up * whole + ends_ref[at(node), :]
            down = down * whole + ends_ref[at(NGY - 1 - node), :]
        up = up * closing
        down = down * closing
        ups, downs = [], [None] * NGY
        for node in range(NGY):
            ups.append(up)
            up = up * whole + ends_ref[at(node), :]
            downs[NGY - 1 - node] = down
            down = down * whole + ends_ref[at(NGY - 1 - node), :]
        for node in range(NGY):
            out_ref[at(node), :] = jnp.where(upward, ups[node], downs[node])


def ring_scan(ranks, ends, own):
    shape = jax.ShapeDtypeStruct(ends.shape, f32)
    return kernel_call(ring_kernel, shape, VMEM, [SMEM, VMEM, VMEM], name="ring_scan")(
        ranks, ends, own
    )


def coefficient_kernel(
    rank_ref, near_ref, far_low_ref, far_high_ref,
    table_ref, green_ref, ends_ref, carry_ref, share_ref, spread_ref, reach_ref, eta_ref,
):
    rank = rank_ref[0]
    lane, row = lanes(), rows_of()
    eta_ref[0:2, :] = far_low_ref[1:3, :]
    eta_ref[2:5, :] = near_ref[0:3, :]
    eta_ref[5:8, :] = far_high_ref[0:3, :]
    eta = pltpu.roll(eta_ref[...], lax.rem(rank + 5, 8), 0)

    def before(x, fill):
        y = pltpu.roll(x, 1, 1)
        return jnp.where(lane == 0, jnp.where(row == 0, fill, pltpu.roll(y, 1, 0)), y)

    def after(x, fill):
        y = pltpu.roll(x, CZ - 1, 1)
        edge = jnp.where(row == NGZ - 1, fill, pltpu.roll(y, NGZ - 1, 0))
        return jnp.where(lane == CZ - 1, edge, y)

    def last_of(x, end):
        return jnp.broadcast_to(x[:, end : end + 1], (8, CZ))

    face_low = z_rate * 0.5 * (before(eta, 0.0) + eta)
    face_high = z_rate * 0.5 * (eta + after(eta, 0.0))

    def pivots(face, up):
        scale = 1.0 / (1.0 + face)
        a = jnp.ones((8, CZ), f32)
        b = face * scale
        c = scale
        d = b
        step = 1
        while step < CZ:
            shift = step if up else CZ - step
            inside = lane >= step if up else lane < CZ - step
            pa, pb, pc, pd = (pltpu.roll(x, shift, 1) for x in (a, b, c, d))
            na, nb = a * pa + b * pc, a * pb + b * pd
            nc, nd = c * pa + d * pc, c * pb + d * pd
            a, b = jnp.where(inside, na, a), jnp.where(inside, nb, b)
            c, d = jnp.where(inside, nc, c), jnp.where(inside, nd, d)
            step *= 2
        end = CZ - 1 if up else 0
        ta, tb, tc, td = (last_of(x, end) for x in (a, b, c, d))
        edge = row == (0 if up else NGZ - 1)
        va, vc = jnp.ones((8, CZ), f32), jnp.zeros((8, CZ), f32)
        for _ in range(NGZ - 1):
            na, nc = ta * va + tb * vc, tc * va + td * vc
            size = 1.0 / (na + nc)
            shift = 1 if up else NGZ - 1
            va = jnp.where(edge, 1.0, pltpu.roll(na * size, shift, 0))
            vc = jnp.where(edge, 0.0, pltpu.roll(nc * size, shift, 0))
        return (a * va + b * vc) / (c * va + d * vc)

    delta_up = pivots(face_low, True)
    delta_down = pivots(face_high, False)
    inverse = 1.0 / (delta_up + delta_down - 1.0)
    first_cell = (lane == 0) & (row == 0)
    last_cell = (lane == CZ - 1) & (row == NGZ - 1)
    link_up = jnp.where(first_cell, 0.0, face_low / (face_low + before(delta_up, 1.0)))
    link_down = jnp.where(last_cell, 0.0, face_high / (face_high + after(delta_down, 1.0)))

    def running(x, up):
        step = 1
        while step < CZ:
            moved = pltpu.roll(x, step if up else CZ - step, 1)
            x = jnp.where(lane >= step if up else lane < CZ - step, x * moved, x)
            step *= 2
        return x

    product_up, product_down = running(link_up, True), running(link_down, False)
    across_up, across_down = last_of(product_up, CZ - 1), last_of(product_down, 0)
    share_up = jnp.zeros((8, CZ), f32)
    share_down = jnp.zeros((8, CZ), f32)
    for _ in range(NGZ - 1):
        moved = pltpu.roll(across_up * share_up, NGZ - 1, 0)
        share_up = jnp.where(row == rank - 1, 1.0, jnp.where(row < rank - 1, moved, 0.0))
        moved = pltpu.roll(across_down * share_down, 1, 0)
        share_down = jnp.where(row == rank + 1, 1.0, jnp.where(row > rank + 1, moved, 0.0))

    def own(x):
        return jnp.sum(jnp.where(row == rank, x, 0.0), axis=0, keepdims=True)

    scale = own(inverse)
    own_up, own_down = own(link_up), own(link_down)
    share_ref[0] = share_up * jnp.broadcast_to(own_up[:, :1], (8, CZ))
    share_ref[1] = share_down * jnp.broadcast_to(own_down[:, CZ - 1 :], (8, CZ))
    lane_1 = lanes((1, CZ))
    within_up = running(jnp.broadcast_to(jnp.where(lane_1 == 0, 1.0, own_up), (8, CZ)), True)
    within_down = running(
        jnp.broadcast_to(jnp.where(lane_1 == CZ - 1, 1.0, own_down), (8, CZ)), False
    )
    square = (CZ, CZ)
    lane_sq, row_sq = lanes(square), rows_of(square)
    carry = jnp.where(
        row_sq < CZ // 2,
        jnp.broadcast_to(within_up[:1] * scale, square),
        jnp.broadcast_to(within_down[:1] * scale, square),
    )
    identity = jnp.where(lane_sq == row_sq, 1.0, 0.0).astype(f32)

    def triangle(link, up):
        link = jnp.where(lanes((1, CZ)) == (0 if up else CZ - 1), 0.0, link)
        link = jnp.broadcast_to(link, (8, CZ))
        out = identity
        step = 1
        while step < CZ:
            shift = step if up else CZ - step
            out = out + jnp.broadcast_to(link[0:1, :], square) * pltpu.roll(out, shift, 1)
            link = link * pltpu.roll(link, shift, 1)
            step *= 2
        return out

    lower, upper = triangle(own_up, True), triangle(own_down, False)
    green = 2.0 * (lower + upper - identity) * jnp.broadcast_to(scale, square)
    ends = 2.0 * jnp.where(
        lane_sq < CZ // 2,
        jnp.broadcast_to(lower[:, CZ - 1 : CZ], square),
        jnp.broadcast_to(upper[:, 0:1], square),
    )
    for matrix, ref in ((green, green_ref), (ends, ends_ref), (carry, carry_ref)):
        for half, part in enumerate(split(matrix)):
            for rows in range(2):
                ref[pl.ds(rows * CZ, CZ), pl.ds(half * CZ, CZ)] = part

    decay, peak = root_of(own(eta))
    y = row_sq & 63
    wide = jnp.broadcast_to(decay, square)
    start = jnp.broadcast_to(peak * decay, square)
    response_up = start * raised(wide, y)
    response_down = start * raised(wide, 63 - y)
    table_ref[0] = response_up[:CY]
    table_ref[1] = response_down[:CY]
    seen = jnp.transpose(ends)
    reach_ref[0] = jnp.transpose(response_up * seen)
    reach_ref[1] = jnp.transpose(response_down * seen)
    y_in, side = flux_place(row_sq)
    low_side = side == 0
    base = jnp.where(
        low_side,
        jnp.broadcast_to(decay[:, :1], square),
        jnp.broadcast_to(decay[:, CZ - 1 :], square),
    )
    top = jnp.where(
        low_side,
        jnp.broadcast_to(peak[:, :1], square),
        jnp.broadcast_to(peak[:, CZ - 1 :], square),
    )
    apart = jnp.abs(y_in - (lane_sq & 63))
    spread = jnp.where(low_side == (lane_sq < CZ // 2), top * raised(base, apart), 0.0)
    spread_ref[0] = 2.0 * spread
    half = row_sq < CZ // 2
    same_y = (lane_sq & 63) == y
    first = jnp.broadcast_to(ends[0:1, :], square)
    final = jnp.broadcast_to(ends[CZ - 1 :, :], square)
    spread_ref[1] = exact_dot(spread, jnp.where(same_y, jnp.where(half, first, final), 0.0))


def coefficients(ranks, near, far_low, far_high):
    matrix = jax.ShapeDtypeStruct((2 * CZ, 2 * CZ), bf16)
    square = jax.ShapeDtypeStruct((2, CZ, CZ), f32)
    return kernel_call(
        coefficient_kernel,
        [
            jax.ShapeDtypeStruct((2, CY, CZ), f32),
            matrix,
            matrix,
            matrix,
            jax.ShapeDtypeStruct((2, NGZ, CZ), f32),
            square,
            square,
        ],
        [VMEM] * 7,
        [SMEM] + [VMEM] * 3,
        [pltpu.VMEM((NGZ, CZ), f32)],
        name="z_coefficients",
        us=3,
    )(ranks, near, far_low, far_high)


def split_rows(left_ref, rows, x):
    high, mid = split(x)
    left_ref[rows, 0:CZ] = high
    left_ref[rows, CZ : 2 * CZ] = mid


def halves(result):
    return result[:, :CZ] + result[:, CZ:]


def fetches_of(u_hbm, m_hbm, u_ref, m_ref, sems):
    def fetches(i):
        return (
            pltpu.make_async_copy(pitched(m_hbm, i), pitched(m_ref, i), sems.at[0, i]),
            pltpu.make_async_copy(chunk(u_hbm, i), chunk(u_ref, i), sems.at[1, i]),
        )

    return fetches


def sums_kernel(m_hbm, u_hbm, ends_ref, sums_ref, m_ref, u_ref, left_ref, sems):
    mask = unit_mask((CY, CZ))

    def work(i):
        for g in range(PER // GROUP):
            left = left_ref.at[g % SLOTS]
            first = i * PER + g * GROUP
            for c in range(GROUP):
                line = first + c
                change = m_ref[pl.ds(line * PITCH, CY), :] - u_ref[line]
                split_rows(left, pl.ds(c * CY, CY), change)
            result = halves(jnp.dot(left[...], ends_ref[...], preferred_element_type=f32))
            for c in range(GROUP):
                part = jnp.where(mask, result[c * CY : (c + 1) * CY], 0.0)
                sums_ref[pl.ds(first + c, 1), :] = jnp.sum(part, axis=0, keepdims=True)

    pipeline(fetches_of(u_hbm, m_hbm, u_ref, m_ref, sems), no_copies, work)


def local_sums(m, u, ends):
    return kernel_call(
        sums_kernel,
        FLAT,
        VMEM,
        [HBM, HBM, VMEM],
        [
            pltpu.VMEM(PITCHED, f32),
            pltpu.VMEM((LINES, CY, CZ), f32),
            pltpu.VMEM((SLOTS, GROUP * CY, 2 * CZ), bf16),
            pltpu.SemaphoreType.DMA((2, STEPS)),
        ],
        name="z_local_sums",
        us=8,
    )(m, u, ends)


def messages_kernel(
    rank_ref, sums_ref, carry_ref, reach_ref, flux_ref, spread_ref, out_ref, layer_ref
):
    rank = rank_ref[0]
    flux = flux_ref[...]
    layer_ref[...] = exact_dot(flux, spread_ref[0])
    sums = sums_ref[...] + exact_dot(flux, spread_ref[1])
    sums = sums + exact_dot(carry_ref[0], reach_ref[0])
    sums = sums + exact_dot(carry_ref[1], reach_ref[1])
    first, second = sums[:ROWS], sums[ROWS:]
    lower = lanes((ROWS, CZ)) < 64
    up = jnp.where(lower, first, pltpu.roll(second, 64, 1))
    down = jnp.where(lower, pltpu.roll(first, 64, 1), second)
    for k in range(NGZ):
        out_ref[k] = jnp.where(rank > k, down, up)


def messages_of(ranks, sums, carries, reach, flux, spread):
    shapes = [jax.ShapeDtypeStruct((NGZ, ROWS, CZ), f32), FLAT]
    call = kernel_call(messages_kernel, shapes, [VMEM] * 2, [SMEM] + [VMEM] * 5, name="z_messages")
    return call(ranks, sums, carries, reach, flux, spread)


def solve_kernel(
    m_hbm, u_hbm, carry_ref, table_ref, green_ref, y_hbm, m_ref, u_ref, y_ref, left_ref, sems
):
    tall = (CY, CZ)

    def stores(i):
        return (pltpu.make_async_copy(chunk(y_ref, i), chunk(y_hbm, i), sems.at[2, i]),)

    def work(i):
        for g in range(PER // GROUP):
            left = left_ref.at[g % SLOTS]
            first = i * PER + g * GROUP
            for c in range(GROUP):
                line = first + c
                carry_up = jnp.broadcast_to(carry_ref[0, pl.ds(line, 1), :], tall)
                carry_down = jnp.broadcast_to(carry_ref[1, pl.ds(line, 1), :], tall)
                change = m_ref[pl.ds(line * PITCH, CY), :] - u_ref[line]
                change = change + table_ref[0] * carry_up + table_ref[1] * carry_down
                split_rows(left, pl.ds(c * CY, CY), change)
            result = halves(jnp.dot(left[...], green_ref[...], preferred_element_type=f32))
            for c in range(GROUP):
                y_ref[first + c] = u_ref[first + c] + result[c * CY : (c + 1) * CY]

    pipeline(fetches_of(u_hbm, m_hbm, u_ref, m_ref, sems), stores, work)


def local_solve(m, u, carries, table, green):
    return kernel_call(
        solve_kernel,
        CUBE,
        HBM,
        [HBM, HBM] + [VMEM] * 3,
        [
            pltpu.VMEM(PITCHED, f32),
            pltpu.VMEM((LINES, CY, CZ), f32),
            pltpu.VMEM((LINES, CY, CZ), f32),
            pltpu.VMEM((SLOTS, GROUP * CY, 2 * CZ), bf16),
            pltpu.SemaphoreType.DMA((3, STEPS)),
        ],
        name="z_local_solve",
        us=8,
    )(m, u, carries, table, green)


def finish_kernel(
    y_hbm, matrix_ref, share_ref, layer_ref, got_ref,
    out_hbm, y_ref, out_ref, left_ref, high_ref, mid_ref, sems,
):
    lower = lanes((ROWS, CZ)) < 64
    tall = (CY, CZ)
    mask = unit_mask(tall)

    def fetches(i):
        return (pltpu.make_async_copy(chunk(y_hbm, i), chunk(y_ref, i), sems.at[0, i]),)

    def stores(i):
        return (pltpu.make_async_copy(chunk(out_ref, i), chunk(out_hbm, i), sems.at[1, i]),)

    def prepare():
        up = jnp.zeros((ROWS, CZ), f32)
        down = jnp.zeros((ROWS, CZ), f32)
        for k in range(NGZ):
            value = got_ref[k]
            up += jnp.broadcast_to(share_ref[0, k : k + 1, :], (ROWS, CZ)) * value
            down += jnp.broadcast_to(share_ref[1, k : k + 1, :], (ROWS, CZ)) * value
        both = (
            jnp.where(lower, up, pltpu.roll(down, 64, 1)),
            jnp.where(lower, pltpu.roll(up, 64, 1), down),
        )
        for half in range(2):
            at = pl.ds(half * ROWS, ROWS)
            high, mid = split(both[half] + layer_ref[at, :])
            high_ref[at, :] = high.astype(f32)
            mid_ref[at, :] = mid.astype(f32)

    def work(i):
        for g in range(PER // GROUP):
            left = left_ref.at[g % SLOTS]
            first = i * PER + g * GROUP
            for c in range(GROUP):
                line = pl.ds(first + c, 1)
                at = pl.ds(c * CY, CY)
                high = jnp.broadcast_to(high_ref[line, :], tall)
                mid = jnp.broadcast_to(mid_ref[line, :], tall)
                left[at, 0:CZ] = jnp.where(mask, high, 0.0).astype(bf16)
                left[at, CZ:] = jnp.where(mask, mid, 0.0).astype(bf16)
            result = halves(jnp.dot(left[...], matrix_ref[...], preferred_element_type=f32))
            for c in range(GROUP):
                out_ref[first + c] = y_ref[first + c] + result[c * CY : (c + 1) * CY]

    pipeline(fetches, stores, work, prepare)


def finish(y, matrix, share, layer, got):
    return kernel_call(
        finish_kernel,
        CUBE,
        HBM,
        [HBM] + [VMEM] * 4,
        [
            pltpu.VMEM((LINES, CY, CZ), f32),
            pltpu.VMEM((LINES, CY, CZ), f32),
            pltpu.VMEM((SLOTS, GROUP * CY, 2 * CZ), bf16),
            pltpu.VMEM((LINES, CZ), f32),
            pltpu.VMEM((LINES, CZ), f32),
            pltpu.SemaphoreType.DMA((2, STEPS)),
        ],
        name="z_carries",
        us=8,
    )(y, matrix, share, layer, got)


def shifted(x, axis, by):
    n = lax.axis_size(axis)
    return lax.ppermute(x, axis, [(i, (i + by) % n) for i in range(n)])


def body(fields, source_term, resistivity):
    u = fields.reshape(LINES, CY, CZ)
    q = source_term.reshape(LINES, CY, CZ)
    ranks = jnp.stack([lax.axis_index("gz"), lax.axis_index("gy")]).astype(jnp.int32)
    own = resistivity.reshape(1, CZ)
    m, ends, columns = sweeps(u, q, own)
    low, high = shifted(columns, "gz", 1), shifted(columns, "gz", -1)
    ends, flux, near = repair(ranks, ends, columns, low, high)
    nodes = lax.all_to_all(ends.reshape(2 * LINES, CZ), "gy", 0, 0, tiled=True)
    far_low, far_high = shifted(near, "gz", 3), shifted(near, "gz", -3)
    table, green, last, vector, share, spread, reach = coefficients(ranks, near, far_low, far_high)
    nodes = ring_scan(ranks, nodes, own)
    carries = lax.all_to_all(nodes, "gy", 0, 0, tiled=True).reshape(2, LINES, CZ)
    sums = local_sums(m, u, last)
    messages, layer = messages_of(ranks, sums, carries, reach, flux, spread)
    got = lax.all_to_all(messages.reshape(NGZ * ROWS, CZ), "gz", 0, 0, tiled=True)
    y = local_solve(m, u, carries, table, green)
    got = got.reshape(NGZ, ROWS, CZ)
    return finish(y, vector, share, layer, got).reshape(fields.shape)


def solution(mesh):
    return jax.shard_map(
        body,
        mesh=mesh,
        in_specs=(P(None, None, "gy", "gz"), P(None, None, "gy", "gz"), P("gz")),
        out_specs=P(None, None, "gy", "gz"),
        check_vma=False,
    )
```

time: 117 us -> 86.5 us (0.74)
  Pallas kernels: 64.9 us -> 45.8 us
  starting transfers between devices: 21.7 us -> 15.3 us
  waiting for transfers between devices: 11 us -> 6.73 us
    pallas_call x6 -> x8, Pallas kernels: 64.9 us -> 45.8 us  [the longest x1 12 us: sweeps(): kernel_call(sweep_kernel, [jax.ShapeDtypeStruct(PITCHED, f32), jax.ShapeD...]
    ppermute x13 -> x4, starting transfers between devices: 18.2 us -> 8.18 us  [shifted(): return lax.ppermute(x, axis, [(i, (i + by) % n) for i in range(n)])]
    ppermute x13 -> x4, waiting for transfers between devices: 11 us -> 6.72 us  [shifted(): return lax.ppermute(x, axis, [(i, (i + by) % n) for i in range(n)])]
    all_to_all x0 -> x1, starting transfers between devices: none -> 3.58 us  [body(): lax.all_to_all(messages.reshape(NGZ * ROWS, CZ), 'gz', 0, 0, tiled=True)]
    unnamed x18 -> x12, local copies, waits for them, and re-layouts: 2.52 us -> 2.69 us
  transfers between devices with their start and end apart: 14 -> 6, of which waited for: 5 -> 3; matrix products, arithmetic and copies ran while one was open for 1% -> 1% of each run, Pallas kernels for 7% -> 23%
where the time goes in v1:
time: 86.5 us; the launch traced here: 85.9 us
  Pallas kernels  45.8 us (53%)
  starting transfers between devices  15.3 us (18%)
  blocking collectives  14.8 us (17%)
  waiting for transfers between devices  6.73 us (8%)
  local copies, waits for them, and re-layouts  2.69 us (3%)
    all_to_all x1, blocking collectives, body(): nodes = lax.all_to_all(ends.reshape(2 * LINES, CZ), 'gy', 0, 0, tiled=True)  14.8 us
    pallas_call x1, Pallas kernels, sweeps(): kernel_call(sweep_kernel, [jax.ShapeDtypeStruct(PITCHED, f32), jax.ShapeD...  12 us
    pallas_call x1, Pallas kernels, local_solve(): kernel_call(solve_kernel, CUBE, HBM, [HBM, HBM] + [VMEM] * 3, [pltpu.VMEM...  9.19 us
    ppermute x4, starting transfers between devices, shifted(): return lax.ppermute(x, axis, [(i, (i + by) % n) for i in range(n)])  8.18 us
    pallas_call x1, Pallas kernels, finish(): kernel_call(finish_kernel, CUBE, HBM, [HBM] + [VMEM] * 4, [pltpu.VMEM((LI...  7.54 us
    pallas_call x1, Pallas kernels, local_sums(): kernel_call(sums_kernel, FLAT, VMEM, [HBM, HBM, VMEM], [pltpu.VMEM(PITCHE...  7.08 us
    ppermute x4, waiting for transfers between devices, shifted(): return lax.ppermute(x, axis, [(i, (i + by) % n) for i in range(n)])  6.72 us
    all_to_all x1, starting transfers between devices, body(): lax.all_to_all(messages.reshape(NGZ * ROWS, CZ), 'gz', 0, 0, tiled=True)  3.58 us
  transfers between devices with their start and end apart: 6, of which 3 were waited for; matrix products, arithmetic and copies ran while one was open for 1% of the time, Pallas kernels for 23%

profile of v1, /device:TPU:1, one launch (start us, length us, event | category | flops | bytes accessed | tf_op | source)
XLA Modules:
  0.0 85.9 jit_solution(12291348238368238520)
XLA Ops:
  0.0 12.0 %y_sweeps.1 = (f32[12480,128]{1,0:T(8,128)}, f32[2,192,128]{2,1,0:T(8,128)}, f32[200,128]{1,0:T(8,128)}) custom-call(f32[192,64,128]{2,1,0:T(8,128)} %bitcast.10, bf16[192,64,128]{2,1,0:T(8,128)(2,1)} %bitcast.13, f32[1,128]{1,0:T(1,128)} %bitcast.19), custom_call_target="tpu_custom_call" | custom-call | bytes 36000000 | tf_op jit(solution)/shard_map/y_sweeps/pallas_call | solution.py:187
  12.0 1.4 %collective-permute-start.1 = (f32[200,128]{1,0:T(8,128)}, f32[200,128]{1,0:T(8,128)S(1)}, u32[]{:S(2)}, u32[]{:S(2)}) collective-permute-start(f32[200,128]{1,0:T(8,128)} %get-tuple-element.22.columns_ref), channel_id=1, source_target_pairs={{0,7},{1,0},{2,1},{3,2},{4,3},{5,4},{6,5},{7,6},{8,15},{9,8},{10,9... | collective-permute-start | bytes 307208 | tf_op jit(solution)/shard_map/ppermute | solution.py:696
  13.4 1.2 %collective-permute-start = (f32[200,128]{1,0:T(8,128)}, f32[200,128]{1,0:T(8,128)S(1)}, u32[]{:S(2)}, u32[]{:S(2)}) collective-permute-start(f32[200,128]{1,0:T(8,128)} %get-tuple-element.22.columns_ref), channel_id=1, source_target_pairs={{0,1},{1,2},{2,3},{3,4},{4,5},{5,6},{6,7},{7,0},{8,9},{9,10},{10,1... | collective-permute-start | bytes 307208 | tf_op jit(solution)/shard_map/ppermute | solution.py:696
  14.7 0.6 pad_add_fusion.rank_ref
  15.2 2.0 %collective-permute-done.1.high_ref = f32[200,128]{1,0:T(8,128)S(1)} collective-permute-done((f32[200,128]{1,0:T(8,128)}, f32[200,128]{1,0:T(8,128)S(1)}, u32[]{:S(2)}, u32[]{:S(2)}) %collective-permute-start.1) | collective-permute-done | bytes 102432 | tf_op jit(solution)/shard_map/ppermute | solution.py:696
  17.2 0.0 collective-permute-done.low_ref
  17.2 0.6 copy-done.2
  17.8 0.0 copy-done.3
  17.9 2.6 %repair.1 = (f32[2,192,128]{2,1,0:T(8,128)}, f32[192,128]{1,0:T(8,128)}, f32[8,128]{1,0:T(8,128)}) custom-call(s32[2]{0:T(128)} %pad_add_fusion.rank_ref, f32[2,192,128]{2,1,0:T(8,128)} %get-tuple-element.21.ends_ref, f32[200,128]{1,0:T(8,128)} %get-tuple-element.22.columns_ref, f32[200,128]{1,0:T(8,128)} %copy-done.3, f32[200,128]{1,0:T(8,128)} %copy-done.2), custom_call_target="tpu_custom_call" | custom-call | bytes 3000000 | tf_op jit(solution)/shard_map/repair/pallas_call | solution.py:282
  20.4 14.8 %all_to_all.26 = f32[16,24,128]{2,1,0:T(8,128)} all-to-all(f32[16,24,128]{2,1,0:T(8,128)} %bitcast.18), channel_id=1, replica_groups=mesh['gy'=16,'gz'=8] {'gy'}, dimensions={0} | all-to-all | bytes 393216 | tf_op jit(solution)/shard_map/all_to_all | solution.py:707
  35.2 1.7 %ring_scan.1 = f32[384,128]{1,0:T(8,128)} custom-call(s32[2]{0:T(128)} %pad_add_fusion.rank_ref, f32[384,128]{1,0:T(8,128)} %bitcast.17, f32[1,128]{1,0:T(1,128)} %bitcast.20), custom_call_target="tpu_custom_call" | custom-call | bytes 3000000 | tf_op jit(solution)/shard_map/ring_scan/pallas_call | solution.py:318
  36.9 3.5 %all-to-all-start.1 = ((f32[16,24,128]{2,1,0:T(8,128)}), f32[16,24,128]{2,1,0:T(8,128)S(1)}, u32[]{:S(2)}, u32[]{:S(2)}) async-start(f32[16,24,128]{2,1,0:T(8,128)} %bitcast.16), calls=%async_computation.1 | async-start | bytes 393216 | tf_op jit(solution)/shard_map/all_to_all | solution.py:711
  40.5 5.5 %collective-permute-start.3 = (f32[8,128]{1,0:T(8,128)}, f32[8,128]{1,0:T(8,128)S(1)}, u32[]{:S(2)}, u32[]{:S(2)}) collective-permute-start(f32[8,128]{1,0:T(8,128)} %get-tuple-element.24.near_ref), channel_id=1, source_target_pairs={{0,5},{1,6},{2,7},{3,0},{4,1},{5,2},{6,3},{7,4},{8,13},{9,14},{10,... | collective-permute-start | bytes 12296 | tf_op jit(solution)/shard_map/ppermute | solution.py:696
  46.0 1.0 %collective-permute-done.3.far_high_ref = f32[8,128]{1,0:T(8,128)S(1)} collective-permute-done((f32[8,128]{1,0:T(8,128)}, f32[8,128]{1,0:T(8,128)S(1)}, u32[]{:S(2)}, u32[]{:S(2)}) %collective-permute-start.3) | collective-permute-done | bytes 4128 | tf_op jit(solution)/shard_map/ppermute | solution.py:696
  47.0 3.8 %collective-permute-done.2.far_low_ref = f32[8,128]{1,0:T(8,128)S(1)} collective-permute-done((f32[8,128]{1,0:T(8,128)}, f32[8,128]{1,0:T(8,128)S(1)}, u32[]{:S(2)}, u32[]{:S(2)}) %collective-permute-start.2) | collective-permute-done | bytes 4128 | tf_op jit(solution)/shard_map/ppermute | solution.py:696
  50.8 0.6 copy-done.5
  51.3 3.2 %z_coefficients.1 = (f32[2,64,128]{2,1,0:T(8,128)}, bf16[256,256]{1,0:T(8,128)(2,1)}, bf16[256,256]{1,0:T(8,128)(2,1)}, bf16[256,256]{1,0:T(8,128)(2,1)}, f32[2,...) custom-call(s32[2]{0:T(128)} %pad_add_fusion.rank_ref, f32[8,128]{1,0:T(8,128)} %get-tuple-element.24.near_ref, ...), custom_call_target="tpu_custom_call" | custom-call | bytes 9000000 | tf_op jit(solution)/shard_map/z_coefficients/pallas_call | solution.py:484
  54.6 7.1 %z_local_sums.1.sums_ref = f32[192,128]{1,0:T(8,128)} custom-call(f32[12480,128]{1,0:T(8,128)} %get-tuple-element.20.m_hbm, f32[192,64,128]{2,1,0:T(8,128)} %bitcast.11, bf16[256,256]{1,0:T(8,128)(2,1)} %get-tuple-element.29.ends_ref), custom_call_target="tpu_custom_call" | custom-call | bytes 24000000 | tf_op jit(solution)/shard_map/z_local_sums/pallas_call | solution.py:543
  61.7 0.7 copy-done
  62.4 2.5 %z_messages.1 = (f32[8,96,128]{2,1,0:T(8,128)}, f32[192,128]{1,0:T(8,128)}) custom-call(s32[2]{0:T(128)} %pad_add_fusion.rank_ref, f32[192,128]{1,0:T(8,128)} %z_local_sums.1.sums_ref, f32[2,192,128]{2,1,0:T(8,128)} %bitcast.14, f32[2,128,128]{2,1,0:T(8,128)} %get-tuple-element.30.reach_ref, f32[192,128]{1,0:T(8,128)} %get-tuple-element.31.flux_ref, ...), custom_call_target="tpu_custom_call" | custom-call | bytes 3000000 | tf_op jit(solution)/shard_map/z_messages/pallas_call | solution.py:579
  64.8 3.6 %all-to-all-start.2 = ((f32[8,96,128]{2,1,0:T(8,128)}), f32[8,96,128]{2,1,0:T(8,128)S(1)}, u32[]{:S(2)}, u32[]{:S(2)}) async-start(f32[8,96,128]{2,1,0:T(8,128)} %get-tuple-element.34), calls=%async_computation.2 | async-start | bytes 786432 | tf_op jit(solution)/shard_map/all_to_all | solution.py:714
  68.4 9.2 %z_local_solve.1.y_hbm = f32[192,64,128]{2,1,0:T(8,128)} custom-call(f32[12480,128]{1,0:T(8,128)} %get-tuple-element.20.m_hbm, f32[192,64,128]{2,1,0:T(8,128)} %bitcast.12, f32[2,192,128]{2,1,0:T(8,128)} %bitcast.15, f32[2,64,128]{2,1,0:T(8,128)} %get-tuple-element.25.table_ref, bf16[256,256]{1,0:T(8,128)(2,1)} %get-tuple-element.26.green_ref), custom_call_target="tpu_custom_call" | custom-call | bytes 24000000 | tf_op jit(solution)/shard_map/z_local_solve/pallas_call | solution.py:609
  77.6 0.7 copy-done.1
  78.4 7.5 %z_carries.1 = f32[192,64,128]{2,1,0:T(8,128)} custom-call(f32[192,64,128]{2,1,0:T(8,128)} %z_local_solve.1.y_hbm, bf16[256,256]{1,0:T(8,128)(2,1)} %get-tuple-element.27.matrix_ref, f32[2,8,128]{2,1,0:T(8,128)} %get-tuple-element.28.share_ref, f32[192,128]{1,0:T(8,128)} %get-tuple-element.33.layer_ref, f32[8,96,128]{2,1,0:T(8,128)} %copy-done.1), custom_call_target="tpu_custom_call" | custom-call | bytes 24000000 | tf_op jit(solution)/shard_map/z_carries/pallas_call | solution.py:676
  (10 shorter events, 0.0 us)
Async XLA Ops:
  12.0 5.2 %collective-permute-start.1 = (f32[200,128]{1,0:T(8,128)}, f32[200,128]{1,0:T(8,128)S(1)}, u32[]{:S(2)}, u32[]{:S(2)}) collective-permute-start(f32[200,128]{1,0:T(8,128)} %get-tuple-element.22.columns_ref), channel_id=1, source_target_pairs={{0,7},{1,0},{2,1},{3,2},{4,3},{5,4},{6,5},{7,6},{8,15},{9,8},{10,9... | collective-permute-start | bytes 307208 | tf_op jit(solution)/shard_map/ppermute | solution.py:696
  13.4 3.7 %collective-permute-start = (f32[200,128]{1,0:T(8,128)}, f32[200,128]{1,0:T(8,128)S(1)}, u32[]{:S(2)}, u32[]{:S(2)}) collective-permute-start(f32[200,128]{1,0:T(8,128)} %get-tuple-element.22.columns_ref), channel_id=1, source_target_pairs={{0,1},{1,2},{2,3},{3,4},{4,5},{5,6},{6,7},{7,0},{8,9},{9,10},{10,1... | collective-permute-start | bytes 307208 | tf_op jit(solution)/shard_map/ppermute | solution.py:696
  17.2 0.6 copy-start.2
  17.2 0.7 copy-start.3
  36.9 24.7 %all-to-all-start.1 = ((f32[16,24,128]{2,1,0:T(8,128)}), f32[16,24,128]{2,1,0:T(8,128)S(1)}, u32[]{:S(2)}, u32[]{:S(2)}) async-start(f32[16,24,128]{2,1,0:T(8,128)} %bitcast.16), calls=%async_computation.1 | async-start | bytes 393216 | tf_op jit(solution)/shard_map/all_to_all | solution.py:711
  40.5 6.5 %collective-permute-start.3 = (f32[8,128]{1,0:T(8,128)}, f32[8,128]{1,0:T(8,128)S(1)}, u32[]{:S(2)}, u32[]{:S(2)}) collective-permute-start(f32[8,128]{1,0:T(8,128)} %get-tuple-element.24.near_ref), channel_id=1, source_target_pairs={{0,5},{1,6},{2,7},{3,0},{4,1},{5,2},{6,3},{7,4},{8,13},{9,14},{10,... | collective-permute-start | bytes 12296 | tf_op jit(solution)/shard_map/ppermute | solution.py:696
  46.0 4.7 %collective-permute-start.2 = (f32[8,128]{1,0:T(8,128)}, f32[8,128]{1,0:T(8,128)S(1)}, u32[]{:S(2)}, u32[]{:S(2)}) collective-permute-start(f32[8,128]{1,0:T(8,128)} %get-tuple-element.24.near_ref), channel_id=1, source_target_pairs={{0,3},{1,4},{2,5},{3,6},{4,7},{5,0},{6,1},{7,2},{8,11},{9,12},{10,... | collective-permute-start | bytes 12296 | tf_op jit(solution)/shard_map/ppermute | solution.py:696
  47.0 3.8 %copy-start.4 = (f32[8,128]{1,0:T(8,128)}, f32[8,128]{1,0:T(8,128)S(1)}, u32[]{:S(2)}) copy-start(f32[8,128]{1,0:T(8,128)S(1)} %collective-permute-done.3.far_high_ref) | copy-start | bytes 12292
  50.8 0.6 copy-start.5
  61.7 0.7 copy-start
  64.8 12.8 %all-to-all-start.2 = ((f32[8,96,128]{2,1,0:T(8,128)}), f32[8,96,128]{2,1,0:T(8,128)S(1)}, u32[]{:S(2)}, u32[]{:S(2)}) async-start(f32[8,96,128]{2,1,0:T(8,128)} %get-tuple-element.34), calls=%async_computation.2 | async-start | bytes 786432 | tf_op jit(solution)/shard_map/all_to_all | solution.py:714
  77.6 0.8 copy-start.1

commit v2 on v1

--- a/solution.py
+++ b/solution.py
@@ -48,18 +48,33 @@
     return high, (x - high.astype(f32)).astype(bf16)
 
 
+def paired(x):
+    high, mid = split(x)
+    row = jnp.concatenate([high, mid], axis=1)
+    return jnp.concatenate([row, row], axis=0)
+
+
+def pair_dot(x, matrix):
+    high, mid = split(x)
+    result = jnp.dot(
+        jnp.concatenate([high, mid], axis=1), matrix, preferred_element_type=f32
+    )
+    half = result.shape[1] // 2
+    return result[:, :half] + result[:, half:]
+
+
 def chunk(ref, step):
     return ref.at[pl.ds(step * PER, PER)]
 
 
-def kernel_call(kernel, out_shape, out_specs, in_specs, scratch=(), name=None, us=1):
+def kernel_call(kernel, out_shape, out_specs, in_specs, scratch=(), name=None, us=1, mib=8):
     return pl.pallas_call(
         kernel,
         in_specs=in_specs,
         out_specs=out_specs,
         out_shape=out_shape,
         scratch_shapes=list(scratch),
-        compiler_params=pltpu.CompilerParams(vmem_limit_bytes=60 * 1024 * 1024),
+        compiler_params=pltpu.CompilerParams(vmem_limit_bytes=mib * 1024 * 1024),
         cost_estimate=pl.CostEstimate(flops=0, bytes_accessed=us * 3_000_000, transcendentals=0),
         name=name,
     )
@@ -114,10 +129,12 @@
 FLAT = jax.ShapeDtypeStruct((LINES, CZ), f32)
 PITCHED = (LINES * PITCH, CZ)
 ROWS = LINES // 2
+HALO = jax.ShapeDtypeStruct((ROWS, CZ), f32)
 
 
 def sweep_kernel(
-    u_hbm, q_hbm, eta_ref, m_hbm, ends_ref, columns_ref, u_ref, q_ref, m_ref, x_buf, f_buf, sems
+    u_hbm, q_hbm, eta_ref, m_hbm, ends_ref, columns_ref, up_ref, down_ref,
+    u_ref, q_ref, m_ref, x_buf, f_buf, sems,
 ):
     lane = lanes()
     place = ((lane + 1) >> 1) & 63
@@ -132,55 +149,95 @@
         return (pltpu.make_async_copy(pitched(m_ref, i), pitched(m_hbm, i), sems.at[2, i]),)
 
     eta = jnp.broadcast_to(eta_ref[...], (8, CZ))
-    columns_ref[pl.ds(LINES, 8), :] = eta
     face_low = jnp.where(lane == 0, 0.0, z_rate * 0.5 * (pltpu.roll(eta, 1, 1) + eta))
     face_high = jnp.where(lane == CZ - 1, 0.0, z_rate * 0.5 * (eta + pltpu.roll(eta, CZ - 1, 1)))
     decay, peak = root_of(eta)
     groups = PER // GROUP
 
-    def work(i):
-        def rows(g):
-            return pl.ds(pl.multiple_of(i * PER + g * GROUP, 8), GROUP)
-
-        def right_side(g, _):
-            acc = jnp.zeros((8, CZ), f32)
-            for k in range(8 * GROUP):
-                c, at = g * GROUP + k // 8, pl.ds((k % 8) * 8, 8)
-                here = u_ref[i * PER + c, at, :]
-                under = pltpu.roll(here, 1, 1)
-                over = pltpu.roll(here, CZ - 1, 1)
-                acc = jnp.where(place == k, pltpu.roll(here, 2 * k, 1) if k else here, acc)
-                q = q_ref[i * PER + c, at, :].astype(f32)
-                explicit = face_high * (over - here) - face_low * (here - under)
-                x_buf[pl.ds(c * PITCH + (k % 8) * 8, 8), :] = here + explicit + q
-            columns_ref[rows(g), :] = acc
-            return 0
-
-        lax.fori_loop(0, groups, right_side, 0)
+    size = PER * PITCH
+    half = CY // 2
+
+    def rows(i, g):
+        return pl.ds(pl.multiple_of(i * PER + g * GROUP, 8), GROUP)
+
+    def right_side(i, tiles, acc):
+        for tile in tiles:
+            g, k = tile // 64, tile % 64
+            c, at = tile // 8, pl.ds((tile % 8) * 8, 8)
+            here = u_ref[i * PER + c, at, :]
+            under = pltpu.roll(here, 1, 1)
+            over = pltpu.roll(here, CZ - 1, 1)
+            acc = jnp.where(place == k, pltpu.roll(here, 2 * k, 1) if k else here, acc)
+            q = q_ref[i * PER + c, at, :].astype(f32)
+            explicit = face_high * (over - here) - face_low * (here - under)
+            x_buf[pl.ds((i % 2) * size + c * PITCH + (tile % 8) * 8, 8), :] = here + explicit + q
+            if k == 63:
+                columns_ref[rows(i, g), :] = acc
+        return acc
+
+    def sweep(i, ahead):
+        def x_at(g, y):
+            return x_buf[pl.ds((i % 2) * size + g * GROUP * PITCH + y, GROUP, stride=PITCH), :]
 
         def at(g, y):
             return pl.ds(g * GROUP * PITCH + y, GROUP, stride=PITCH)
 
         def out(g, y):
-            return pl.ds((i * PER + g * GROUP) * PITCH + y, GROUP, stride=PITCH)
-
-        total = [jnp.zeros((8, CZ), f32) for _ in range(groups)]
-        for y in range(CY):
+            return pl.ds(i * size + g * GROUP * PITCH + y, GROUP, stride=PITCH)
+
+        acc = jnp.zeros((8, CZ), f32)
+        forth = [acc] * groups
+        back = [acc] * groups
+        for s in range(CY):
+            low, high = s, CY - 1 - s
             for g in range(groups):
-                total[g] = total[g] * decay + x_buf[at(g, y), :]
-                f_buf[at(g, y), :] = total[g]
+                forth[g] = forth[g] * decay + x_at(g, low)
+                kept = back[g] * decay
+                back[g] = kept + x_at(g, high)
+                if s < half:
+                    f_buf[at(g, low), :] = forth[g]
+                    f_buf[at(g, high), :] = kept
+                else:
+                    m_ref[out(g, low), :] = peak * (forth[g] + f_buf[at(g, low), :])
+                    m_ref[out(g, high), :] = peak * (f_buf[at(g, high), :] + kept)
+            if ahead:
+                each = PER * CY // 8 // CY
+                acc = right_side(i + 1, range(s * each, (s + 1) * each), acc)
         for g in range(groups):
-            ends_ref[0, rows(g), :] = total[g]
-        total = [jnp.zeros((8, CZ), f32) for _ in range(groups)]
-        for y in reversed(range(CY)):
-            for g in range(groups):
-                kept = total[g] * decay
-                total[g] = kept + x_buf[at(g, y), :]
-                m_ref[out(g, y), :] = peak * (f_buf[at(g, y), :] + kept)
-        for g in range(groups):
-            ends_ref[1, rows(g), :] = total[g]
-
-    pipeline(fetches, stores, work)
+            ends_ref[0, rows(i, g), :] = forth[g]
+            ends_ref[1, rows(i, g), :] = back[g]
+
+    for i in range(AHEAD):
+        for copy in fetches(i):
+            copy.start()
+    for copy in fetches(0):
+        copy.wait()
+    right_side(0, range(PER * CY // 8), jnp.zeros((8, CZ), f32))
+
+    def step(i, _):
+        @pl.when(i + AHEAD < STEPS)
+        def _():
+            for copy in fetches(i + AHEAD):
+                copy.start()
+
+        for copy in fetches(i + 1):
+            copy.wait()
+        sweep(i, True)
+        for copy in stores(i):
+            copy.start()
+        return 0
+
+    lax.fori_loop(0, STEPS - 1, step, 0)
+    sweep(STEPS - 1, False)
+    for copy in stores(STEPS - 1):
+        copy.start()
+    for i in range(STEPS):
+        for copy in stores(i):
+            copy.wait()
+    first, second = columns_ref[:ROWS], columns_ref[ROWS:]
+    odd = lanes((ROWS, CZ)) & 1 == 1
+    up_ref[...] = jnp.where(odd, first, pltpu.roll(second, 1, 1))
+    down_ref[...] = jnp.where(odd, pltpu.roll(second, CZ - 1, 1), first)
 
 
 def sweeps(u, q, own):
@@ -189,19 +246,22 @@
         [
             jax.ShapeDtypeStruct(PITCHED, f32),
             jax.ShapeDtypeStruct((2, LINES, CZ), f32),
-            jax.ShapeDtypeStruct((LINES + 8, CZ), f32),
+            FLAT,
+            HALO,
+            HALO,
         ],
-        [HBM, VMEM, VMEM],
+        [HBM] + [VMEM] * 4,
         [HBM, HBM, VMEM],
         [
             pltpu.VMEM((LINES, CY, CZ), f32),
             pltpu.VMEM((LINES, CY, CZ), bf16),
             pltpu.VMEM(PITCHED, f32),
-            pltpu.VMEM((PER * PITCH, CZ), f32),
+            pltpu.VMEM((2 * PER * PITCH, CZ), f32),
             pltpu.VMEM((PER * PITCH, CZ), f32),
             pltpu.SemaphoreType.DMA((3, STEPS)),
         ],
         name="y_sweeps",
+        mib=51,
         us=12,
     )(u, q, own)
 
@@ -212,10 +272,6 @@
         out = jnp.where((exponent >> bit) & 1 == 1, out * base, out)
         base = base * base
     return out
-
-
-def exact_dot(a, b):
-    return jnp.dot(a, b, preferred_element_type=f32, precision=lax.Precision.HIGHEST)
 
 
 def flux_place(l):
@@ -234,63 +290,39 @@
     return x
 
 
-def repair_kernel(rank_ref, ends_ref, columns_ref, low_ref, high_ref, out_ref, flux_ref, near_ref):
+def repair_kernel(
+    rank_ref, ends_ref, columns_ref, low_ref, high_ref, face_ref, repair_ref, out_ref, flux_ref
+):
     rank = rank_ref[0]
-    square = (CZ, CZ)
-    lane = lanes(square)
-    inner_low, inner_high = rank > 0, rank < NGZ - 1
-    own_eta, low_eta, high_eta = (
-        ref[pl.ds(LINES, 8), :] for ref in (columns_ref, low_ref, high_ref)
-    )
-    row = rows_of()
-    near_ref[...] = jnp.where(row == 0, low_eta, jnp.where(row == 1, own_eta, high_eta))
-    own = own_eta[:1]
-    low_eta = jnp.where(inner_low, low_eta[:1], 0.0)[:, CZ - 1 :]
-    high_eta = jnp.where(inner_high, high_eta[:1], 0.0)[:, :1]
-    face_low = jnp.broadcast_to(z_rate * 0.5 * (low_eta + own[:, :1]), (1, CZ))
-    face_high = jnp.broadcast_to(z_rate * 0.5 * (own[:, CZ - 1 :] + high_eta), (1, CZ))
-    even = lanes((LINES, CZ)) & 1 == 0
-    low, high, columns = (ref[pl.ds(0, LINES), :] for ref in (low_ref, high_ref, columns_ref))
-    outer = jnp.where(
-        even,
-        jnp.where(inner_low, pltpu.roll(low, 1, 1), 0.0),
-        jnp.where(inner_high, pltpu.roll(high, 1, 1), 0.0),
-    )
-    inner = jnp.where(even, columns, pltpu.roll(columns, 2, 1))
-    face = jnp.where(lanes((1, CZ)) & 1 == 0, face_low, face_high)
-    flux = turned(jnp.broadcast_to(face, (LINES, CZ)) * (outer - inner))
-    flux_ref[...] = flux
-    decay, _ = root_of(own)
-    y, side = flux_place(rows_of(square))
-    base = jnp.where(
-        side == 0,
-        jnp.broadcast_to(decay[:, :1], square),
-        jnp.broadcast_to(decay[:, CZ - 1 :], square),
-    )
-    place = lane == jnp.where(side == 0, 0, CZ - 1)
-    out_ref[0] = ends_ref[0] + exact_dot(flux, jnp.where(place, raised(base, 63 - y), 0.0))
-    out_ref[1] = ends_ref[1] + exact_dot(flux, jnp.where(place, raised(base, y), 0.0))
-
-
-def repair(ranks, ends, columns, low, high):
-    shapes = [
-        jax.ShapeDtypeStruct((2, LINES, CZ), f32),
-        FLAT,
-        jax.ShapeDtypeStruct((NGZ, CZ), f32),
-    ]
-    call = kernel_call(repair_kernel, shapes, [VMEM] * 3, [SMEM] + [VMEM] * 4, name="repair")
-    return call(ranks, ends, columns, low, high)
-
-
-def ring_kernel(rank_ref, ends_ref, eta_ref, out_ref):
+    even = lanes((ROWS, CZ)) & 1 == 0
+    face = jnp.broadcast_to(face_ref[:1], (ROWS, CZ))
+    low = jnp.where(rank > 0, low_ref[...], 0.0)
+    high = jnp.where(rank < NGZ - 1, high_ref[...], 0.0)
+    outer = (
+        jnp.where(even, pltpu.roll(low, 1, 1), pltpu.roll(high, 1, 1)),
+        jnp.where(even, low, pltpu.roll(high, 2, 1)),
+    )
+    for half in range(2):
+        at = pl.ds(half * ROWS, ROWS)
+        columns = columns_ref[at, :]
+        inner = jnp.where(even, columns, pltpu.roll(columns, 2, 1))
+        flux = turned(face * (outer[half] - inner))
+        flux_ref[at, :] = flux
+        added = pair_dot(flux, repair_ref[...])
+        out_ref[0, at, :] = ends_ref[0, at, :] + added[:, :CZ]
+        out_ref[1, at, :] = ends_ref[1, at, :] + added[:, CZ:]
+
+
+def repair(ranks, ends, columns, low, high, face, matrix):
+    shapes = [jax.ShapeDtypeStruct((2, LINES, CZ), f32), FLAT]
+    call = kernel_call(repair_kernel, shapes, [VMEM] * 2, [SMEM] + [VMEM] * 6, name="repair")
+    return call(ranks, ends, columns, low, high, face, matrix)
+
+
+def ring_kernel(rank_ref, ends_ref, turn_ref, out_ref):
     rows = 2 * LINES // NGY
     upward = rank_ref[1] < NGY // 2
-    decay, _ = root_of(jnp.broadcast_to(eta_ref[...], (8, CZ)))
-    whole = power_64(decay)
-    turn = whole
-    for _ in range(4):
-        turn = turn * turn
-    closing = 1.0 / (1.0 - turn)
+    whole, closing = turn_ref[0], turn_ref[1]
     for part in range(rows // 8):
 
         def at(node):
@@ -313,23 +345,20 @@
             out_ref[at(node), :] = jnp.where(upward, ups[node], downs[node])
 
 
-def ring_scan(ranks, ends, own):
+def ring_scan(ranks, ends, turn):
     shape = jax.ShapeDtypeStruct(ends.shape, f32)
     return kernel_call(ring_kernel, shape, VMEM, [SMEM, VMEM, VMEM], name="ring_scan")(
-        ranks, ends, own
+        ranks, ends, turn
     )
 
 
 def coefficient_kernel(
-    rank_ref, near_ref, far_low_ref, far_high_ref,
-    table_ref, green_ref, ends_ref, carry_ref, share_ref, spread_ref, reach_ref, eta_ref,
+    rank_ref, eta_ref, face_ref, repair_ref, table_ref,
+    turn_ref, green_ref, ends_ref, carry_ref, share_ref, layer_ref, reach_ref,
 ):
     rank = rank_ref[0]
     lane, row = lanes(), rows_of()
-    eta_ref[0:2, :] = far_low_ref[1:3, :]
-    eta_ref[2:5, :] = near_ref[0:3, :]
-    eta_ref[5:8, :] = far_high_ref[0:3, :]
-    eta = pltpu.roll(eta_ref[...], lax.rem(rank + 5, 8), 0)
+    eta = eta_ref[...]
 
     def before(x, fill):
         y = pltpu.roll(x, 1, 1)
@@ -441,63 +470,76 @@
         jnp.broadcast_to(upper[:, 0:1], square),
     )
     for matrix, ref in ((green, green_ref), (ends, ends_ref), (carry, carry_ref)):
-        for half, part in enumerate(split(matrix)):
-            for rows in range(2):
-                ref[pl.ds(rows * CZ, CZ), pl.ds(half * CZ, CZ)] = part
+        ref[...] = paired(matrix)
 
     decay, peak = root_of(own(eta))
+    whole = power_64(jnp.broadcast_to(decay, (8, CZ)))
+    around = whole
+    for _ in range(4):
+        around = around * around
+    turn_ref[0] = whole
+    turn_ref[1] = 1.0 / (1.0 - around)
     y = row_sq & 63
     wide = jnp.broadcast_to(decay, square)
     start = jnp.broadcast_to(peak * decay, square)
-    response_up = start * raised(wide, y)
-    response_down = start * raised(wide, 63 - y)
-    table_ref[0] = response_up[:CY]
-    table_ref[1] = response_down[:CY]
     seen = jnp.transpose(ends)
-    reach_ref[0] = jnp.transpose(response_up * seen)
-    reach_ref[1] = jnp.transpose(response_down * seen)
-    y_in, side = flux_place(row_sq)
-    low_side = side == 0
-    base = jnp.where(
-        low_side,
-        jnp.broadcast_to(decay[:, :1], square),
-        jnp.broadcast_to(decay[:, CZ - 1 :], square),
-    )
-    top = jnp.where(
-        low_side,
-        jnp.broadcast_to(peak[:, :1], square),
-        jnp.broadcast_to(peak[:, CZ - 1 :], square),
-    )
-    apart = jnp.abs(y_in - (lane_sq & 63))
-    spread = jnp.where(low_side == (lane_sq < CZ // 2), top * raised(base, apart), 0.0)
-    spread_ref[0] = 2.0 * spread
-    half = row_sq < CZ // 2
-    same_y = (lane_sq & 63) == y
+    reach = []
+    for way in range(2):
+        response = start * raised(wide, (y, CY - 1 - y)[way])
+        table_ref[way] = response[:CY]
+        reach.append(jnp.transpose(response * seen))
+    reach_ref[...] = paired(jnp.concatenate(reach, axis=0))
+    y, side = flux_place(row_sq)
+    low = side == 0
+
+    def sided(x):
+        return jnp.where(
+            low, jnp.broadcast_to(x[:, :1], square), jnp.broadcast_to(x[:, CZ - 1 :], square)
+        )
+
+    face = jnp.where(
+        lane_1 & 1 == 0,
+        jnp.broadcast_to(own(face_low)[:, :1], (1, CZ)),
+        jnp.broadcast_to(own(face_high)[:, CZ - 1 :], (1, CZ)),
+    )
+    face_ref[...] = jnp.broadcast_to(face, (8, CZ))
+    base = sided(decay)
+    place = lane_sq == jnp.where(low, 0, CZ - 1)
+    forth = jnp.where(place, raised(base, CY - 1 - y), 0.0)
+    back = jnp.where(place, raised(base, y), 0.0)
+    repair_ref[...] = paired(jnp.concatenate([forth, back], axis=1))
+    apart = jnp.abs(y - (lane_sq & 63))
+    spread = jnp.where(low == (lane_sq < 64), sided(peak) * raised(base, apart), 0.0)
+    same_y = (lane_sq & 63) == (row_sq & 63)
     first = jnp.broadcast_to(ends[0:1, :], square)
     final = jnp.broadcast_to(ends[CZ - 1 :, :], square)
-    spread_ref[1] = exact_dot(spread, jnp.where(same_y, jnp.where(half, first, final), 0.0))
-
-
-def coefficients(ranks, near, far_low, far_high):
-    matrix = jax.ShapeDtypeStruct((2 * CZ, 2 * CZ), bf16)
-    square = jax.ShapeDtypeStruct((2, CZ, CZ), f32)
+    layer = jnp.where(same_y, jnp.where(row_sq < 64, first, final), 0.0)
+    layer_ref[...] = paired(jnp.concatenate([2.0 * spread, pair_dot(spread, paired(layer))], axis=1))
+
+
+def coefficients(ranks, etas):
+    def matrix(rows, columns):
+        return jax.ShapeDtypeStruct((2 * rows * CZ, 2 * columns * CZ), bf16)
+
     return kernel_call(
         coefficient_kernel,
         [
+            jax.ShapeDtypeStruct((8, CZ), f32),
+            matrix(1, 2),
             jax.ShapeDtypeStruct((2, CY, CZ), f32),
-            matrix,
-            matrix,
-            matrix,
+            jax.ShapeDtypeStruct((2, 8, CZ), f32),
+            matrix(1, 1),
+            matrix(1, 1),
+            matrix(1, 1),
             jax.ShapeDtypeStruct((2, NGZ, CZ), f32),
-            square,
-            square,
+            matrix(1, 2),
+            matrix(2, 1),
         ],
-        [VMEM] * 7,
-        [SMEM] + [VMEM] * 3,
-        [pltpu.VMEM((NGZ, CZ), f32)],
+        [VMEM] * 10,
+        [SMEM, VMEM],
         name="z_coefficients",
-        us=3,
-    )(ranks, near, far_low, far_high)
+        us=4,
+    )(ranks, etas)
 
 
 def split_rows(left_ref, rows, x):
@@ -520,8 +562,15 @@
     return fetches
 
 
-def sums_kernel(m_hbm, u_hbm, ends_ref, sums_ref, m_ref, u_ref, left_ref, sems):
+def sums_kernel(
+    m_hbm, u_hbm, ends_ref, flux_ref, spread_ref, sums_ref, layer_ref, m_ref, u_ref, left_ref, seen_ref, sems
+):
     mask = unit_mask((CY, CZ))
+
+    def prepare():
+        both = pair_dot(flux_ref[...], spread_ref[...])
+        layer_ref[...] = both[:, :CZ]
+        seen_ref[...] = both[:, CZ:]
 
     def work(i):
         for g in range(PER // GROUP):
@@ -536,35 +585,33 @@
                 part = jnp.where(mask, result[c * CY : (c + 1) * CY], 0.0)
                 sums_ref[pl.ds(first + c, 1), :] = jnp.sum(part, axis=0, keepdims=True)
 
-    pipeline(fetches_of(u_hbm, m_hbm, u_ref, m_ref, sems), no_copies, work)
-
-
-def local_sums(m, u, ends):
+    pipeline(fetches_of(u_hbm, m_hbm, u_ref, m_ref, sems), no_copies, work, prepare)
+    sums_ref[...] += seen_ref[...]
+
+
+def local_sums(m, u, ends, flux, spread):
     return kernel_call(
         sums_kernel,
-        FLAT,
-        VMEM,
-        [HBM, HBM, VMEM],
+        [FLAT, FLAT],
+        [VMEM] * 2,
+        [HBM, HBM] + [VMEM] * 3,
         [
             pltpu.VMEM(PITCHED, f32),
             pltpu.VMEM((LINES, CY, CZ), f32),
             pltpu.VMEM((SLOTS, GROUP * CY, 2 * CZ), bf16),
+            pltpu.VMEM((LINES, CZ), f32),
             pltpu.SemaphoreType.DMA((2, STEPS)),
         ],
         name="z_local_sums",
+        mib=48,
         us=8,
-    )(m, u, ends)
-
-
-def messages_kernel(
-    rank_ref, sums_ref, carry_ref, reach_ref, flux_ref, spread_ref, out_ref, layer_ref
-):
+    )(m, u, ends, flux, spread)
+
+
+def messages_kernel(rank_ref, sums_ref, carry_ref, reach_ref, out_ref):
     rank = rank_ref[0]
-    flux = flux_ref[...]
-    layer_ref[...] = exact_dot(flux, spread_ref[0])
-    sums = sums_ref[...] + exact_dot(flux, spread_ref[1])
-    sums = sums + exact_dot(carry_ref[0], reach_ref[0])
-    sums = sums + exact_dot(carry_ref[1], reach_ref[1])
+    carries = jnp.concatenate([carry_ref[0], carry_ref[1]], axis=1)
+    sums = sums_ref[...] + pair_dot(carries, reach_ref[...])
     first, second = sums[:ROWS], sums[ROWS:]
     lower = lanes((ROWS, CZ)) < 64
     up = jnp.where(lower, first, pltpu.roll(second, 64, 1))
@@ -573,10 +620,10 @@
         out_ref[k] = jnp.where(rank > k, down, up)
 
 
-def messages_of(ranks, sums, carries, reach, flux, spread):
-    shapes = [jax.ShapeDtypeStruct((NGZ, ROWS, CZ), f32), FLAT]
-    call = kernel_call(messages_kernel, shapes, [VMEM] * 2, [SMEM] + [VMEM] * 5, name="z_messages")
-    return call(ranks, sums, carries, reach, flux, spread)
+def messages_of(ranks, sums, carries, reach):
+    shape = jax.ShapeDtypeStruct((NGZ, ROWS, CZ), f32)
+    call = kernel_call(messages_kernel, shape, VMEM, [SMEM] + [VMEM] * 3, name="z_messages")
+    return call(ranks, sums, carries, reach)
 
 
 def solve_kernel(
@@ -619,6 +666,7 @@
             pltpu.SemaphoreType.DMA((3, STEPS)),
         ],
         name="z_local_solve",
+        mib=48,
         us=8,
     )(m, u, carries, table, green)
 
@@ -687,6 +735,7 @@
             pltpu.SemaphoreType.DMA((2, STEPS)),
         ],
         name="z_carries",
+        mib=48,
         us=8,
     )(y, matrix, share, layer, got)
 
@@ -701,16 +750,16 @@
     q = source_term.reshape(LINES, CY, CZ)
     ranks = jnp.stack([lax.axis_index("gz"), lax.axis_index("gy")]).astype(jnp.int32)
     own = resistivity.reshape(1, CZ)
-    m, ends, columns = sweeps(u, q, own)
-    low, high = shifted(columns, "gz", 1), shifted(columns, "gz", -1)
-    ends, flux, near = repair(ranks, ends, columns, low, high)
+    etas = lax.all_to_all(jnp.broadcast_to(own, (NGZ, CZ)), "gz", 0, 0, tiled=True)
+    m, ends, columns, up, down = sweeps(u, q, own)
+    low, high = shifted(up, "gz", 1), shifted(down, "gz", -1)
+    face, matrix, table, turn, green, last, vector, share, layers, reach = coefficients(ranks, etas)
+    ends, flux = repair(ranks, ends, columns, low, high, face, matrix)
     nodes = lax.all_to_all(ends.reshape(2 * LINES, CZ), "gy", 0, 0, tiled=True)
-    far_low, far_high = shifted(near, "gz", 3), shifted(near, "gz", -3)
-    table, green, last, vector, share, spread, reach = coefficients(ranks, near, far_low, far_high)
-    nodes = ring_scan(ranks, nodes, own)
+    nodes = ring_scan(ranks, nodes, turn)
     carries = lax.all_to_all(nodes, "gy", 0, 0, tiled=True).reshape(2, LINES, CZ)
-    sums = local_sums(m, u, last)
-    messages, layer = messages_of(ranks, sums, carries, reach, flux, spread)
+    sums, layer = local_sums(m, u, last, flux, layers)
+    messages = messages_of(ranks, sums, carries, reach)
     got = lax.all_to_all(messages.reshape(NGZ * ROWS, CZ), "gz", 0, 0, tiled=True)
     y = local_solve(m, u, carries, table, green)
     got = got.reshape(NGZ, ROWS, CZ)

time: 86.5 us -> 73.3 us (0.85)
  Pallas kernels: 45.8 us -> 35.9 us
  waiting for transfers between devices: 6.73 us -> 2.44 us
  starting transfers between devices: 15.3 us -> 17.8 us
    ppermute x4 -> x2, starting transfers between devices: 8.18 us -> 1.64 us  [shifted(): return lax.ppermute(x, axis, [(i, (i + by) % n) for i in range(n)])]
    all_to_all x0 -> x1, starting transfers between devices: none -> 5.8 us  [body(): lax.all_to_all(jnp.broadcast_to(own, (NGZ, CZ)), 'gz', 0, 0, tiled=True)]
    ppermute x4 -> x2, waiting for transfers between devices: 6.72 us -> 1 us  [shifted(): return lax.ppermute(x, axis, [(i, (i + by) % n) for i in range(n)])]
    pallas_call x4, Pallas kernels: 15.3 us -> 10.6 us  [the longest x1 5.58 us: local_sums(): kernel_call(sums_kernel, [FLAT, FLAT], [VMEM] * 2, [HBM, HBM] + [VMEM] *...]
    all_to_all x1, starting transfers between devices: 3.58 us -> 6.82 us  [body(): lax.all_to_all(messages.reshape(NGZ * ROWS, CZ), 'gz', 0, 0, tiled=True)]
    pallas_call x1, Pallas kernels: 12 us -> 9.38 us  [sweeps(): kernel_call(sweep_kernel, [jax.ShapeDtypeStruct(PITCHED, f32), jax.ShapeD...]
    unnamed x12 -> x2, local copies, waits for them, and re-layouts: 2.69 us -> 0.65 us
    all_to_all x1, waiting for transfers between devices: 0.01 us -> 1.43 us  [body(): lax.all_to_all(nodes, 'gy', 0, 0, tiled=True).reshape(2, LINES, CZ)]
  transfers between devices with their start and end apart: 6 -> 5, of which waited for: 3 -> 2; matrix products, arithmetic and copies ran while one was open for 1% -> 0% of each run, Pallas kernels for 23% -> 35%
where the time goes in v2:
time: 73.3 us; the launch traced here: 72.9 us
  Pallas kernels  35.9 us (49%)
  starting transfers between devices  17.8 us (24%)
  blocking collectives  14.7 us (20%)
  waiting for transfers between devices  2.44 us (3%)
  local copies, waits for them, and re-layouts  1.9 us (3%)
    all_to_all x1, blocking collectives, body(): nodes = lax.all_to_all(ends.reshape(2 * LINES, CZ), 'gy', 0, 0, tiled=True)  14.7 us
    pallas_call x1, Pallas kernels, sweeps(): kernel_call(sweep_kernel, [jax.ShapeDtypeStruct(PITCHED, f32), jax.ShapeD...  9.38 us
    pallas_call x1, Pallas kernels, local_solve(): kernel_call(solve_kernel, CUBE, HBM, [HBM, HBM] + [VMEM] * 3, [pltpu.VMEM...  8.15 us
    all_to_all x1, starting transfers between devices, body(): lax.all_to_all(messages.reshape(NGZ * ROWS, CZ), 'gz', 0, 0, tiled=True)  6.82 us
    pallas_call x1, Pallas kernels, finish(): kernel_call(finish_kernel, CUBE, HBM, [HBM] + [VMEM] * 4, [pltpu.VMEM((LI...  6.44 us
    all_to_all x1, starting transfers between devices, body(): lax.all_to_all(jnp.broadcast_to(own, (NGZ, CZ)), 'gz', 0, 0, tiled=True)  5.8 us
    pallas_call x1, Pallas kernels, local_sums(): kernel_call(sums_kernel, [FLAT, FLAT], [VMEM] * 2, [HBM, HBM] + [VMEM] *...  5.58 us
    all_to_all x1, starting transfers between devices, body(): lax.all_to_all(nodes, 'gy', 0, 0, tiled=True).reshape(2, LINES, CZ)  3.57 us
  transfers between devices with their start and end apart: 5, of which 2 were waited for; matrix products, arithmetic and copies ran while one was open for 0% of the time, Pallas kernels for 35%

profile of v2, /device:TPU:1, one launch (start us, length us, event | category | flops | bytes accessed | tf_op | source)
XLA Modules:
  0.0 72.9 jit_solution(15143729061228070923)
XLA Ops:
  0.0 1.2 %broadcast_in_dim.2 = f32[8,1,128]{2,1,0:T(1,128)} broadcast(f32[128]{0:T(128)} %param.5), dimensions={2} | broadcast | bytes 4608 | tf_op jit(solution)/shard_map/broadcast_in_dim | solution.py:753
  1.2 5.8 %all-to-all-start = ((f32[8,1,128]{2,1,0:T(1,128)}), f32[8,1,128]{2,1,0:T(1,128)S(1)}, u32[]{:S(2)}, u32[]{:S(2)}) async-start(f32[8,1,128]{2,1,0:T(1,128)} %broadcast_in_dim.2), calls=%async_computation | async-start | bytes 8192 | tf_op jit(solution)/shard_map/all_to_all | solution.py:753
  7.1 0.0 copy-start
  7.1 0.7 copy-done
  7.7 9.4 %y_sweeps.1 = (f32[12480,128]{1,0:T(8,128)}, f32[2,192,128]{2,1,0:T(8,128)S(1)}, f32[192,128]{1,0:T(8,128)S(1)}, f32[96,128]{1,0:T(8,128)S(1)}, f32[96,128]{1,0:T(8,128)S(1)}) custom-call(f32[192,64,128]{2,1,0:T(8,128)} %bitcast.17, bf16[192,64,128]{2,1,0:T(8,128)(2,1)} %bitcast.20, f32[1,128]{1,0:T(1,128)S(1)} %bitcast.16), custom_call_target="tpu_custom_call" | custom-call | bytes 36000000 | tf_op jit(solution)/shard_map/y_sweeps/pallas_call | solution.py:244
  17.1 1.6 %collective-permute-start = (f32[96,128]{1,0:T(8,128)S(1)}, f32[96,128]{1,0:T(8,128)S(1)}, u32[]{:S(2)}, u32[]{:S(2)}) collective-permute-start(f32[96,128]{1,0:T(8,128)S(1)} %get-tuple-element.27), channel_id=1, source_target_pairs={{0,1},{1,2},{2,3},{3,4},{4,5},{5,6},{6,7},{7,0},{8,9},{9,10},{10,1... | collective-permute-start | bytes 147464 | tf_op jit(solution)/shard_map/ppermute | solution.py:745
  18.7 0.0 collective-permute-start.1
  18.7 0.1 pad_add_fusion.rank_ref
  18.8 0.0 all-to-all-done
  18.8 2.4 %z_coefficients.1 = (f32[8,128]{1,0:T(8,128)S(1)}, bf16[256,512]{1,0:T(8,128)(2,1)S(1)}, f32[2,64,128]{2,1,0:T(8,128)S(1)}, f32[2,8,128]{2,1,0:T(8,128)S(1)}, bf...) custom-call(s32[2]{0:T(128)S(1)} %pad_add_fusion.rank_ref, ...), custom_call_target="tpu_custom_call" | custom-call | bytes 12000000 | tf_op jit(solution)/shard_map/z_coefficients/pallas_call | solution.py:524
  21.2 0.0 collective-permute-done.low_ref
  21.3 1.0 %collective-permute-done.1.high_ref = f32[96,128]{1,0:T(8,128)S(1)} collective-permute-done((f32[96,128]{1,0:T(8,128)S(1)}, f32[96,128]{1,0:T(8,128)S(1)}, u32[]{:S(2)}, u32[]{:S(2)}) %collective-permute-start.1) | collective-permute-done | bytes 49184 | tf_op jit(solution)/shard_map/ppermute | solution.py:745
  22.2 1.1 %repair.1 = (f32[2,192,128]{2,1,0:T(8,128)S(1)}, f32[192,128]{1,0:T(8,128)S(1)}) custom-call(s32[2]{0:T(128)S(1)} %pad_add_fusion.rank_ref, f32[2,192,128]{2,1,0:T(8,128)S(1)} %get-tuple-element.25.ends_ref, f32[192,128]{1,0:T(8,128)S(1)} %get-tuple-element.26.columns_ref, f32[96,128]{1,0:T(8,128)S(1)} %collective-permute-done.low_ref, ...), custom_call_target="tpu_custom_call" | custom-call | bytes 3000000 | tf_op jit(solution)/shard_map/repair/pallas_call | solution.py:319
  23.3 14.7 %all_to_all.34 = f32[16,24,128]{2,1,0:T(8,128)S(1)} all-to-all(f32[16,24,128]{2,1,0:T(8,128)S(1)} %bitcast.14), channel_id=1, replica_groups=mesh['gy'=16,'gz'=8] {'gy'}, dimensions={0} | all-to-all | bytes 393216 | tf_op jit(solution)/shard_map/all_to_all | solution.py:758
  38.0 1.3 %ring_scan.1 = f32[384,128]{1,0:T(8,128)} custom-call(s32[2]{0:T(128)S(1)} %pad_add_fusion.rank_ref, f32[384,128]{1,0:T(8,128)S(1)} %bitcast.13, f32[2,8,128]{2,1,0:T(8,128)S(1)} %get-tuple-element.32.turn_ref), custom_call_target="tpu_custom_call" | custom-call | bytes 3000000 | tf_op jit(solution)/shard_map/ring_scan/pallas_call | solution.py:350
  39.3 3.6 %all-to-all-start.2 = ((f32[16,24,128]{2,1,0:T(8,128)}), f32[16,24,128]{2,1,0:T(8,128)S(1)}, u32[]{:S(2)}, u32[]{:S(2)}) async-start(f32[16,24,128]{2,1,0:T(8,128)} %bitcast.8), calls=%async_computation.2 | async-start | bytes 393216 | tf_op jit(solution)/shard_map/all_to_all | solution.py:760
  42.9 5.6 %z_local_sums.1 = (f32[192,128]{1,0:T(8,128)S(1)}, f32[192,128]{1,0:T(8,128)S(1)}) custom-call(f32[12480,128]{1,0:T(8,128)} %get-tuple-element.24.m_hbm, f32[192,64,128]{2,1,0:T(8,128)} %bitcast.18, bf16[256,256]{1,0:T(8,128)(2,1)S(1)} %get-tuple-element.37.ends_ref, f32[192,128]{1,0:T(8,128)S(1)} %get-tuple-element.38.flux_ref, ...), custom_call_target="tpu_custom_call" | custom-call | bytes 24000000 | tf_op jit(solution)/shard_map/z_local_sums/pallas_call | solution.py:593
  48.4 1.4 %all-to-all-done.2 = f32[16,24,128]{2,1,0:T(8,128)S(1)} async-done(((f32[16,24,128]{2,1,0:T(8,128)}), f32[16,24,128]{2,1,0:T(8,128)S(1)}, u32[]{:S(2)}, u32[]{:S(2)}) %all-to-all-start.2) | async-done | bytes 196640 | tf_op jit(solution)/shard_map/all_to_all | solution.py:760
  49.9 1.6 %z_messages.1 = f32[8,96,128]{2,1,0:T(8,128)} custom-call(s32[2]{0:T(128)S(1)} %pad_add_fusion.rank_ref, f32[192,128]{1,0:T(8,128)S(1)} %get-tuple-element.41.sums_ref, f32[2,192,128]{2,1,0:T(8,128)S(1)} %bitcast.11, bf16[512,256]{1,0:T(8,128)(2,1)S(1)} %get-tuple-element.42.reach_ref), custom_call_target="tpu_custom_call" | custom-call | bytes 3000000 | tf_op jit(solution)/shard_map/z_messages/pallas_call | solution.py:626
  51.5 6.8 %all-to-all-start.3 = ((f32[8,96,128]{2,1,0:T(8,128)}), f32[8,96,128]{2,1,0:T(8,128)S(1)}, u32[]{:S(2)}, u32[]{:S(2)}) async-start(f32[8,96,128]{2,1,0:T(8,128)} %z_messages.1), calls=%async_computation.3 | async-start | bytes 786432 | tf_op jit(solution)/shard_map/all_to_all | solution.py:763
  58.3 8.2 %z_local_solve.1.y_hbm = f32[192,64,128]{2,1,0:T(8,128)} custom-call(f32[12480,128]{1,0:T(8,128)} %get-tuple-element.24.m_hbm, f32[192,64,128]{2,1,0:T(8,128)} %bitcast.19, f32[2,192,128]{2,1,0:T(8,128)S(1)} %bitcast.12, f32[2,64,128]{2,1,0:T(8,128)S(1)} %get-tuple-element.33.table_ref, bf16[256,256]{1,0:T(8,128)(2,1)S(1)} %get-tuple-element.34.green_ref), custom_call_target="tpu_custom_call" | custom-call | bytes 24000000 | tf_op jit(solution)/shard_map/z_local_solve/pallas_call | solution.py:656
  66.4 0.0 all-to-all-done.3.got_ref
  66.4 6.4 %z_carries.1 = f32[192,64,128]{2,1,0:T(8,128)} custom-call(f32[192,64,128]{2,1,0:T(8,128)} %z_local_solve.1.y_hbm, bf16[256,256]{1,0:T(8,128)(2,1)S(1)} %get-tuple-element.35.matrix_ref, f32[2,8,128]{2,1,0:T(8,128)S(1)} %get-tuple-element.36.share_ref, f32[192,128]{1,0:T(8,128)S(1)} %get-tuple-element.40.layer_ref, f32[8,96,128]{2,1,0:T(8,128)S(1)} %all-to-all-done.3.got_ref), custom_call_target="tpu_custom_call" | custom-call | bytes 24000000 | tf_op jit(solution)/shard_map/z_carries/pallas_call | solution.py:724
Async XLA Ops:
  1.2 17.6 %all-to-all-start = ((f32[8,1,128]{2,1,0:T(1,128)}), f32[8,1,128]{2,1,0:T(1,128)S(1)}, u32[]{:S(2)}, u32[]{:S(2)}) async-start(f32[8,1,128]{2,1,0:T(1,128)} %broadcast_in_dim.2), calls=%async_computation | async-start | bytes 8192 | tf_op jit(solution)/shard_map/all_to_all | solution.py:753
  7.1 0.7 copy-start
  17.1 4.2 %collective-permute-start = (f32[96,128]{1,0:T(8,128)S(1)}, f32[96,128]{1,0:T(8,128)S(1)}, u32[]{:S(2)}, u32[]{:S(2)}) collective-permute-start(f32[96,128]{1,0:T(8,128)S(1)} %get-tuple-element.27), channel_id=1, source_target_pairs={{0,1},{1,2},{2,3},{3,4},{4,5},{5,6},{6,7},{7,0},{8,9},{9,10},{10,1... | collective-permute-start | bytes 147464 | tf_op jit(solution)/shard_map/ppermute | solution.py:745
  18.7 3.5 %collective-permute-start.1 = (f32[96,128]{1,0:T(8,128)S(1)}, f32[96,128]{1,0:T(8,128)S(1)}, u32[]{:S(2)}, u32[]{:S(2)}) collective-permute-start(f32[96,128]{1,0:T(8,128)S(1)} %get-tuple-element.28), channel_id=1, source_target_pairs={{0,7},{1,0},{2,1},{3,2},{4,3},{5,4},{6,5},{7,6},{8,15},{9,8},{10,9... | collective-permute-start | bytes 147464 | tf_op jit(solution)/shard_map/ppermute | solution.py:745
  39.3 10.6 %all-to-all-start.2 = ((f32[16,24,128]{2,1,0:T(8,128)}), f32[16,24,128]{2,1,0:T(8,128)S(1)}, u32[]{:S(2)}, u32[]{:S(2)}) async-start(f32[16,24,128]{2,1,0:T(8,128)} %bitcast.8), calls=%async_computation.2 | async-start | bytes 393216 | tf_op jit(solution)/shard_map/all_to_all | solution.py:760
  51.5 15.0 %all-to-all-start.3 = ((f32[8,96,128]{2,1,0:T(8,128)}), f32[8,96,128]{2,1,0:T(8,128)S(1)}, u32[]{:S(2)}, u32[]{:S(2)}) async-start(f32[8,96,128]{2,1,0:T(8,128)} %z_messages.1), calls=%async_computation.3 | async-start | bytes 786432 | tf_op jit(solution)/shard_map/all_to_all | solution.py:763

commit v3 on v2

--- a/solution.py
+++ b/solution.py
@@ -129,12 +129,12 @@
 FLAT = jax.ShapeDtypeStruct((LINES, CZ), f32)
 PITCHED = (LINES * PITCH, CZ)
 ROWS = LINES // 2
-HALO = jax.ShapeDtypeStruct((ROWS, CZ), f32)
+HALO = jax.ShapeDtypeStruct((ROWS + 8, CZ), f32)
 
 
 def sweep_kernel(
-    u_hbm, q_hbm, eta_ref, m_hbm, ends_ref, columns_ref, up_ref, down_ref,
-    u_ref, q_ref, m_ref, x_buf, f_buf, sems,
+    u_hbm, q_hbm, eta_hbm, m_hbm, ends_ref, columns_ref, up_ref, down_ref,
+    u_ref, q_ref, m_ref, x_buf, f_buf, eta_ref, eta_sem, sems,
 ):
     lane = lanes()
     place = ((lane + 1) >> 1) & 63
@@ -148,7 +148,15 @@
     def stores(i):
         return (pltpu.make_async_copy(pitched(m_ref, i), pitched(m_hbm, i), sems.at[2, i]),)
 
+    eta_copy = pltpu.make_async_copy(eta_hbm, eta_ref, eta_sem)
+    eta_copy.start()
+    for i in range(AHEAD):
+        for copy in fetches(i):
+            copy.start()
+    eta_copy.wait()
     eta = jnp.broadcast_to(eta_ref[...], (8, CZ))
+    up_ref[pl.ds(ROWS, 8), :] = eta
+    down_ref[pl.ds(ROWS, 8), :] = eta
     face_low = jnp.where(lane == 0, 0.0, z_rate * 0.5 * (pltpu.roll(eta, 1, 1) + eta))
     face_high = jnp.where(lane == CZ - 1, 0.0, z_rate * 0.5 * (eta + pltpu.roll(eta, CZ - 1, 1)))
     decay, peak = root_of(eta)
@@ -207,9 +215,6 @@
             ends_ref[0, rows(i, g), :] = forth[g]
             ends_ref[1, rows(i, g), :] = back[g]
 
-    for i in range(AHEAD):
-        for copy in fetches(i):
-            copy.start()
     for copy in fetches(0):
         copy.wait()
     right_side(0, range(PER * CY // 8), jnp.zeros((8, CZ), f32))
@@ -236,8 +241,8 @@
             copy.wait()
     first, second = columns_ref[:ROWS], columns_ref[ROWS:]
     odd = lanes((ROWS, CZ)) & 1 == 1
-    up_ref[...] = jnp.where(odd, first, pltpu.roll(second, 1, 1))
-    down_ref[...] = jnp.where(odd, pltpu.roll(second, CZ - 1, 1), first)
+    up_ref[:ROWS] = jnp.where(odd, first, pltpu.roll(second, 1, 1))
+    down_ref[:ROWS] = jnp.where(odd, pltpu.roll(second, CZ - 1, 1), first)
 
 
 def sweeps(u, q, own):
@@ -251,13 +256,15 @@
             HALO,
         ],
         [HBM] + [VMEM] * 4,
-        [HBM, HBM, VMEM],
+        [HBM] * 3,
         [
             pltpu.VMEM((LINES, CY, CZ), f32),
             pltpu.VMEM((LINES, CY, CZ), bf16),
             pltpu.VMEM(PITCHED, f32),
             pltpu.VMEM((2 * PER * PITCH, CZ), f32),
             pltpu.VMEM((PER * PITCH, CZ), f32),
+            pltpu.VMEM((1, CZ), f32),
+            pltpu.SemaphoreType.DMA,
             pltpu.SemaphoreType.DMA((3, STEPS)),
         ],
         name="y_sweeps",
@@ -290,14 +297,60 @@
     return x
 
 
+def sided_by(low):
+    def sided(x):
+        return jnp.where(
+            low, jnp.broadcast_to(x[:, :1], low.shape), jnp.broadcast_to(x[:, CZ - 1 :], low.shape)
+        )
+
+    return sided
+
+
+def line_kernel(up_ref, repair_ref, turn_ref):
+    decay, _ = root_of(up_ref[pl.ds(ROWS, 8), :])
+    whole = power_64(decay)
+    around = whole
+    for _ in range(4):
+        around = around * around
+    turn_ref[0] = whole
+    turn_ref[1] = 1.0 / (1.0 - around)
+    square = (CZ, CZ)
+    y, side = flux_place(rows_of(square))
+    low = side == 0
+    base = sided_by(low)(decay[:1])
+    place = lanes(square) == jnp.where(low, 0, CZ - 1)
+    forth = jnp.where(place, raised(base, CY - 1 - y), 0.0)
+    back = jnp.where(place, raised(base, y), 0.0)
+    repair_ref[...] = paired(jnp.concatenate([forth, back], axis=1))
+
+
+def line_matrices(up):
+    shapes = [
+        jax.ShapeDtypeStruct((2 * CZ, 4 * CZ), bf16),
+        jax.ShapeDtypeStruct((2, 8, CZ), f32),
+    ]
+    return kernel_call(line_kernel, shapes, [VMEM] * 2, [VMEM], name="line_matrices")(up)
+
+
 def repair_kernel(
-    rank_ref, ends_ref, columns_ref, low_ref, high_ref, face_ref, repair_ref, out_ref, flux_ref
+    rank_ref, ends_ref, columns_ref, up_ref, low_ref, high_ref, repair_ref,
+    out_ref, flux_ref, near_ref,
 ):
     rank = rank_ref[0]
+    inner_low, inner_high = rank > 0, rank < NGZ - 1
+    own, low_eta, high_eta = (ref[pl.ds(ROWS, 8), :] for ref in (up_ref, low_ref, high_ref))
+    row = rows_of()
+    near_ref[...] = jnp.where(row == 0, low_eta, jnp.where(row == 1, own, high_eta))
+    own = own[:1]
+    low_eta = jnp.where(inner_low, low_eta[:1], 0.0)[:, CZ - 1 :]
+    high_eta = jnp.where(inner_high, high_eta[:1], 0.0)[:, :1]
+    face_low = jnp.broadcast_to(z_rate * 0.5 * (low_eta + own[:, :1]), (1, CZ))
+    face_high = jnp.broadcast_to(z_rate * 0.5 * (own[:, CZ - 1 :] + high_eta), (1, CZ))
+    face = jnp.where(lanes((1, CZ)) & 1 == 0, face_low, face_high)
+    face = jnp.broadcast_to(face, (ROWS, CZ))
     even = lanes((ROWS, CZ)) & 1 == 0
-    face = jnp.broadcast_to(face_ref[:1], (ROWS, CZ))
-    low = jnp.where(rank > 0, low_ref[...], 0.0)
-    high = jnp.where(rank < NGZ - 1, high_ref[...], 0.0)
+    low = jnp.where(inner_low, low_ref[:ROWS], 0.0)
+    high = jnp.where(inner_high, high_ref[:ROWS], 0.0)
     outer = (
         jnp.where(even, pltpu.roll(low, 1, 1), pltpu.roll(high, 1, 1)),
         jnp.where(even, low, pltpu.roll(high, 2, 1)),
@@ -313,13 +366,23 @@
         out_ref[1, at, :] = ends_ref[1, at, :] + added[:, CZ:]
 
 
-def repair(ranks, ends, columns, low, high, face, matrix):
-    shapes = [jax.ShapeDtypeStruct((2, LINES, CZ), f32), FLAT]
-    call = kernel_call(repair_kernel, shapes, [VMEM] * 2, [SMEM] + [VMEM] * 6, name="repair")
-    return call(ranks, ends, columns, low, high, face, matrix)
-
-
-def ring_kernel(rank_ref, ends_ref, turn_ref, out_ref):
+def repair(ranks, ends, columns, up, low, high, matrix):
+    shapes = [
+        jax.ShapeDtypeStruct((2, LINES, CZ), f32),
+        FLAT,
+        jax.ShapeDtypeStruct((NGZ, CZ), f32),
+    ]
+    call = kernel_call(repair_kernel, shapes, [VMEM] * 3, [SMEM] + [VMEM] * 6, name="repair")
+    return call(ranks, ends, columns, up, low, high, matrix)
+
+
+def ring_kernel(
+    rank_ref, ends_ref, turn_ref, near_ref, far_low_ref, far_high_ref, out_ref, eta_ref, eta_buf
+):
+    eta_buf[0:2, :] = far_low_ref[1:3, :]
+    eta_buf[2:5, :] = near_ref[0:3, :]
+    eta_buf[5:8, :] = far_high_ref[0:3, :]
+    eta_ref[...] = pltpu.roll(eta_buf[...], lax.rem(rank_ref[0] + 5, 8), 0)
     rows = 2 * LINES // NGY
     upward = rank_ref[1] < NGY // 2
     whole, closing = turn_ref[0], turn_ref[1]
@@ -345,16 +408,20 @@
             out_ref[at(node), :] = jnp.where(upward, ups[node], downs[node])
 
 
-def ring_scan(ranks, ends, turn):
-    shape = jax.ShapeDtypeStruct(ends.shape, f32)
-    return kernel_call(ring_kernel, shape, VMEM, [SMEM, VMEM, VMEM], name="ring_scan")(
-        ranks, ends, turn
-    )
+def ring_scan(ranks, ends, turn, near, far_low, far_high):
+    rows = jax.ShapeDtypeStruct((NGZ, CZ), f32)
+    return kernel_call(
+        ring_kernel,
+        [jax.ShapeDtypeStruct(ends.shape, f32), rows],
+        [VMEM] * 2,
+        [SMEM] + [VMEM] * 5,
+        [pltpu.VMEM((NGZ, CZ), f32)],
+        name="ring_scan",
+    )(ranks, ends, turn, near, far_low, far_high)
 
 
 def coefficient_kernel(
-    rank_ref, eta_ref, face_ref, repair_ref, table_ref,
-    turn_ref, green_ref, ends_ref, carry_ref, share_ref, layer_ref, reach_ref,
+    rank_ref, eta_ref, table_ref, green_ref, ends_ref, carry_ref, share_ref, layer_ref, reach_ref,
 ):
     rank = rank_ref[0]
     lane, row = lanes(), rows_of()
@@ -434,8 +501,11 @@
 
     scale = own(inverse)
     own_up, own_down = own(link_up), own(link_down)
-    share_ref[0] = share_up * jnp.broadcast_to(own_up[:, :1], (8, CZ))
-    share_ref[1] = share_down * jnp.broadcast_to(own_down[:, CZ - 1 :], (8, CZ))
+    turned_by = lax.rem(NGZ - rank, NGZ)
+    share_up = share_up * jnp.broadcast_to(own_up[:, :1], (8, CZ))
+    share_down = share_down * jnp.broadcast_to(own_down[:, CZ - 1 :], (8, CZ))
+    share_ref[0] = pltpu.roll(share_up, turned_by, 0)
+    share_ref[1] = pltpu.roll(share_down, turned_by, 0)
     lane_1 = lanes((1, CZ))
     within_up = running(jnp.broadcast_to(jnp.where(lane_1 == 0, 1.0, own_up), (8, CZ)), True)
     within_down = running(
@@ -473,12 +543,6 @@
         ref[...] = paired(matrix)
 
     decay, peak = root_of(own(eta))
-    whole = power_64(jnp.broadcast_to(decay, (8, CZ)))
-    around = whole
-    for _ in range(4):
-        around = around * around
-    turn_ref[0] = whole
-    turn_ref[1] = 1.0 / (1.0 - around)
     y = row_sq & 63
     wide = jnp.broadcast_to(decay, square)
     start = jnp.broadcast_to(peak * decay, square)
@@ -491,23 +555,8 @@
     reach_ref[...] = paired(jnp.concatenate(reach, axis=0))
     y, side = flux_place(row_sq)
     low = side == 0
-
-    def sided(x):
-        return jnp.where(
-            low, jnp.broadcast_to(x[:, :1], square), jnp.broadcast_to(x[:, CZ - 1 :], square)
-        )
-
-    face = jnp.where(
-        lane_1 & 1 == 0,
-        jnp.broadcast_to(own(face_low)[:, :1], (1, CZ)),
-        jnp.broadcast_to(own(face_high)[:, CZ - 1 :], (1, CZ)),
-    )
-    face_ref[...] = jnp.broadcast_to(face, (8, CZ))
+    sided = sided_by(low)
     base = sided(decay)
-    place = lane_sq == jnp.where(low, 0, CZ - 1)
-    forth = jnp.where(place, raised(base, CY - 1 - y), 0.0)
-    back = jnp.where(place, raised(base, y), 0.0)
-    repair_ref[...] = paired(jnp.concatenate([forth, back], axis=1))
     apart = jnp.abs(y - (lane_sq & 63))
     spread = jnp.where(low == (lane_sq < 64), sided(peak) * raised(base, apart), 0.0)
     same_y = (lane_sq & 63) == (row_sq & 63)
@@ -524,10 +573,7 @@
     return kernel_call(
         coefficient_kernel,
         [
-            jax.ShapeDtypeStruct((8, CZ), f32),
-            matrix(1, 2),
             jax.ShapeDtypeStruct((2, CY, CZ), f32),
-            jax.ShapeDtypeStruct((2, 8, CZ), f32),
             matrix(1, 1),
             matrix(1, 1),
             matrix(1, 1),
@@ -535,7 +581,7 @@
             matrix(1, 2),
             matrix(2, 1),
         ],
-        [VMEM] * 10,
+        [VMEM] * 7,
         [SMEM, VMEM],
         name="z_coefficients",
         us=4,
@@ -608,7 +654,7 @@
     )(m, u, ends, flux, spread)
 
 
-def messages_kernel(rank_ref, sums_ref, carry_ref, reach_ref, out_ref):
+def messages_kernel(rank_ref, sums_ref, carry_ref, reach_ref, *out_refs):
     rank = rank_ref[0]
     carries = jnp.concatenate([carry_ref[0], carry_ref[1]], axis=1)
     sums = sums_ref[...] + pair_dot(carries, reach_ref[...])
@@ -616,23 +662,21 @@
     lower = lanes((ROWS, CZ)) < 64
     up = jnp.where(lower, first, pltpu.roll(second, 64, 1))
     down = jnp.where(lower, pltpu.roll(first, 64, 1), second)
-    for k in range(NGZ):
-        out_ref[k] = jnp.where(rank > k, down, up)
+    for k in range(1, NGZ):
+        out_refs[k - 1][...] = jnp.where(rank >= k, down, up)
 
 
 def messages_of(ranks, sums, carries, reach):
-    shape = jax.ShapeDtypeStruct((NGZ, ROWS, CZ), f32)
-    call = kernel_call(messages_kernel, shape, VMEM, [SMEM] + [VMEM] * 3, name="z_messages")
+    shapes = [jax.ShapeDtypeStruct((ROWS, CZ), f32)] * (NGZ - 1)
+    specs = [VMEM] * (NGZ - 1)
+    call = kernel_call(messages_kernel, shapes, specs, [SMEM] + [VMEM] * 3, name="z_messages")
     return call(ranks, sums, carries, reach)
 
 
 def solve_kernel(
-    m_hbm, u_hbm, carry_ref, table_ref, green_ref, y_hbm, m_ref, u_ref, y_ref, left_ref, sems
+    m_hbm, u_hbm, carry_ref, table_ref, green_ref, y_ref, m_ref, u_ref, left_ref, sems
 ):
     tall = (CY, CZ)
-
-    def stores(i):
-        return (pltpu.make_async_copy(chunk(y_ref, i), chunk(y_hbm, i), sems.at[2, i]),)
 
     def work(i):
         for g in range(PER // GROUP):
@@ -649,47 +693,44 @@
             for c in range(GROUP):
                 y_ref[first + c] = u_ref[first + c] + result[c * CY : (c + 1) * CY]
 
-    pipeline(fetches_of(u_hbm, m_hbm, u_ref, m_ref, sems), stores, work)
+    pipeline(fetches_of(u_hbm, m_hbm, u_ref, m_ref, sems), no_copies, work)
 
 
 def local_solve(m, u, carries, table, green):
     return kernel_call(
         solve_kernel,
         CUBE,
-        HBM,
+        VMEM,
         [HBM, HBM] + [VMEM] * 3,
         [
             pltpu.VMEM(PITCHED, f32),
-            pltpu.VMEM((LINES, CY, CZ), f32),
             pltpu.VMEM((LINES, CY, CZ), f32),
             pltpu.VMEM((SLOTS, GROUP * CY, 2 * CZ), bf16),
             pltpu.SemaphoreType.DMA((3, STEPS)),
         ],
         name="z_local_solve",
-        mib=48,
+        mib=42,
         us=8,
     )(m, u, carries, table, green)
 
 
 def finish_kernel(
-    y_hbm, matrix_ref, share_ref, layer_ref, got_ref,
-    out_hbm, y_ref, out_ref, left_ref, high_ref, mid_ref, sems,
+    y_ref, matrix_ref, share_ref, layer_ref, *rest
 ):
+    got_refs = rest[: NGZ - 1]
+    out_hbm, out_ref, left_ref, high_ref, mid_ref, sems = rest[NGZ - 1 :]
     lower = lanes((ROWS, CZ)) < 64
     tall = (CY, CZ)
     mask = unit_mask(tall)
 
-    def fetches(i):
-        return (pltpu.make_async_copy(chunk(y_hbm, i), chunk(y_ref, i), sems.at[0, i]),)
-
     def stores(i):
         return (pltpu.make_async_copy(chunk(out_ref, i), chunk(out_hbm, i), sems.at[1, i]),)
 
     def prepare():
         up = jnp.zeros((ROWS, CZ), f32)
         down = jnp.zeros((ROWS, CZ), f32)
-        for k in range(NGZ):
-            value = got_ref[k]
+        for k in range(1, NGZ):
+            value = got_refs[k - 1][...]
             up += jnp.broadcast_to(share_ref[0, k : k + 1, :], (ROWS, CZ)) * value
             down += jnp.broadcast_to(share_ref[1, k : k + 1, :], (ROWS, CZ)) * value
         both = (
@@ -717,7 +758,7 @@
             for c in range(GROUP):
                 out_ref[first + c] = y_ref[first + c] + result[c * CY : (c + 1) * CY]
 
-    pipeline(fetches, stores, work, prepare)
+    pipeline(no_copies, stores, work, prepare)
 
 
 def finish(y, matrix, share, layer, got):
@@ -725,9 +766,8 @@
         finish_kernel,
         CUBE,
         HBM,
-        [HBM] + [VMEM] * 4,
+        [VMEM] * (NGZ + 3),
         [
-            pltpu.VMEM((LINES, CY, CZ), f32),
             pltpu.VMEM((LINES, CY, CZ), f32),
             pltpu.VMEM((SLOTS, GROUP * CY, 2 * CZ), bf16),
             pltpu.VMEM((LINES, CZ), f32),
@@ -735,9 +775,9 @@
             pltpu.SemaphoreType.DMA((2, STEPS)),
         ],
         name="z_carries",
-        mib=48,
+        mib=42,
         us=8,
-    )(y, matrix, share, layer, got)
+    )(y, matrix, share, layer, *got)
 
 
 def shifted(x, axis, by):
@@ -750,19 +790,19 @@
     q = source_term.reshape(LINES, CY, CZ)
     ranks = jnp.stack([lax.axis_index("gz"), lax.axis_index("gy")]).astype(jnp.int32)
     own = resistivity.reshape(1, CZ)
-    etas = lax.all_to_all(jnp.broadcast_to(own, (NGZ, CZ)), "gz", 0, 0, tiled=True)
     m, ends, columns, up, down = sweeps(u, q, own)
     low, high = shifted(up, "gz", 1), shifted(down, "gz", -1)
-    face, matrix, table, turn, green, last, vector, share, layers, reach = coefficients(ranks, etas)
-    ends, flux = repair(ranks, ends, columns, low, high, face, matrix)
+    matrix, turn = line_matrices(up)
+    ends, flux, near = repair(ranks, ends, columns, up, low, high, matrix)
     nodes = lax.all_to_all(ends.reshape(2 * LINES, CZ), "gy", 0, 0, tiled=True)
-    nodes = ring_scan(ranks, nodes, turn)
+    far_low, far_high = shifted(near, "gz", 3), shifted(near, "gz", -3)
+    nodes, etas = ring_scan(ranks, nodes, turn, near, far_low, far_high)
     carries = lax.all_to_all(nodes, "gy", 0, 0, tiled=True).reshape(2, LINES, CZ)
+    table, green, last, vector, share, layers, reach = coefficients(ranks, etas)
     sums, layer = local_sums(m, u, last, flux, layers)
     messages = messages_of(ranks, sums, carries, reach)
-    got = lax.all_to_all(messages.reshape(NGZ * ROWS, CZ), "gz", 0, 0, tiled=True)
+    got = [shifted(x, "gz", -k) for k, x in enumerate(messages, start=1)]
     y = local_solve(m, u, carries, table, green)
-    got = got.reshape(NGZ, ROWS, CZ)
     return finish(y, vector, share, layer, got).reshape(fields.shape)
 
 

time: 73.3 us -> 67.8 us (0.925)
  blocking collectives: 14.7 us -> 0 us
  starting transfers between devices: 17.8 us -> 27.3 us
  waiting for transfers between devices: 2.44 us -> 7.2 us
  Pallas kernels: 35.9 us -> 32.1 us
  local copies, waits for them, and re-layouts: 1.9 us -> 0.65 us
    all_to_all x1 -> x0, blocking collectives: 14.7 us -> none  [body(): nodes = lax.all_to_all(ends.reshape(2 * LINES, CZ), 'gy', 0, 0, tiled=True)]
    ppermute x2 -> x11, starting transfers between devices: 1.64 us -> 13.2 us  [shifted(): return lax.ppermute(x, axis, [(i, (i + by) % n) for i in range(n)])]
    ppermute x2 -> x11, waiting for transfers between devices: 1 us -> 6.92 us  [shifted(): return lax.ppermute(x, axis, [(i, (i + by) % n) for i in range(n)])]
    all_to_all x2 -> x1, starting transfers between devices: 12.6 us -> 7.77 us  [body(): nodes = lax.all_to_all(ends.reshape(2 * LINES, CZ), 'gy', 0, 0, tiled=True)]
    pallas_call x5 -> x6, Pallas kernels: 19.4 us -> 16.3 us  [the longest x1 6.23 us: local_solve(): kernel_call(solve_kernel, CUBE, VMEM, [HBM, HBM] + [VMEM] * 3, [pltpu.VME...]
    all_to_all x1, starting transfers between devices: 3.57 us -> 6.3 us  [body(): lax.all_to_all(nodes, 'gy', 0, 0, tiled=True).reshape(2, LINES, CZ)]
    all_to_all x1, waiting for transfers between devices: 1.43 us -> 0.01 us  [body(): lax.all_to_all(nodes, 'gy', 0, 0, tiled=True).reshape(2, LINES, CZ)]
    broadcast_in_dim x1 -> x0, local copies, waits for them, and re-layouts: 1.25 us -> none  [body(): jnp.broadcast_to(own, (NGZ, CZ))]
  transfers between devices with their start and end apart: 5 -> 13, of which waited for: 2 -> 5; matrix products, arithmetic and copies ran while one was open for 0% -> 0% of each run, Pallas kernels for 35% -> 21%
where the time goes in v3:
time: 67.8 us; the launch traced here: 67.4 us
  Pallas kernels  32.1 us (47%)
  starting transfers between devices  27.3 us (40%)
  waiting for transfers between devices  7.2 us (11%)
    ppermute x11, starting transfers between devices, shifted(): return lax.ppermute(x, axis, [(i, (i + by) % n) for i in range(n)])  13.2 us
    pallas_call x1, Pallas kernels, sweeps(): kernel_call(sweep_kernel, [jax.ShapeDtypeStruct(PITCHED, f32), jax.ShapeD...  9.38 us
    all_to_all x1, starting transfers between devices, body(): nodes = lax.all_to_all(ends.reshape(2 * LINES, CZ), 'gy', 0, 0, tiled=True)  7.77 us
    ppermute x11, waiting for transfers between devices, shifted(): return lax.ppermute(x, axis, [(i, (i + by) % n) for i in range(n)])  6.92 us
    all_to_all x1, starting transfers between devices, body(): lax.all_to_all(nodes, 'gy', 0, 0, tiled=True).reshape(2, LINES, CZ)  6.3 us
    pallas_call x1, Pallas kernels, local_solve(): kernel_call(solve_kernel, CUBE, VMEM, [HBM, HBM] + [VMEM] * 3, [pltpu.VME...  6.23 us
    pallas_call x1, Pallas kernels, local_sums(): kernel_call(sums_kernel, [FLAT, FLAT], [VMEM] * 2, [HBM, HBM] + [VMEM] *...  5.58 us
    pallas_call x1, Pallas kernels, finish(): kernel_call(finish_kernel, CUBE, HBM, [VMEM] * (NGZ + 3), [pltpu.VMEM((LI...  4.44 us
  transfers between devices with their start and end apart: 13, of which 5 were waited for; matrix products, arithmetic and copies ran while one was open for 0% of the time, Pallas kernels for 21%

profile of v3, /device:TPU:1, one launch (start us, length us, event | category | flops | bytes accessed | tf_op | source)
XLA Modules:
  0.0 67.4 jit_solution(16769100575289437394)
XLA Ops:
  0.0 0.7 copy-done
  0.7 9.4 %y_sweeps.1 = (f32[12480,128]{1,0:T(8,128)}, f32[2,192,128]{2,1,0:T(8,128)S(1)}, f32[192,128]{1,0:T(8,128)S(1)}, f32[104,128]{1,0:T(8,128)S(1)}, f32[104,128]{1,0:T(8,128)S(1)}) custom-call(f32[192,64,128]{2,1,0:T(8,128)} %bitcast.14, bf16[192,64,128]{2,1,0:T(8,128)(2,1)} %bitcast.17, f32[1,128]{1,0:T(1,128)S(1)} %bitcast.13), custom_call_target="tpu_custom_call" | custom-call | bytes 36000000 | tf_op jit(solution)/shard_map/y_sweeps/pallas_call | solution.py:249
  10.0 2.6 %collective-permute-start = (f32[104,128]{1,0:T(8,128)S(1)}, f32[104,128]{1,0:T(8,128)S(1)}, u32[]{:S(2)}, u32[]{:S(2)}) collective-permute-start(f32[104,128]{1,0:T(8,128)S(1)} %get-tuple-element.36.up_ref), channel_id=1, source_target_pairs={{0,1},{1,2},{2,3},{3,4},{4,5},{5,6},{6,7},{7,0},{8,9},{9,10},{10,1... | collective-permute-start | bytes 159752 | tf_op jit(solution)/shard_map/ppermute | solution.py:785
  13.0 0.9 %collective-permute-done.low_ref = f32[104,128]{1,0:T(8,128)S(1)} collective-permute-done((f32[104,128]{1,0:T(8,128)S(1)}, f32[104,128]{1,0:T(8,128)S(1)}, u32[]{:S(2)}, u32[]{:S(2)}) %collective-permute-start) | collective-permute-done | bytes 53280 | tf_op jit(solution)/shard_map/ppermute | solution.py:785
  13.9 2.3 %collective-permute-done.1.high_ref = f32[104,128]{1,0:T(8,128)S(1)} collective-permute-done((f32[104,128]{1,0:T(8,128)S(1)}, f32[104,128]{1,0:T(8,128)S(1)}, u32[]{:S(2)}, u32[]{:S(2)}) %collective-permute-start.1) | collective-permute-done | bytes 53280 | tf_op jit(solution)/shard_map/ppermute | solution.py:785
  16.2 1.8 %repair.1 = (f32[2,192,128]{2,1,0:T(8,128)}, f32[192,128]{1,0:T(8,128)S(1)}, f32[8,128]{1,0:T(8,128)S(1)}) custom-call(s32[2]{0:T(128)S(1)} %pad_add_fusion.rank_ref, f32[2,192,128]{2,1,0:T(8,128)S(1)} %get-tuple-element.34.ends_ref, f32[192,128]{1,0:T(8,128)S(1)} %get-tuple-element.35.columns_ref, f32[104,128]{1,0:T(8,128)S(1)} %get-tuple-element.36.up_ref, ...), custom_call_target="tpu_custom_call" | custom-call | bytes 3000000 | tf_op jit(solution)/shard_map/repair/pallas_call | solution.py:376
  18.0 7.8 %all-to-all-start = ((f32[16,24,128]{2,1,0:T(8,128)}), f32[16,24,128]{2,1,0:T(8,128)S(1)}, u32[]{:S(2)}, u32[]{:S(2)}) async-start(f32[16,24,128]{2,1,0:T(8,128)} %bitcast.5), calls=%async_computation | async-start | bytes 393216 | tf_op jit(solution)/shard_map/all_to_all | solution.py:797
  25.8 1.9 %collective-permute-start.2 = (f32[8,128]{1,0:T(8,128)S(1)}, f32[8,128]{1,0:T(8,128)S(1)}, u32[]{:S(2)}, u32[]{:S(2)}) collective-permute-start(f32[8,128]{1,0:T(8,128)S(1)} %get-tuple-element.41.near_ref), channel_id=1, source_target_pairs={{0,3},{1,4},{2,5},{3,6},{4,7},{5,0},{6,1},{7,2},{8,11},{9,12},{10,... | collective-permute-start | bytes 12296 | tf_op jit(solution)/shard_map/ppermute | solution.py:785
  27.7 1.1 %collective-permute-start.3 = (f32[8,128]{1,0:T(8,128)S(1)}, f32[8,128]{1,0:T(8,128)S(1)}, u32[]{:S(2)}, u32[]{:S(2)}) collective-permute-start(f32[8,128]{1,0:T(8,128)S(1)} %get-tuple-element.41.near_ref), channel_id=1, source_target_pairs={{0,5},{1,6},{2,7},{3,0},{4,1},{5,2},{6,3},{7,4},{8,13},{9,14},{10,... | collective-permute-start | bytes 12296 | tf_op jit(solution)/shard_map/ppermute | solution.py:785
  28.8 1.6 %collective-permute-done.2.far_low_ref = f32[8,128]{1,0:T(8,128)S(1)} collective-permute-done((f32[8,128]{1,0:T(8,128)S(1)}, f32[8,128]{1,0:T(8,128)S(1)}, u32[]{:S(2)}, u32[]{:S(2)}) %collective-permute-start.2) | collective-permute-done | bytes 4128 | tf_op jit(solution)/shard_map/ppermute | solution.py:785
  30.4 2.1 %collective-permute-done.3.far_high_ref = f32[8,128]{1,0:T(8,128)S(1)} collective-permute-done((f32[8,128]{1,0:T(8,128)S(1)}, f32[8,128]{1,0:T(8,128)S(1)}, u32[]{:S(2)}, u32[]{:S(2)}) %collective-permute-start.3) | collective-permute-done | bytes 4128 | tf_op jit(solution)/shard_map/ppermute | solution.py:785
  32.8 1.3 %ring_scan.1 = (f32[384,128]{1,0:T(8,128)}, f32[8,128]{1,0:T(8,128)S(1)}) custom-call(s32[2]{0:T(128)S(1)} %pad_add_fusion.rank_ref, f32[384,128]{1,0:T(8,128)S(1)} %bitcast.12, f32[2,8,128]{2,1,0:T(8,128)S(1)} %get-tuple-element.40.turn_ref, f32[8,128]{1,0:T(8,128)S(1)} %get-tuple-element.41.near_ref, f32[8,128]{1,0:T(8,128)S(1)} %collective-permute-done.2.far_low_ref, ...), custom_call_target="tpu_custom_call" | custom-call | bytes 3000000 | tf_op jit(solution)/shard_map/ring_scan/pallas_call | solution.py:413
  34.1 6.3 %all-to-all-start.1 = ((f32[16,24,128]{2,1,0:T(8,128)}), f32[16,24,128]{2,1,0:T(8,128)S(1)}, u32[]{:S(2)}, u32[]{:S(2)}) async-start(f32[16,24,128]{2,1,0:T(8,128)} %bitcast.7), calls=%async_computation.1 | async-start | bytes 393216 | tf_op jit(solution)/shard_map/all_to_all | solution.py:800
  40.4 2.3 %z_coefficients.1 = (f32[2,64,128]{2,1,0:T(8,128)S(1)}, bf16[256,256]{1,0:T(8,128)(2,1)S(1)}, bf16[256,256]{1,0:T(8,128)(2,1)S(1)}, bf16[256,256]{1,0:T(8,128)(2...) custom-call(s32[2]{0:T(128)S(1)} %pad_add_fusion.rank_ref, ...), custom_call_target="tpu_custom_call" | custom-call | bytes 12000000 | tf_op jit(solution)/shard_map/z_coefficients/pallas_call | solution.py:573
  42.7 5.6 %z_local_sums.1 = (f32[192,128]{1,0:T(8,128)S(1)}, f32[192,128]{1,0:T(8,128)S(1)}) custom-call(f32[12480,128]{1,0:T(8,128)} %get-tuple-element.33.m_hbm, f32[192,64,128]{2,1,0:T(8,128)} %bitcast.15, bf16[256,256]{1,0:T(8,128)(2,1)S(1)} %get-tuple-element.48.ends_ref, f32[192,128]{1,0:T(8,128)S(1)} %get-tuple-element.49.flux_ref, ...), custom_call_target="tpu_custom_call" | custom-call | bytes 24000000 | tf_op jit(solution)/shard_map/z_local_sums/pallas_call | solution.py:639
  48.3 0.8 %z_messages.1 = (f32[96,128]{1,0:T(8,128)S(1)}, f32[96,128]{1,0:T(8,128)S(1)}, f32[96,128]{1,0:T(8,128)S(1)}, f32[96,128]{1,0:T(8,128)S(1)}, f32[96,128]{1,0:T(8...) custom-call(s32[2]{0:T(128)S(1)} %pad_add_fusion.rank_ref, f32[192,128]{1,0:T(8,128)S(1)} %get-tuple-element.52.sums_ref, ...), custom_call_target="tpu_custom_call" | custom-call | bytes 3000000 | tf_op jit(solution)/shard_map/z_messages/pallas_call | solution.py:673
  49.1 0.4 collective-permute-start.10
  49.6 1.8 %collective-permute-start.5 = (f32[96,128]{1,0:T(8,128)S(1)}, f32[96,128]{1,0:T(8,128)S(1)}, u32[]{:S(2)}, u32[]{:S(2)}) collective-permute-start(f32[96,128]{1,0:T(8,128)S(1)} %get-tuple-element.55), channel_id=1, source_target_pairs={{0,6},{1,7},{2,0},{3,1},{4,2},{5,3},{6,4},{7,5},{8,14},{9,15},{10,... | collective-permute-start | bytes 147464 | tf_op jit(solution)/shard_map/ppermute | solution.py:785
  51.4 2.2 %collective-permute-start.6 = (f32[96,128]{1,0:T(8,128)S(1)}, f32[96,128]{1,0:T(8,128)S(1)}, u32[]{:S(2)}, u32[]{:S(2)}) collective-permute-start(f32[96,128]{1,0:T(8,128)S(1)} %get-tuple-element.56), channel_id=1, source_target_pairs={{0,5},{1,6},{2,7},{3,0},{4,1},{5,2},{6,3},{7,4},{8,13},{9,14},{10,... | collective-permute-start | bytes 147464 | tf_op jit(solution)/shard_map/ppermute | solution.py:785
  53.6 1.6 %collective-permute-start.7 = (f32[96,128]{1,0:T(8,128)S(1)}, f32[96,128]{1,0:T(8,128)S(1)}, u32[]{:S(2)}, u32[]{:S(2)}) collective-permute-start(f32[96,128]{1,0:T(8,128)S(1)} %get-tuple-element.57), channel_id=1, source_target_pairs={{0,4},{1,5},{2,6},{3,7},{4,0},{5,1},{6,2},{7,3},{8,12},{9,13},{10,... | collective-permute-start | bytes 147464 | tf_op jit(solution)/shard_map/ppermute | solution.py:785
  55.2 1.1 %collective-permute-start.8 = (f32[96,128]{1,0:T(8,128)S(1)}, f32[96,128]{1,0:T(8,128)S(1)}, u32[]{:S(2)}, u32[]{:S(2)}) collective-permute-start(f32[96,128]{1,0:T(8,128)S(1)} %get-tuple-element.58), channel_id=1, source_target_pairs={{0,3},{1,4},{2,5},{3,6},{4,7},{5,0},{6,1},{7,2},{8,11},{9,12},{10,... | collective-permute-start | bytes 147464 | tf_op jit(solution)/shard_map/ppermute | solution.py:785
  56.3 0.4 collective-permute-start.9
  56.7 6.2 %z_local_solve.1.y_ref = f32[192,64,128]{2,1,0:T(8,128)S(1)} custom-call(f32[12480,128]{1,0:T(8,128)} %get-tuple-element.33.m_hbm, f32[192,64,128]{2,1,0:T(8,128)} %bitcast.16, f32[2,192,128]{2,1,0:T(8,128)S(1)} %bitcast.11, f32[2,64,128]{2,1,0:T(8,128)S(1)} %get-tuple-element.44.table_ref, bf16[256,256]{1,0:T(8,128)(2,1)S(1)} %get-tuple-element.45.green_ref), custom_call_target="tpu_custom_call" | custom-call | bytes 24000000 | tf_op jit(solution)/shard_map/z_local_solve/pallas_call | solution.py:700
  63.0 4.4 %z_carries.1 = f32[192,64,128]{2,1,0:T(8,128)} custom-call(f32[192,64,128]{2,1,0:T(8,128)S(1)} %z_local_solve.1.y_ref, bf16[256,256]{1,0:T(8,128)(2,1)S(1)} %get-tuple-element.46.matrix_ref, f32[2,8,128]{2,1,0:T(8,128)S(1)} %get-tuple-element.47.share_ref, f32[192,128]{1,0:T(8,128)S(1)} %get-tuple-element.51.layer_ref, ...), custom_call_target="tpu_custom_call" | custom-call | bytes 24000000 | tf_op jit(solution)/shard_map/z_carries/pallas_call | solution.py:765
  (14 shorter events, 0.8 us)
Async XLA Ops:
  0.0 0.7 copy-start
  10.0 3.8 %collective-permute-start = (f32[104,128]{1,0:T(8,128)S(1)}, f32[104,128]{1,0:T(8,128)S(1)}, u32[]{:S(2)}, u32[]{:S(2)}) collective-permute-start(f32[104,128]{1,0:T(8,128)S(1)} %get-tuple-element.36.up_ref), channel_id=1, source_target_pairs={{0,1},{1,2},{2,3},{3,4},{4,5},{5,6},{6,7},{7,0},{8,9},{9,10},{10,1... | collective-permute-start | bytes 159752 | tf_op jit(solution)/shard_map/ppermute | solution.py:785
  12.7 3.6 %collective-permute-start.1 = (f32[104,128]{1,0:T(8,128)S(1)}, f32[104,128]{1,0:T(8,128)S(1)}, u32[]{:S(2)}, u32[]{:S(2)}) collective-permute-start(f32[104,128]{1,0:T(8,128)S(1)} %get-tuple-element.37), channel_id=1, source_target_pairs={{0,7},{1,0},{2,1},{3,2},{4,3},{5,4},{6,5},{7,6},{8,15},{9,8},{10,9... | collective-permute-start | bytes 159752 | tf_op jit(solution)/shard_map/ppermute | solution.py:785
  18.0 14.8 %all-to-all-start = ((f32[16,24,128]{2,1,0:T(8,128)}), f32[16,24,128]{2,1,0:T(8,128)S(1)}, u32[]{:S(2)}, u32[]{:S(2)}) async-start(f32[16,24,128]{2,1,0:T(8,128)} %bitcast.5), calls=%async_computation | async-start | bytes 393216 | tf_op jit(solution)/shard_map/all_to_all | solution.py:797
  25.8 4.6 %collective-permute-start.2 = (f32[8,128]{1,0:T(8,128)S(1)}, f32[8,128]{1,0:T(8,128)S(1)}, u32[]{:S(2)}, u32[]{:S(2)}) collective-permute-start(f32[8,128]{1,0:T(8,128)S(1)} %get-tuple-element.41.near_ref), channel_id=1, source_target_pairs={{0,3},{1,4},{2,5},{3,6},{4,7},{5,0},{6,1},{7,2},{8,11},{9,12},{10,... | collective-permute-start | bytes 12296 | tf_op jit(solution)/shard_map/ppermute | solution.py:785
  27.7 4.8 %collective-permute-start.3 = (f32[8,128]{1,0:T(8,128)S(1)}, f32[8,128]{1,0:T(8,128)S(1)}, u32[]{:S(2)}, u32[]{:S(2)}) collective-permute-start(f32[8,128]{1,0:T(8,128)S(1)} %get-tuple-element.41.near_ref), channel_id=1, source_target_pairs={{0,5},{1,6},{2,7},{3,0},{4,1},{5,2},{6,3},{7,4},{8,13},{9,14},{10,... | collective-permute-start | bytes 12296 | tf_op jit(solution)/shard_map/ppermute | solution.py:785
  34.1 14.2 %all-to-all-start.1 = ((f32[16,24,128]{2,1,0:T(8,128)}), f32[16,24,128]{2,1,0:T(8,128)S(1)}, u32[]{:S(2)}, u32[]{:S(2)}) async-start(f32[16,24,128]{2,1,0:T(8,128)} %bitcast.7), calls=%async_computation.1 | async-start | bytes 393216 | tf_op jit(solution)/shard_map/all_to_all | solution.py:800
  49.1 6.1 %collective-permute-start.10 = (f32[96,128]{1,0:T(8,128)S(1)}, f32[96,128]{1,0:T(8,128)S(1)}, u32[]{:S(2)}, u32[]{:S(2)}) collective-permute-start(f32[96,128]{1,0:T(8,128)S(1)} %get-tuple-element.60), channel_id=1, source_target_pairs={{0,1},{1,2},{2,3},{3,4},{4,5},{5,6},{6,7},{7,0},{8,9},{9,10},{10,1... | collective-permute-start | bytes 147464 | tf_op jit(solution)/shard_map/ppermute | solution.py:785
  49.5 6.8 %collective-permute-start.4 = (f32[96,128]{1,0:T(8,128)S(1)}, f32[96,128]{1,0:T(8,128)S(1)}, u32[]{:S(2)}, u32[]{:S(2)}) collective-permute-start(f32[96,128]{1,0:T(8,128)S(1)} %get-tuple-element.54), channel_id=1, source_target_pairs={{0,7},{1,0},{2,1},{3,2},{4,3},{5,4},{6,5},{7,6},{8,15},{9,8},{10,9... | collective-permute-start | bytes 147464 | tf_op jit(solution)/shard_map/ppermute | solution.py:785
  49.6 13.3 %collective-permute-start.5 = (f32[96,128]{1,0:T(8,128)S(1)}, f32[96,128]{1,0:T(8,128)S(1)}, u32[]{:S(2)}, u32[]{:S(2)}) collective-permute-start(f32[96,128]{1,0:T(8,128)S(1)} %get-tuple-element.55), channel_id=1, source_target_pairs={{0,6},{1,7},{2,0},{3,1},{4,2},{5,3},{6,4},{7,5},{8,14},{9,15},{10,... | collective-permute-start | bytes 147464 | tf_op jit(solution)/shard_map/ppermute | solution.py:785
  51.4 11.5 %collective-permute-start.6 = (f32[96,128]{1,0:T(8,128)S(1)}, f32[96,128]{1,0:T(8,128)S(1)}, u32[]{:S(2)}, u32[]{:S(2)}) collective-permute-start(f32[96,128]{1,0:T(8,128)S(1)} %get-tuple-element.56), channel_id=1, source_target_pairs={{0,5},{1,6},{2,7},{3,0},{4,1},{5,2},{6,3},{7,4},{8,13},{9,14},{10,... | collective-permute-start | bytes 147464 | tf_op jit(solution)/shard_map/ppermute | solution.py:785
  53.6 9.3 %collective-permute-start.7 = (f32[96,128]{1,0:T(8,128)S(1)}, f32[96,128]{1,0:T(8,128)S(1)}, u32[]{:S(2)}, u32[]{:S(2)}) collective-permute-start(f32[96,128]{1,0:T(8,128)S(1)} %get-tuple-element.57), channel_id=1, source_target_pairs={{0,4},{1,5},{2,6},{3,7},{4,0},{5,1},{6,2},{7,3},{8,12},{9,13},{10,... | collective-permute-start | bytes 147464 | tf_op jit(solution)/shard_map/ppermute | solution.py:785
  55.2 7.7 %collective-permute-start.8 = (f32[96,128]{1,0:T(8,128)S(1)}, f32[96,128]{1,0:T(8,128)S(1)}, u32[]{:S(2)}, u32[]{:S(2)}) collective-permute-start(f32[96,128]{1,0:T(8,128)S(1)} %get-tuple-element.58), channel_id=1, source_target_pairs={{0,3},{1,4},{2,5},{3,6},{4,7},{5,0},{6,1},{7,2},{8,11},{9,12},{10,... | collective-permute-start | bytes 147464 | tf_op jit(solution)/shard_map/ppermute | solution.py:785
  56.3 6.6 %collective-permute-start.9 = (f32[96,128]{1,0:T(8,128)S(1)}, f32[96,128]{1,0:T(8,128)S(1)}, u32[]{:S(2)}, u32[]{:S(2)}) collective-permute-start(f32[96,128]{1,0:T(8,128)S(1)} %get-tuple-element.59), channel_id=1, source_target_pairs={{0,2},{1,3},{2,4},{3,5},{4,6},{5,7},{6,0},{7,1},{8,10},{9,11},{10,... | collective-permute-start | bytes 147464 | tf_op jit(solution)/shard_map/ppermute | solution.py:785

commit v4 on v3

--- a/solution.py
+++ b/solution.py
@@ -16,8 +16,9 @@
 GROUP = 8
 PER = 32
 STEPS = LINES // PER
+BATCH = 16
 SLOTS = 2
-AHEAD = 3
+AHEAD = 6
 PITCH = 65
 NGY = 16
 NGZ = 8
@@ -111,7 +112,10 @@
 
 
 def pitched(ref, step):
-    return ref.at[pl.ds(step * PER * PITCH, PER * PITCH)]
+    start = step * PER * PITCH
+    if not isinstance(step, int):
+        start = pl.multiple_of(start, 8)
+    return ref.at[pl.ds(start, PER * PITCH)]
 
 
 def no_copies(i):
@@ -619,15 +623,16 @@
         seen_ref[...] = both[:, CZ:]
 
     def work(i):
-        for g in range(PER // GROUP):
+        near_m = pitched(m_ref, i)
+        for g in range(PER // BATCH):
             left = left_ref.at[g % SLOTS]
-            first = i * PER + g * GROUP
-            for c in range(GROUP):
+            first = i * PER + g * BATCH
+            for c in range(BATCH):
                 line = first + c
-                change = m_ref[pl.ds(line * PITCH, CY), :] - u_ref[line]
+                change = near_m[pl.ds((g * BATCH + c) * PITCH, CY), :] - u_ref[line]
                 split_rows(left, pl.ds(c * CY, CY), change)
             result = halves(jnp.dot(left[...], ends_ref[...], preferred_element_type=f32))
-            for c in range(GROUP):
+            for c in range(BATCH):
                 part = jnp.where(mask, result[c * CY : (c + 1) * CY], 0.0)
                 sums_ref[pl.ds(first + c, 1), :] = jnp.sum(part, axis=0, keepdims=True)
 
@@ -644,7 +649,7 @@
         [
             pltpu.VMEM(PITCHED, f32),
             pltpu.VMEM((LINES, CY, CZ), f32),
-            pltpu.VMEM((SLOTS, GROUP * CY, 2 * CZ), bf16),
+            pltpu.VMEM((SLOTS, BATCH * CY, 2 * CZ), bf16),
             pltpu.VMEM((LINES, CZ), f32),
             pltpu.SemaphoreType.DMA((2, STEPS)),
         ],
@@ -679,18 +684,19 @@
     tall = (CY, CZ)
 
     def work(i):
-        for g in range(PER // GROUP):
+        near_m = pitched(m_ref, i)
+        for g in range(PER // BATCH):
             left = left_ref.at[g % SLOTS]
-            first = i * PER + g * GROUP
-            for c in range(GROUP):
+            first = i * PER + g * BATCH
+            for c in range(BATCH):
                 line = first + c
                 carry_up = jnp.broadcast_to(carry_ref[0, pl.ds(line, 1), :], tall)
                 carry_down = jnp.broadcast_to(carry_ref[1, pl.ds(line, 1), :], tall)
-                change = m_ref[pl.ds(line * PITCH, CY), :] - u_ref[line]
+                change = near_m[pl.ds((g * BATCH + c) * PITCH, CY), :] - u_ref[line]
                 change = change + table_ref[0] * carry_up + table_ref[1] * carry_down
                 split_rows(left, pl.ds(c * CY, CY), change)
             result = halves(jnp.dot(left[...], green_ref[...], preferred_element_type=f32))
-            for c in range(GROUP):
+            for c in range(BATCH):
                 y_ref[first + c] = u_ref[first + c] + result[c * CY : (c + 1) * CY]
 
     pipeline(fetches_of(u_hbm, m_hbm, u_ref, m_ref, sems), no_copies, work)
@@ -705,7 +711,7 @@
         [
             pltpu.VMEM(PITCHED, f32),
             pltpu.VMEM((LINES, CY, CZ), f32),
-            pltpu.VMEM((SLOTS, GROUP * CY, 2 * CZ), bf16),
+            pltpu.VMEM((SLOTS, BATCH * CY, 2 * CZ), bf16),
             pltpu.SemaphoreType.DMA((3, STEPS)),
         ],
         name="z_local_solve",
@@ -744,10 +750,10 @@
             mid_ref[at, :] = mid.astype(f32)
 
     def work(i):
-        for g in range(PER // GROUP):
+        for g in range(PER // BATCH):
             left = left_ref.at[g % SLOTS]
-            first = i * PER + g * GROUP
-            for c in range(GROUP):
+            first = i * PER + g * BATCH
+            for c in range(BATCH):
                 line = pl.ds(first + c, 1)
                 at = pl.ds(c * CY, CY)
                 high = jnp.broadcast_to(high_ref[line, :], tall)
@@ -755,7 +761,7 @@
                 left[at, 0:CZ] = jnp.where(mask, high, 0.0).astype(bf16)
                 left[at, CZ:] = jnp.where(mask, mid, 0.0).astype(bf16)
             result = halves(jnp.dot(left[...], matrix_ref[...], preferred_element_type=f32))
-            for c in range(GROUP):
+            for c in range(BATCH):
                 out_ref[first + c] = y_ref[first + c] + result[c * CY : (c + 1) * CY]
 
     pipeline(no_copies, stores, work, prepare)
@@ -769,7 +775,7 @@
         [VMEM] * (NGZ + 3),
         [
             pltpu.VMEM((LINES, CY, CZ), f32),
-            pltpu.VMEM((SLOTS, GROUP * CY, 2 * CZ), bf16),
+            pltpu.VMEM((SLOTS, BATCH * CY, 2 * CZ), bf16),
             pltpu.VMEM((LINES, CZ), f32),
             pltpu.VMEM((LINES, CZ), f32),
             pltpu.SemaphoreType.DMA((2, STEPS)),

time: 67.8 us -> 66.8 us (0.985)
  Pallas kernels: 32.1 us -> 30.8 us
  transfers between devices with their start and end apart: 13 -> 13, of which waited for: 5 -> 6; matrix products, arithmetic and copies ran while one was open for 0% -> 0% of each run, Pallas kernels for 21% -> 20%
where the time goes in v4:
time: 66.8 us; the launch traced here: 66.4 us
  Pallas kernels  30.8 us (46%)
  starting transfers between devices  27.5 us (41%)
  waiting for transfers between devices  7.29 us (11%)
    ppermute x11, starting transfers between devices, shifted(): return lax.ppermute(x, axis, [(i, (i + by) % n) for i in range(n)])  13.5 us
    pallas_call x1, Pallas kernels, sweeps(): kernel_call(sweep_kernel, [jax.ShapeDtypeStruct(PITCHED, f32), jax.ShapeD...  9.38 us
    all_to_all x1, starting transfers between devices, body(): nodes = lax.all_to_all(ends.reshape(2 * LINES, CZ), 'gy', 0, 0, tiled=True)  7.77 us
    ppermute x11, waiting for transfers between devices, shifted(): return lax.ppermute(x, axis, [(i, (i + by) % n) for i in range(n)])  6.92 us
    all_to_all x1, starting transfers between devices, body(): lax.all_to_all(nodes, 'gy', 0, 0, tiled=True).reshape(2, LINES, CZ)  6.3 us
    pallas_call x1, Pallas kernels, local_solve(): kernel_call(solve_kernel, CUBE, VMEM, [HBM, HBM] + [VMEM] * 3, [pltpu.VME...  5.72 us
    pallas_call x1, Pallas kernels, local_sums(): kernel_call(sums_kernel, [FLAT, FLAT], [VMEM] * 2, [HBM, HBM] + [VMEM] *...  5.23 us
    pallas_call x1, Pallas kernels, finish(): kernel_call(finish_kernel, CUBE, HBM, [VMEM] * (NGZ + 3), [pltpu.VMEM((LI...  3.98 us
  transfers between devices with their start and end apart: 13, of which 6 were waited for; matrix products, arithmetic and copies ran while one was open for 0% of the time, Pallas kernels for 20%

profile of v4, /device:TPU:1, one launch (start us, length us, event | category | flops | bytes accessed | tf_op | source)
XLA Modules:
  0.0 66.4 jit_solution(8073132971434990668)
XLA Ops:
  0.0 0.7 copy-done
  0.7 9.4 %y_sweeps.1 = (f32[12480,128]{1,0:T(8,128)}, f32[2,192,128]{2,1,0:T(8,128)S(1)}, f32[192,128]{1,0:T(8,128)S(1)}, f32[104,128]{1,0:T(8,128)S(1)}, f32[104,128]{1,0:T(8,128)S(1)}) custom-call(f32[192,64,128]{2,1,0:T(8,128)} %bitcast.14, bf16[192,64,128]{2,1,0:T(8,128)(2,1)} %bitcast.17, f32[1,128]{1,0:T(1,128)S(1)} %bitcast.13), custom_call_target="tpu_custom_call" | custom-call | bytes 36000000 | tf_op jit(solution)/shard_map/y_sweeps/pallas_call | solution.py:253
  10.0 2.6 %collective-permute-start = (f32[104,128]{1,0:T(8,128)S(1)}, f32[104,128]{1,0:T(8,128)S(1)}, u32[]{:S(2)}, u32[]{:S(2)}) collective-permute-start(f32[104,128]{1,0:T(8,128)S(1)} %get-tuple-element.36.up_ref), channel_id=1, source_target_pairs={{0,1},{1,2},{2,3},{3,4},{4,5},{5,6},{6,7},{7,0},{8,9},{9,10},{10,1... | collective-permute-start | bytes 159752 | tf_op jit(solution)/shard_map/ppermute | solution.py:791
  13.0 0.9 %collective-permute-done.low_ref = f32[104,128]{1,0:T(8,128)S(1)} collective-permute-done((f32[104,128]{1,0:T(8,128)S(1)}, f32[104,128]{1,0:T(8,128)S(1)}, u32[]{:S(2)}, u32[]{:S(2)}) %collective-permute-start) | collective-permute-done | bytes 53280 | tf_op jit(solution)/shard_map/ppermute | solution.py:791
  13.9 2.3 %collective-permute-done.1.high_ref = f32[104,128]{1,0:T(8,128)S(1)} collective-permute-done((f32[104,128]{1,0:T(8,128)S(1)}, f32[104,128]{1,0:T(8,128)S(1)}, u32[]{:S(2)}, u32[]{:S(2)}) %collective-permute-start.1) | collective-permute-done | bytes 53280 | tf_op jit(solution)/shard_map/ppermute | solution.py:791
  16.2 1.8 %repair.1 = (f32[2,192,128]{2,1,0:T(8,128)}, f32[192,128]{1,0:T(8,128)S(1)}, f32[8,128]{1,0:T(8,128)S(1)}) custom-call(s32[2]{0:T(128)S(1)} %pad_add_fusion.rank_ref, f32[2,192,128]{2,1,0:T(8,128)S(1)} %get-tuple-element.34.ends_ref, f32[192,128]{1,0:T(8,128)S(1)} %get-tuple-element.35.columns_ref, f32[104,128]{1,0:T(8,128)S(1)} %get-tuple-element.36.up_ref, ...), custom_call_target="tpu_custom_call" | custom-call | bytes 3000000 | tf_op jit(solution)/shard_map/repair/pallas_call | solution.py:380
  18.0 7.8 %all-to-all-start = ((f32[16,24,128]{2,1,0:T(8,128)}), f32[16,24,128]{2,1,0:T(8,128)S(1)}, u32[]{:S(2)}, u32[]{:S(2)}) async-start(f32[16,24,128]{2,1,0:T(8,128)} %bitcast.5), calls=%async_computation | async-start | bytes 393216 | tf_op jit(solution)/shard_map/all_to_all | solution.py:803
  25.8 1.9 %collective-permute-start.2 = (f32[8,128]{1,0:T(8,128)S(1)}, f32[8,128]{1,0:T(8,128)S(1)}, u32[]{:S(2)}, u32[]{:S(2)}) collective-permute-start(f32[8,128]{1,0:T(8,128)S(1)} %get-tuple-element.41.near_ref), channel_id=1, source_target_pairs={{0,3},{1,4},{2,5},{3,6},{4,7},{5,0},{6,1},{7,2},{8,11},{9,12},{10,... | collective-permute-start | bytes 12296 | tf_op jit(solution)/shard_map/ppermute | solution.py:791
  27.7 1.1 %collective-permute-start.3 = (f32[8,128]{1,0:T(8,128)S(1)}, f32[8,128]{1,0:T(8,128)S(1)}, u32[]{:S(2)}, u32[]{:S(2)}) collective-permute-start(f32[8,128]{1,0:T(8,128)S(1)} %get-tuple-element.41.near_ref), channel_id=1, source_target_pairs={{0,5},{1,6},{2,7},{3,0},{4,1},{5,2},{6,3},{7,4},{8,13},{9,14},{10,... | collective-permute-start | bytes 12296 | tf_op jit(solution)/shard_map/ppermute | solution.py:791
  28.8 1.6 %collective-permute-done.2.far_low_ref = f32[8,128]{1,0:T(8,128)S(1)} collective-permute-done((f32[8,128]{1,0:T(8,128)S(1)}, f32[8,128]{1,0:T(8,128)S(1)}, u32[]{:S(2)}, u32[]{:S(2)}) %collective-permute-start.2) | collective-permute-done | bytes 4128 | tf_op jit(solution)/shard_map/ppermute | solution.py:791
  30.4 2.1 %collective-permute-done.3.far_high_ref = f32[8,128]{1,0:T(8,128)S(1)} collective-permute-done((f32[8,128]{1,0:T(8,128)S(1)}, f32[8,128]{1,0:T(8,128)S(1)}, u32[]{:S(2)}, u32[]{:S(2)}) %collective-permute-start.3) | collective-permute-done | bytes 4128 | tf_op jit(solution)/shard_map/ppermute | solution.py:791
  32.8 1.3 %ring_scan.1 = (f32[384,128]{1,0:T(8,128)}, f32[8,128]{1,0:T(8,128)S(1)}) custom-call(s32[2]{0:T(128)S(1)} %pad_add_fusion.rank_ref, f32[384,128]{1,0:T(8,128)S(1)} %bitcast.12, f32[2,8,128]{2,1,0:T(8,128)S(1)} %get-tuple-element.40.turn_ref, f32[8,128]{1,0:T(8,128)S(1)} %get-tuple-element.41.near_ref, f32[8,128]{1,0:T(8,128)S(1)} %collective-permute-done.2.far_low_ref, ...), custom_call_target="tpu_custom_call" | custom-call | bytes 3000000 | tf_op jit(solution)/shard_map/ring_scan/pallas_call | solution.py:417
  34.1 6.3 %all-to-all-start.1 = ((f32[16,24,128]{2,1,0:T(8,128)}), f32[16,24,128]{2,1,0:T(8,128)S(1)}, u32[]{:S(2)}, u32[]{:S(2)}) async-start(f32[16,24,128]{2,1,0:T(8,128)} %bitcast.7), calls=%async_computation.1 | async-start | bytes 393216 | tf_op jit(solution)/shard_map/all_to_all | solution.py:806
  40.4 2.3 %z_coefficients.1 = (f32[2,64,128]{2,1,0:T(8,128)S(1)}, bf16[256,256]{1,0:T(8,128)(2,1)S(1)}, bf16[256,256]{1,0:T(8,128)(2,1)S(1)}, bf16[256,256]{1,0:T(8,128)(2...) custom-call(s32[2]{0:T(128)S(1)} %pad_add_fusion.rank_ref, ...), custom_call_target="tpu_custom_call" | custom-call | bytes 12000000 | tf_op jit(solution)/shard_map/z_coefficients/pallas_call | solution.py:577
  42.7 5.2 %z_local_sums.1 = (f32[192,128]{1,0:T(8,128)S(1)}, f32[192,128]{1,0:T(8,128)S(1)}) custom-call(f32[12480,128]{1,0:T(8,128)} %get-tuple-element.33.m_hbm, f32[192,64,128]{2,1,0:T(8,128)} %bitcast.15, bf16[256,256]{1,0:T(8,128)(2,1)S(1)} %get-tuple-element.48.ends_ref, f32[192,128]{1,0:T(8,128)S(1)} %get-tuple-element.49.flux_ref, ...), custom_call_target="tpu_custom_call" | custom-call | bytes 24000000 | tf_op jit(solution)/shard_map/z_local_sums/pallas_call | solution.py:644
  48.0 0.8 %z_messages.1 = (f32[96,128]{1,0:T(8,128)S(1)}, f32[96,128]{1,0:T(8,128)S(1)}, f32[96,128]{1,0:T(8,128)S(1)}, f32[96,128]{1,0:T(8,128)S(1)}, f32[96,128]{1,0:T(8...) custom-call(s32[2]{0:T(128)S(1)} %pad_add_fusion.rank_ref, f32[192,128]{1,0:T(8,128)S(1)} %get-tuple-element.52.sums_ref, ...), custom_call_target="tpu_custom_call" | custom-call | bytes 3000000 | tf_op jit(solution)/shard_map/z_messages/pallas_call | solution.py:678
  48.8 0.7 collective-permute-start.10
  49.5 1.9 %collective-permute-start.5 = (f32[96,128]{1,0:T(8,128)S(1)}, f32[96,128]{1,0:T(8,128)S(1)}, u32[]{:S(2)}, u32[]{:S(2)}) collective-permute-start(f32[96,128]{1,0:T(8,128)S(1)} %get-tuple-element.55), channel_id=1, source_target_pairs={{0,6},{1,7},{2,0},{3,1},{4,2},{5,3},{6,4},{7,5},{8,14},{9,15},{10,... | collective-permute-start | bytes 147464 | tf_op jit(solution)/shard_map/ppermute | solution.py:791
  51.4 2.2 %collective-permute-start.6 = (f32[96,128]{1,0:T(8,128)S(1)}, f32[96,128]{1,0:T(8,128)S(1)}, u32[]{:S(2)}, u32[]{:S(2)}) collective-permute-start(f32[96,128]{1,0:T(8,128)S(1)} %get-tuple-element.56), channel_id=1, source_target_pairs={{0,5},{1,6},{2,7},{3,0},{4,1},{5,2},{6,3},{7,4},{8,13},{9,14},{10,... | collective-permute-start | bytes 147464 | tf_op jit(solution)/shard_map/ppermute | solution.py:791
  53.6 1.6 %collective-permute-start.7 = (f32[96,128]{1,0:T(8,128)S(1)}, f32[96,128]{1,0:T(8,128)S(1)}, u32[]{:S(2)}, u32[]{:S(2)}) collective-permute-start(f32[96,128]{1,0:T(8,128)S(1)} %get-tuple-element.57), channel_id=1, source_target_pairs={{0,4},{1,5},{2,6},{3,7},{4,0},{5,1},{6,2},{7,3},{8,12},{9,13},{10,... | collective-permute-start | bytes 147464 | tf_op jit(solution)/shard_map/ppermute | solution.py:791
  55.2 1.1 %collective-permute-start.8 = (f32[96,128]{1,0:T(8,128)S(1)}, f32[96,128]{1,0:T(8,128)S(1)}, u32[]{:S(2)}, u32[]{:S(2)}) collective-permute-start(f32[96,128]{1,0:T(8,128)S(1)} %get-tuple-element.58), channel_id=1, source_target_pairs={{0,3},{1,4},{2,5},{3,6},{4,7},{5,0},{6,1},{7,2},{8,11},{9,12},{10,... | collective-permute-start | bytes 147464 | tf_op jit(solution)/shard_map/ppermute | solution.py:791
  56.3 0.4 collective-permute-start.9
  56.7 5.7 %z_local_solve.1.y_ref = f32[192,64,128]{2,1,0:T(8,128)S(1)} custom-call(f32[12480,128]{1,0:T(8,128)} %get-tuple-element.33.m_hbm, f32[192,64,128]{2,1,0:T(8,128)} %bitcast.16, f32[2,192,128]{2,1,0:T(8,128)S(1)} %bitcast.11, f32[2,64,128]{2,1,0:T(8,128)S(1)} %get-tuple-element.44.table_ref, bf16[256,256]{1,0:T(8,128)(2,1)S(1)} %get-tuple-element.45.green_ref), custom_call_target="tpu_custom_call" | custom-call | bytes 24000000 | tf_op jit(solution)/shard_map/z_local_solve/pallas_call | solution.py:706
  62.5 4.0 %z_carries.1 = f32[192,64,128]{2,1,0:T(8,128)} custom-call(f32[192,64,128]{2,1,0:T(8,128)S(1)} %z_local_solve.1.y_ref, bf16[256,256]{1,0:T(8,128)(2,1)S(1)} %get-tuple-element.46.matrix_ref, f32[2,8,128]{2,1,0:T(8,128)S(1)} %get-tuple-element.47.share_ref, f32[192,128]{1,0:T(8,128)S(1)} %get-tuple-element.51.layer_ref, ...), custom_call_target="tpu_custom_call" | custom-call | bytes 24000000 | tf_op jit(solution)/shard_map/z_carries/pallas_call | solution.py:771
  (14 shorter events, 0.7 us)
Async XLA Ops:
  0.0 0.7 copy-start
  10.0 3.8 %collective-permute-start = (f32[104,128]{1,0:T(8,128)S(1)}, f32[104,128]{1,0:T(8,128)S(1)}, u32[]{:S(2)}, u32[]{:S(2)}) collective-permute-start(f32[104,128]{1,0:T(8,128)S(1)} %get-tuple-element.36.up_ref), channel_id=1, source_target_pairs={{0,1},{1,2},{2,3},{3,4},{4,5},{5,6},{6,7},{7,0},{8,9},{9,10},{10,1... | collective-permute-start | bytes 159752 | tf_op jit(solution)/shard_map/ppermute | solution.py:791
  12.7 3.6 %collective-permute-start.1 = (f32[104,128]{1,0:T(8,128)S(1)}, f32[104,128]{1,0:T(8,128)S(1)}, u32[]{:S(2)}, u32[]{:S(2)}) collective-permute-start(f32[104,128]{1,0:T(8,128)S(1)} %get-tuple-element.37), channel_id=1, source_target_pairs={{0,7},{1,0},{2,1},{3,2},{4,3},{5,4},{6,5},{7,6},{8,15},{9,8},{10,9... | collective-permute-start | bytes 159752 | tf_op jit(solution)/shard_map/ppermute | solution.py:791
  18.0 14.8 %all-to-all-start = ((f32[16,24,128]{2,1,0:T(8,128)}), f32[16,24,128]{2,1,0:T(8,128)S(1)}, u32[]{:S(2)}, u32[]{:S(2)}) async-start(f32[16,24,128]{2,1,0:T(8,128)} %bitcast.5), calls=%async_computation | async-start | bytes 393216 | tf_op jit(solution)/shard_map/all_to_all | solution.py:803
  25.8 4.6 %collective-permute-start.2 = (f32[8,128]{1,0:T(8,128)S(1)}, f32[8,128]{1,0:T(8,128)S(1)}, u32[]{:S(2)}, u32[]{:S(2)}) collective-permute-start(f32[8,128]{1,0:T(8,128)S(1)} %get-tuple-element.41.near_ref), channel_id=1, source_target_pairs={{0,3},{1,4},{2,5},{3,6},{4,7},{5,0},{6,1},{7,2},{8,11},{9,12},{10,... | collective-permute-start | bytes 12296 | tf_op jit(solution)/shard_map/ppermute | solution.py:791
  27.7 4.8 %collective-permute-start.3 = (f32[8,128]{1,0:T(8,128)S(1)}, f32[8,128]{1,0:T(8,128)S(1)}, u32[]{:S(2)}, u32[]{:S(2)}) collective-permute-start(f32[8,128]{1,0:T(8,128)S(1)} %get-tuple-element.41.near_ref), channel_id=1, source_target_pairs={{0,5},{1,6},{2,7},{3,0},{4,1},{5,2},{6,3},{7,4},{8,13},{9,14},{10,... | collective-permute-start | bytes 12296 | tf_op jit(solution)/shard_map/ppermute | solution.py:791
  34.1 13.9 %all-to-all-start.1 = ((f32[16,24,128]{2,1,0:T(8,128)}), f32[16,24,128]{2,1,0:T(8,128)S(1)}, u32[]{:S(2)}, u32[]{:S(2)}) async-start(f32[16,24,128]{2,1,0:T(8,128)} %bitcast.7), calls=%async_computation.1 | async-start | bytes 393216 | tf_op jit(solution)/shard_map/all_to_all | solution.py:806
  48.8 6.4 %collective-permute-start.10 = (f32[96,128]{1,0:T(8,128)S(1)}, f32[96,128]{1,0:T(8,128)S(1)}, u32[]{:S(2)}, u32[]{:S(2)}) collective-permute-start(f32[96,128]{1,0:T(8,128)S(1)} %get-tuple-element.60), channel_id=1, source_target_pairs={{0,1},{1,2},{2,3},{3,4},{4,5},{5,6},{6,7},{7,0},{8,9},{9,10},{10,1... | collective-permute-start | bytes 147464 | tf_op jit(solution)/shard_map/ppermute | solution.py:791
  49.5 6.8 %collective-permute-start.4 = (f32[96,128]{1,0:T(8,128)S(1)}, f32[96,128]{1,0:T(8,128)S(1)}, u32[]{:S(2)}, u32[]{:S(2)}) collective-permute-start(f32[96,128]{1,0:T(8,128)S(1)} %get-tuple-element.54), channel_id=1, source_target_pairs={{0,7},{1,0},{2,1},{3,2},{4,3},{5,4},{6,5},{7,6},{8,15},{9,8},{10,9... | collective-permute-start | bytes 147464 | tf_op jit(solution)/shard_map/ppermute | solution.py:791
  49.5 12.9 %collective-permute-start.5 = (f32[96,128]{1,0:T(8,128)S(1)}, f32[96,128]{1,0:T(8,128)S(1)}, u32[]{:S(2)}, u32[]{:S(2)}) collective-permute-start(f32[96,128]{1,0:T(8,128)S(1)} %get-tuple-element.55), channel_id=1, source_target_pairs={{0,6},{1,7},{2,0},{3,1},{4,2},{5,3},{6,4},{7,5},{8,14},{9,15},{10,... | collective-permute-start | bytes 147464 | tf_op jit(solution)/shard_map/ppermute | solution.py:791
  51.4 11.0 %collective-permute-start.6 = (f32[96,128]{1,0:T(8,128)S(1)}, f32[96,128]{1,0:T(8,128)S(1)}, u32[]{:S(2)}, u32[]{:S(2)}) collective-permute-start(f32[96,128]{1,0:T(8,128)S(1)} %get-tuple-element.56), channel_id=1, source_target_pairs={{0,5},{1,6},{2,7},{3,0},{4,1},{5,2},{6,3},{7,4},{8,13},{9,14},{10,... | collective-permute-start | bytes 147464 | tf_op jit(solution)/shard_map/ppermute | solution.py:791
  53.6 8.8 %collective-permute-start.7 = (f32[96,128]{1,0:T(8,128)S(1)}, f32[96,128]{1,0:T(8,128)S(1)}, u32[]{:S(2)}, u32[]{:S(2)}) collective-permute-start(f32[96,128]{1,0:T(8,128)S(1)} %get-tuple-element.57), channel_id=1, source_target_pairs={{0,4},{1,5},{2,6},{3,7},{4,0},{5,1},{6,2},{7,3},{8,12},{9,13},{10,... | collective-permute-start | bytes 147464 | tf_op jit(solution)/shard_map/ppermute | solution.py:791
  55.2 7.2 %collective-permute-start.8 = (f32[96,128]{1,0:T(8,128)S(1)}, f32[96,128]{1,0:T(8,128)S(1)}, u32[]{:S(2)}, u32[]{:S(2)}) collective-permute-start(f32[96,128]{1,0:T(8,128)S(1)} %get-tuple-element.58), channel_id=1, source_target_pairs={{0,3},{1,4},{2,5},{3,6},{4,7},{5,0},{6,1},{7,2},{8,11},{9,12},{10,... | collective-permute-start | bytes 147464 | tf_op jit(solution)/shard_map/ppermute | solution.py:791
  56.3 6.1 %collective-permute-start.9 = (f32[96,128]{1,0:T(8,128)S(1)}, f32[96,128]{1,0:T(8,128)S(1)}, u32[]{:S(2)}, u32[]{:S(2)}) collective-permute-start(f32[96,128]{1,0:T(8,128)S(1)} %get-tuple-element.59), channel_id=1, source_target_pairs={{0,2},{1,3},{2,4},{3,5},{4,6},{5,7},{6,0},{7,1},{8,10},{9,11},{10,... | collective-permute-start | bytes 147464 | tf_op jit(solution)/shard_map/ppermute | solution.py:791

commit v5 on v4

--- a/solution.py
+++ b/solution.py
@@ -338,13 +338,11 @@
 
 def repair_kernel(
     rank_ref, ends_ref, columns_ref, up_ref, low_ref, high_ref, repair_ref,
-    out_ref, flux_ref, near_ref,
+    out_ref, flux_ref,
 ):
     rank = rank_ref[0]
     inner_low, inner_high = rank > 0, rank < NGZ - 1
     own, low_eta, high_eta = (ref[pl.ds(ROWS, 8), :] for ref in (up_ref, low_ref, high_ref))
-    row = rows_of()
-    near_ref[...] = jnp.where(row == 0, low_eta, jnp.where(row == 1, own, high_eta))
     own = own[:1]
     low_eta = jnp.where(inner_low, low_eta[:1], 0.0)[:, CZ - 1 :]
     high_eta = jnp.where(inner_high, high_eta[:1], 0.0)[:, :1]
@@ -374,9 +372,8 @@
     shapes = [
         jax.ShapeDtypeStruct((2, LINES, CZ), f32),
         FLAT,
-        jax.ShapeDtypeStruct((NGZ, CZ), f32),
     ]
-    call = kernel_call(repair_kernel, shapes, [VMEM] * 3, [SMEM] + [VMEM] * 6, name="repair")
+    call = kernel_call(repair_kernel, shapes, [VMEM] * 2, [SMEM] + [VMEM] * 6, name="repair")
     return call(ranks, ends, columns, up, low, high, matrix)
 
 
@@ -799,7 +796,8 @@
     m, ends, columns, up, down = sweeps(u, q, own)
     low, high = shifted(up, "gz", 1), shifted(down, "gz", -1)
     matrix, turn = line_matrices(up)
-    ends, flux, near = repair(ranks, ends, columns, up, low, high, matrix)
+    near = jnp.concatenate([x[ROWS : ROWS + 1] for x in (low, up, high)] + [up[ROWS + 3 :]], axis=0)
+    ends, flux = repair(ranks, ends, columns, up, low, high, matrix)
     nodes = lax.all_to_all(ends.reshape(2 * LINES, CZ), "gy", 0, 0, tiled=True)
     far_low, far_high = shifted(near, "gz", 3), shifted(near, "gz", -3)
     nodes, etas = ring_scan(ranks, nodes, turn, near, far_low, far_high)

time: 66.8 us -> 66.6 us (level)
  transfers between devices with their start and end apart: 13 -> 13, of which waited for: 6 -> 5; matrix products, arithmetic and copies ran while one was open for 0% -> 0% of each run, Pallas kernels for 20% -> 20%
where the time goes in v5:
time: 66.6 us; the launch traced here: 66.3 us
  Pallas kernels  30.8 us (46%)
  starting transfers between devices  27.5 us (41%)
  waiting for transfers between devices  7.14 us (11%)
  local copies, waits for them, and re-layouts  0.67 us (1%)
    ppermute x11, starting transfers between devices, shifted(): return lax.ppermute(x, axis, [(i, (i + by) % n) for i in range(n)])  13.3 us
    pallas_call x1, Pallas kernels, sweeps(): kernel_call(sweep_kernel, [jax.ShapeDtypeStruct(PITCHED, f32), jax.ShapeD...  9.38 us
    all_to_all x1, starting transfers between devices, body(): nodes = lax.all_to_all(ends.reshape(2 * LINES, CZ), 'gy', 0, 0, tiled=True)  7.77 us
    ppermute x11, waiting for transfers between devices, shifted(): return lax.ppermute(x, axis, [(i, (i + by) % n) for i in range(n)])  6.92 us
    all_to_all x1, starting transfers between devices, body(): lax.all_to_all(nodes, 'gy', 0, 0, tiled=True).reshape(2, LINES, CZ)  6.42 us
    pallas_call x1, Pallas kernels, local_solve(): kernel_call(solve_kernel, CUBE, VMEM, [HBM, HBM] + [VMEM] * 3, [pltpu.VME...  5.72 us
    pallas_call x1, Pallas kernels, local_sums(): kernel_call(sums_kernel, [FLAT, FLAT], [VMEM] * 2, [HBM, HBM] + [VMEM] *...  5.23 us
    pallas_call x1, Pallas kernels, finish(): kernel_call(finish_kernel, CUBE, HBM, [VMEM] * (NGZ + 3), [pltpu.VMEM((LI...  3.98 us
  transfers between devices with their start and end apart: 13, of which 5 were waited for; matrix products, arithmetic and copies ran while one was open for 0% of the time, Pallas kernels for 20%

profile of v5, /device:TPU:1, one launch (start us, length us, event | category | flops | bytes accessed | tf_op | source)
XLA Modules:
  0.0 66.3 jit_solution(8408973775965910790)
XLA Ops:
  0.0 0.7 copy-done
  0.7 9.4 %y_sweeps.1 = (f32[12480,128]{1,0:T(8,128)}, f32[2,192,128]{2,1,0:T(8,128)S(1)}, f32[192,128]{1,0:T(8,128)S(1)}, f32[104,128]{1,0:T(8,128)S(1)}, f32[104,128]{1,0:T(8,128)S(1)}) custom-call(f32[192,64,128]{2,1,0:T(8,128)} %bitcast.14, bf16[192,64,128]{2,1,0:T(8,128)(2,1)} %bitcast.17, f32[1,128]{1,0:T(1,128)S(1)} %bitcast.13), custom_call_target="tpu_custom_call" | custom-call | bytes 36000000 | tf_op jit(solution)/shard_map/y_sweeps/pallas_call | solution.py:253
  10.0 2.6 %collective-permute-start = (f32[104,128]{1,0:T(8,128)S(1)}, f32[104,128]{1,0:T(8,128)S(1)}, u32[]{:S(2)}, u32[]{:S(2)}) collective-permute-start(f32[104,128]{1,0:T(8,128)S(1)} %get-tuple-element.35.up_ref), channel_id=1, source_target_pairs={{0,1},{1,2},{2,3},{3,4},{4,5},{5,6},{6,7},{7,0},{8,9},{9,10},{10,1... | collective-permute-start | bytes 159752 | tf_op jit(solution)/shard_map/ppermute | solution.py:788
  12.7 0.3 line_matrices.1
  13.0 0.9 %collective-permute-done.low_ref = f32[104,128]{1,0:T(8,128)S(1)} collective-permute-done((f32[104,128]{1,0:T(8,128)S(1)}, f32[104,128]{1,0:T(8,128)S(1)}, u32[]{:S(2)}, u32[]{:S(2)}) %collective-permute-start) | collective-permute-done | bytes 53280 | tf_op jit(solution)/shard_map/ppermute | solution.py:788
  13.9 2.3 %collective-permute-done.1.high_ref = f32[104,128]{1,0:T(8,128)S(1)} collective-permute-done((f32[104,128]{1,0:T(8,128)S(1)}, f32[104,128]{1,0:T(8,128)S(1)}, u32[]{:S(2)}, u32[]{:S(2)}) %collective-permute-start.1) | collective-permute-done | bytes 53280 | tf_op jit(solution)/shard_map/ppermute | solution.py:788
  16.2 1.8 %repair.1 = (f32[2,192,128]{2,1,0:T(8,128)}, f32[192,128]{1,0:T(8,128)S(1)}) custom-call(s32[2]{0:T(128)S(1)} %pad_add_fusion.rank_ref, f32[2,192,128]{2,1,0:T(8,128)S(1)} %get-tuple-element.33.ends_ref, f32[192,128]{1,0:T(8,128)S(1)} %get-tuple-element.34.columns_ref, f32[104,128]{1,0:T(8,128)S(1)} %get-tuple-element.35.up_ref, ...), custom_call_target="tpu_custom_call" | custom-call | bytes 3000000 | tf_op jit(solution)/shard_map/repair/pallas_call | solution.py:377
  18.0 7.8 %all-to-all-start = ((f32[16,24,128]{2,1,0:T(8,128)}), f32[16,24,128]{2,1,0:T(8,128)S(1)}, u32[]{:S(2)}, u32[]{:S(2)}) async-start(f32[16,24,128]{2,1,0:T(8,128)} %bitcast.5), calls=%async_computation | async-start | bytes 393216 | tf_op jit(solution)/shard_map/all_to_all | solution.py:801
  25.8 1.9 %collective-permute-start.2 = (f32[8,128]{1,0:T(8,128)S(1)}, f32[8,128]{1,0:T(8,128)S(1)}, u32[]{:S(2)}, u32[]{:S(2)}) collective-permute-start(f32[8,128]{1,0:T(8,128)S(1)} %pad_maximum_fusion.near_ref), channel_id=1, source_target_pairs={{0,3},{1,4},{2,5},{3,6},{4,7},{5,0},{6,1},{7,2},{8,11},{9,12},{10,... | collective-permute-start | bytes 12296 | tf_op jit(solution)/shard_map/ppermute | solution.py:788
  27.7 1.1 %collective-permute-start.3 = (f32[8,128]{1,0:T(8,128)S(1)}, f32[8,128]{1,0:T(8,128)S(1)}, u32[]{:S(2)}, u32[]{:S(2)}) collective-permute-start(f32[8,128]{1,0:T(8,128)S(1)} %pad_maximum_fusion.near_ref), channel_id=1, source_target_pairs={{0,5},{1,6},{2,7},{3,0},{4,1},{5,2},{6,3},{7,4},{8,13},{9,14},{10,... | collective-permute-start | bytes 12296 | tf_op jit(solution)/shard_map/ppermute | solution.py:788
  28.9 1.6 %collective-permute-done.2.far_low_ref = f32[8,128]{1,0:T(8,128)S(1)} collective-permute-done((f32[8,128]{1,0:T(8,128)S(1)}, f32[8,128]{1,0:T(8,128)S(1)}, u32[]{:S(2)}, u32[]{:S(2)}) %collective-permute-start.2) | collective-permute-done | bytes 4128 | tf_op jit(solution)/shard_map/ppermute | solution.py:788
  30.5 2.1 %collective-permute-done.3.far_high_ref = f32[8,128]{1,0:T(8,128)S(1)} collective-permute-done((f32[8,128]{1,0:T(8,128)S(1)}, f32[8,128]{1,0:T(8,128)S(1)}, u32[]{:S(2)}, u32[]{:S(2)}) %collective-permute-start.3) | collective-permute-done | bytes 4128 | tf_op jit(solution)/shard_map/ppermute | solution.py:788
  32.8 1.3 %ring_scan.1 = (f32[384,128]{1,0:T(8,128)}, f32[8,128]{1,0:T(8,128)S(1)}) custom-call(s32[2]{0:T(128)S(1)} %pad_add_fusion.rank_ref, f32[384,128]{1,0:T(8,128)S(1)} %bitcast.12, f32[2,8,128]{2,1,0:T(8,128)S(1)} %get-tuple-element.39.turn_ref, f32[8,128]{1,0:T(8,128)S(1)} %pad_maximum_fusion.near_ref, f32[8,128]{1,0:T(8,128)S(1)} %collective-permute-done.2.far_low_ref, ...), custom_call_target="tpu_custom_call" | custom-call | bytes 3000000 | tf_op jit(solution)/shard_map/ring_scan/pallas_call | solution.py:414
  34.1 6.4 %all-to-all-start.1 = ((f32[16,24,128]{2,1,0:T(8,128)}), f32[16,24,128]{2,1,0:T(8,128)S(1)}, u32[]{:S(2)}, u32[]{:S(2)}) async-start(f32[16,24,128]{2,1,0:T(8,128)} %bitcast.7), calls=%async_computation.1 | async-start | bytes 393216 | tf_op jit(solution)/shard_map/all_to_all | solution.py:804
  40.5 2.3 %z_coefficients.1 = (f32[2,64,128]{2,1,0:T(8,128)S(1)}, bf16[256,256]{1,0:T(8,128)(2,1)S(1)}, bf16[256,256]{1,0:T(8,128)(2,1)S(1)}, bf16[256,256]{1,0:T(8,128)(2...) custom-call(s32[2]{0:T(128)S(1)} %pad_add_fusion.rank_ref, ...), custom_call_target="tpu_custom_call" | custom-call | bytes 12000000 | tf_op jit(solution)/shard_map/z_coefficients/pallas_call | solution.py:574
  42.8 5.2 %z_local_sums.1 = (f32[192,128]{1,0:T(8,128)S(1)}, f32[192,128]{1,0:T(8,128)S(1)}) custom-call(f32[12480,128]{1,0:T(8,128)} %get-tuple-element.32.m_hbm, f32[192,64,128]{2,1,0:T(8,128)} %bitcast.15, bf16[256,256]{1,0:T(8,128)(2,1)S(1)} %get-tuple-element.46.ends_ref, f32[192,128]{1,0:T(8,128)S(1)} %get-tuple-element.47.flux_ref, ...), custom_call_target="tpu_custom_call" | custom-call | bytes 24000000 | tf_op jit(solution)/shard_map/z_local_sums/pallas_call | solution.py:641
  48.0 0.8 %z_messages.1 = (f32[96,128]{1,0:T(8,128)S(1)}, f32[96,128]{1,0:T(8,128)S(1)}, f32[96,128]{1,0:T(8,128)S(1)}, f32[96,128]{1,0:T(8,128)S(1)}, f32[96,128]{1,0:T(8...) custom-call(s32[2]{0:T(128)S(1)} %pad_add_fusion.rank_ref, f32[192,128]{1,0:T(8,128)S(1)} %get-tuple-element.50.sums_ref, ...), custom_call_target="tpu_custom_call" | custom-call | bytes 3000000 | tf_op jit(solution)/shard_map/z_messages/pallas_call | solution.py:675
  48.9 0.5 collective-permute-start.10
  49.4 1.9 %collective-permute-start.5 = (f32[96,128]{1,0:T(8,128)S(1)}, f32[96,128]{1,0:T(8,128)S(1)}, u32[]{:S(2)}, u32[]{:S(2)}) collective-permute-start(f32[96,128]{1,0:T(8,128)S(1)} %get-tuple-element.53), channel_id=1, source_target_pairs={{0,6},{1,7},{2,0},{3,1},{4,2},{5,3},{6,4},{7,5},{8,14},{9,15},{10,... | collective-permute-start | bytes 147464 | tf_op jit(solution)/shard_map/ppermute | solution.py:788
  51.3 2.4 %collective-permute-start.6 = (f32[96,128]{1,0:T(8,128)S(1)}, f32[96,128]{1,0:T(8,128)S(1)}, u32[]{:S(2)}, u32[]{:S(2)}) collective-permute-start(f32[96,128]{1,0:T(8,128)S(1)} %get-tuple-element.54), channel_id=1, source_target_pairs={{0,5},{1,6},{2,7},{3,0},{4,1},{5,2},{6,3},{7,4},{8,13},{9,14},{10,... | collective-permute-start | bytes 147464 | tf_op jit(solution)/shard_map/ppermute | solution.py:788
  53.7 1.3 %collective-permute-start.7 = (f32[96,128]{1,0:T(8,128)S(1)}, f32[96,128]{1,0:T(8,128)S(1)}, u32[]{:S(2)}, u32[]{:S(2)}) collective-permute-start(f32[96,128]{1,0:T(8,128)S(1)} %get-tuple-element.55), channel_id=1, source_target_pairs={{0,4},{1,5},{2,6},{3,7},{4,0},{5,1},{6,2},{7,3},{8,12},{9,13},{10,... | collective-permute-start | bytes 147464 | tf_op jit(solution)/shard_map/ppermute | solution.py:788
  55.0 1.4 %collective-permute-start.8 = (f32[96,128]{1,0:T(8,128)S(1)}, f32[96,128]{1,0:T(8,128)S(1)}, u32[]{:S(2)}, u32[]{:S(2)}) collective-permute-start(f32[96,128]{1,0:T(8,128)S(1)} %get-tuple-element.56), channel_id=1, source_target_pairs={{0,3},{1,4},{2,5},{3,6},{4,7},{5,0},{6,1},{7,2},{8,11},{9,12},{10,... | collective-permute-start | bytes 147464 | tf_op jit(solution)/shard_map/ppermute | solution.py:788
  56.5 5.7 %z_local_solve.1.y_ref = f32[192,64,128]{2,1,0:T(8,128)S(1)} custom-call(f32[12480,128]{1,0:T(8,128)} %get-tuple-element.32.m_hbm, f32[192,64,128]{2,1,0:T(8,128)} %bitcast.16, f32[2,192,128]{2,1,0:T(8,128)S(1)} %bitcast.11, f32[2,64,128]{2,1,0:T(8,128)S(1)} %get-tuple-element.42.table_ref, bf16[256,256]{1,0:T(8,128)(2,1)S(1)} %get-tuple-element.43.green_ref), custom_call_target="tpu_custom_call" | custom-call | bytes 24000000 | tf_op jit(solution)/shard_map/z_local_solve/pallas_call | solution.py:703
  62.3 4.0 %z_carries.1 = f32[192,64,128]{2,1,0:T(8,128)} custom-call(f32[192,64,128]{2,1,0:T(8,128)S(1)} %z_local_solve.1.y_ref, bf16[256,256]{1,0:T(8,128)(2,1)S(1)} %get-tuple-element.44.matrix_ref, f32[2,8,128]{2,1,0:T(8,128)S(1)} %get-tuple-element.45.share_ref, f32[192,128]{1,0:T(8,128)S(1)} %get-tuple-element.49.layer_ref, ...), custom_call_target="tpu_custom_call" | custom-call | bytes 24000000 | tf_op jit(solution)/shard_map/z_carries/pallas_call | solution.py:768
  (19 shorter events, 0.5 us)
Async XLA Ops:
  0.0 0.7 copy-start
  10.0 3.8 %collective-permute-start = (f32[104,128]{1,0:T(8,128)S(1)}, f32[104,128]{1,0:T(8,128)S(1)}, u32[]{:S(2)}, u32[]{:S(2)}) collective-permute-start(f32[104,128]{1,0:T(8,128)S(1)} %get-tuple-element.35.up_ref), channel_id=1, source_target_pairs={{0,1},{1,2},{2,3},{3,4},{4,5},{5,6},{6,7},{7,0},{8,9},{9,10},{10,1... | collective-permute-start | bytes 159752 | tf_op jit(solution)/shard_map/ppermute | solution.py:788
  12.7 3.6 %collective-permute-start.1 = (f32[104,128]{1,0:T(8,128)S(1)}, f32[104,128]{1,0:T(8,128)S(1)}, u32[]{:S(2)}, u32[]{:S(2)}) collective-permute-start(f32[104,128]{1,0:T(8,128)S(1)} %get-tuple-element.36), channel_id=1, source_target_pairs={{0,7},{1,0},{2,1},{3,2},{4,3},{5,4},{6,5},{7,6},{8,15},{9,8},{10,9... | collective-permute-start | bytes 159752 | tf_op jit(solution)/shard_map/ppermute | solution.py:788
  18.0 14.8 %all-to-all-start = ((f32[16,24,128]{2,1,0:T(8,128)}), f32[16,24,128]{2,1,0:T(8,128)S(1)}, u32[]{:S(2)}, u32[]{:S(2)}) async-start(f32[16,24,128]{2,1,0:T(8,128)} %bitcast.5), calls=%async_computation | async-start | bytes 393216 | tf_op jit(solution)/shard_map/all_to_all | solution.py:801
  25.8 4.6 %collective-permute-start.2 = (f32[8,128]{1,0:T(8,128)S(1)}, f32[8,128]{1,0:T(8,128)S(1)}, u32[]{:S(2)}, u32[]{:S(2)}) collective-permute-start(f32[8,128]{1,0:T(8,128)S(1)} %pad_maximum_fusion.near_ref), channel_id=1, source_target_pairs={{0,3},{1,4},{2,5},{3,6},{4,7},{5,0},{6,1},{7,2},{8,11},{9,12},{10,... | collective-permute-start | bytes 12296 | tf_op jit(solution)/shard_map/ppermute | solution.py:788
  27.7 4.8 %collective-permute-start.3 = (f32[8,128]{1,0:T(8,128)S(1)}, f32[8,128]{1,0:T(8,128)S(1)}, u32[]{:S(2)}, u32[]{:S(2)}) collective-permute-start(f32[8,128]{1,0:T(8,128)S(1)} %pad_maximum_fusion.near_ref), channel_id=1, source_target_pairs={{0,5},{1,6},{2,7},{3,0},{4,1},{5,2},{6,3},{7,4},{8,13},{9,14},{10,... | collective-permute-start | bytes 12296 | tf_op jit(solution)/shard_map/ppermute | solution.py:788
  34.1 14.0 %all-to-all-start.1 = ((f32[16,24,128]{2,1,0:T(8,128)}), f32[16,24,128]{2,1,0:T(8,128)S(1)}, u32[]{:S(2)}, u32[]{:S(2)}) async-start(f32[16,24,128]{2,1,0:T(8,128)} %bitcast.7), calls=%async_computation.1 | async-start | bytes 393216 | tf_op jit(solution)/shard_map/all_to_all | solution.py:804
  48.9 6.2 %collective-permute-start.10 = (f32[96,128]{1,0:T(8,128)S(1)}, f32[96,128]{1,0:T(8,128)S(1)}, u32[]{:S(2)}, u32[]{:S(2)}) collective-permute-start(f32[96,128]{1,0:T(8,128)S(1)} %get-tuple-element.58), channel_id=1, source_target_pairs={{0,1},{1,2},{2,3},{3,4},{4,5},{5,6},{6,7},{7,0},{8,9},{9,10},{10,1... | collective-permute-start | bytes 147464 | tf_op jit(solution)/shard_map/ppermute | solution.py:788
  49.4 7.1 %collective-permute-start.4 = (f32[96,128]{1,0:T(8,128)S(1)}, f32[96,128]{1,0:T(8,128)S(1)}, u32[]{:S(2)}, u32[]{:S(2)}) collective-permute-start(f32[96,128]{1,0:T(8,128)S(1)} %get-tuple-element.52), channel_id=1, source_target_pairs={{0,7},{1,0},{2,1},{3,2},{4,3},{5,4},{6,5},{7,6},{8,15},{9,8},{10,9... | collective-permute-start | bytes 147464 | tf_op jit(solution)/shard_map/ppermute | solution.py:788
  49.4 12.9 %collective-permute-start.5 = (f32[96,128]{1,0:T(8,128)S(1)}, f32[96,128]{1,0:T(8,128)S(1)}, u32[]{:S(2)}, u32[]{:S(2)}) collective-permute-start(f32[96,128]{1,0:T(8,128)S(1)} %get-tuple-element.53), channel_id=1, source_target_pairs={{0,6},{1,7},{2,0},{3,1},{4,2},{5,3},{6,4},{7,5},{8,14},{9,15},{10,... | collective-permute-start | bytes 147464 | tf_op jit(solution)/shard_map/ppermute | solution.py:788
  51.3 11.0 %collective-permute-start.6 = (f32[96,128]{1,0:T(8,128)S(1)}, f32[96,128]{1,0:T(8,128)S(1)}, u32[]{:S(2)}, u32[]{:S(2)}) collective-permute-start(f32[96,128]{1,0:T(8,128)S(1)} %get-tuple-element.54), channel_id=1, source_target_pairs={{0,5},{1,6},{2,7},{3,0},{4,1},{5,2},{6,3},{7,4},{8,13},{9,14},{10,... | collective-permute-start | bytes 147464 | tf_op jit(solution)/shard_map/ppermute | solution.py:788
  53.7 8.6 %collective-permute-start.7 = (f32[96,128]{1,0:T(8,128)S(1)}, f32[96,128]{1,0:T(8,128)S(1)}, u32[]{:S(2)}, u32[]{:S(2)}) collective-permute-start(f32[96,128]{1,0:T(8,128)S(1)} %get-tuple-element.55), channel_id=1, source_target_pairs={{0,4},{1,5},{2,6},{3,7},{4,0},{5,1},{6,2},{7,3},{8,12},{9,13},{10,... | collective-permute-start | bytes 147464 | tf_op jit(solution)/shard_map/ppermute | solution.py:788
  55.0 7.2 %collective-permute-start.8 = (f32[96,128]{1,0:T(8,128)S(1)}, f32[96,128]{1,0:T(8,128)S(1)}, u32[]{:S(2)}, u32[]{:S(2)}) collective-permute-start(f32[96,128]{1,0:T(8,128)S(1)} %get-tuple-element.56), channel_id=1, source_target_pairs={{0,3},{1,4},{2,5},{3,6},{4,7},{5,0},{6,1},{7,2},{8,11},{9,12},{10,... | collective-permute-start | bytes 147464 | tf_op jit(solution)/shard_map/ppermute | solution.py:788
  56.4 5.9 %collective-permute-start.9 = (f32[96,128]{1,0:T(8,128)S(1)}, f32[96,128]{1,0:T(8,128)S(1)}, u32[]{:S(2)}, u32[]{:S(2)}) collective-permute-start(f32[96,128]{1,0:T(8,128)S(1)} %get-tuple-element.57), channel_id=1, source_target_pairs={{0,2},{1,3},{2,4},{3,5},{4,6},{5,7},{6,0},{7,1},{8,10},{9,11},{10,... | collective-permute-start | bytes 147464 | tf_op jit(solution)/shard_map/ppermute | solution.py:788
